TPU v7x, 32 devices: a whole 2x2x4 slice. The times are simulated.
32 devices in a mesh: dp: 8 (over z, core), expert: 4 (over y, x).
Axes of the slice: x: 2, y: 2, z: 4, core: 2. Of those that a mesh axis runs over, the one named last changes fastest.
Arguments:
- tokens: bfloat16 [8192, 1024], P(('dp', 'expert')), may hold values from -6 to 6
- cotangent: bfloat16 [8192, 1024], P(('dp', 'expert')), may hold values from -6 to 6
- route_logits: float32 [8192, 2], P(('dp', 'expert')), may hold values from -6 to 6
- expert_ids: int32 [8192, 2], P(('dp', 'expert')), may hold values from 0 to 7, as said below
- slot_pos: int32 [8192, 2], P(('dp', 'expert')), may hold values from 0 to 127, as said below
- w_in: bfloat16 [8, 1024, 1536], P('expert'), may hold values from -0.1875 to 0.1875
- w_down: bfloat16 [8, 768, 1024], P('expert'), may hold values from -0.21875 to 0.21875
Outputs:
- input_grad: bfloat16 [8192, 1024], P(('dp', 'expert'))
- grad_in: float32 [8, 1024, 1536], P('expert', 'dp')
- grad_down: float32 [8, 768, 1024], P('expert', 'dp')
Inputs may be any that keep to these rules, and one draw needn't show every extreme that they name: `expert_ids`: each row names 2 different experts. Within each aligned block of 256 rows (the tokens of one device) no expert is named more than 128 times, and one expert, the same in all blocks, is named exactly 128 times in every block. `slot_pos`: within each aligned block of 256 rows, entries whose matching expert_ids entries name the same expert are distinct.
All inputs are finite; a program needn't handle non-finite values.
Results may differ from a plain program's by a relative error of at most 0.02.
Values may be sent and summed in bfloat16 or wider, within the bound.
No kernel may reach another device: no remote copies, remote signals or barrier semaphores. Data moves between devices by JAX's collectives and lax.ppermute only.
A program may use at most 128 MiB of HBM per device.

v0:
```python
import jax
import jax.numpy as jnp
from jax import lax
from jax.sharding import PartitionSpec as P

TOP = 2


def recompute(input_slots, w_in, hidden_width):
    gate_up = jnp.einsum("ksd,kdf->ksf", input_slots, w_in, preferred_element_type=jnp.float32)
    gate = gate_up[:, :, :hidden_width]
    upper = gate_up[:, :, hidden_width:]
    sigmoid_gate = jax.nn.sigmoid(gate)
    activated = gate * sigmoid_gate
    hidden = (activated * upper).astype(jnp.bfloat16)
    return (gate, upper, sigmoid_gate, activated, hidden)


def per_device(tokens, cotangent, route_logits, expert_ids, slot_pos, w_in, w_down):
    token_count, width = tokens.shape
    local_experts = w_in.shape[0]
    hidden_width = w_down.shape[1]
    experts_all = local_experts * lax.axis_size("expert")
    capacity = 2 * TOP * token_count // experts_all
    first = jax.nn.sigmoid(route_logits[:, 0] - route_logits[:, 1])
    combine = jnp.stack([first, 1.0 - first], axis=1)
    scaled = (combine[:, :, None] * cotangent[:, None, :].astype(jnp.float32)).astype(jnp.bfloat16)
    destination = (expert_ids * capacity + slot_pos).reshape(-1)
    repeated = jnp.broadcast_to(tokens[:, None, :], (token_count, TOP, width)).reshape(-1, width)
    empty = jnp.zeros((experts_all * capacity, width), jnp.bfloat16)
    send_inputs = empty.at[destination].set(repeated).reshape(experts_all, capacity, width)
    send_scaled = (
        empty.at[destination].set(scaled.reshape(-1, width)).reshape(experts_all, capacity, width)
    )
    input_slots, cotangent_slots = (
        lax.all_to_all(send_inputs, "expert", split_axis=0, concat_axis=1, tiled=True),
        lax.all_to_all(send_scaled, "expert", split_axis=0, concat_axis=1, tiled=True),
    )
    gate, upper, sigmoid_gate, activated, hidden = recompute(input_slots, w_in, hidden_width)
    grad_hidden = jnp.einsum(
        "ksd,kfd->ksf", cotangent_slots, w_down, preferred_element_type=jnp.float32
    )
    term_down = jnp.einsum(
        "ksf,ksd->kfd", hidden, cotangent_slots, preferred_element_type=jnp.float32
    )
    grad_gate = grad_hidden * upper * sigmoid_gate * (1.0 + gate * (1.0 - sigmoid_gate))
    grad_up = grad_hidden * activated
    grad_pair = jnp.concatenate([grad_gate, grad_up], axis=2).astype(jnp.bfloat16)
    term_in = jnp.einsum("ksd,ksf->kdf", input_slots, grad_pair, preferred_element_type=jnp.float32)
    returned = jnp.einsum(
        "ksf,kdf->ksd", grad_pair, w_in, preferred_element_type=jnp.float32
    ).astype(jnp.bfloat16)
    arrived = lax.all_to_all(returned, "expert", split_axis=1, concat_axis=0, tiled=True)
    rows = arrived.reshape(-1, width)[destination].reshape(token_count, TOP, width)
    input_grad = jnp.sum(rows.astype(jnp.float32), axis=1).astype(jnp.bfloat16)
    grad_in, grad_down = (
        lax.psum_scatter(
            term_in.astype(jnp.bfloat16), "dp", scatter_dimension=1, tiled=True
        ).astype(jnp.float32),
        lax.psum_scatter(
            term_down.astype(jnp.bfloat16), "dp", scatter_dimension=1, tiled=True
        ).astype(jnp.float32),
    )
    return (input_grad, grad_in, grad_down)


def solution(mesh):
    in_specs = (
        P(("dp", "expert"), None),
        P(("dp", "expert"), None),
        P(("dp", "expert"), None),
        P(("dp", "expert"), None),
        P(("dp", "expert"), None),
        P("expert", None, None),
        P("expert", None, None),
    )
    out_specs = (P(("dp", "expert"), None), P("expert", "dp", None), P("expert", "dp", None))
    return jax.shard_map(
        per_device, mesh=mesh, in_specs=in_specs, out_specs=out_specs, check_vma=False
    )
```

profile of v0, /device:TPU:0, one launch (start us, length us, event | category | flops | bytes accessed | tf_op | source)
XLA Modules:
  0.0 213.9 jit_solution(7043457608537626444)
XLA Ops:
  7.2 0.0 copy-start
  7.2 0.9 multiply_add_fusion
  8.0 0.1 copy.20
  8.2 0.1 reshape.61
  8.3 2.6 %broadcast_in_dim.5 = bf16[256,2,1024]{2,1,0:T(2,128)(2,1)} broadcast(bf16[256,1024]{1,0:T(8,128)(2,1)} %param.7), dimensions={0,2} | broadcast | bytes 1572864 | tf_op jit(solution)/shard_map/broadcast_in_dim | solution.py:29
  10.9 2.2 %reshape.87 = bf16[512,1024]{1,0:T(8,128)(2,1)} reshape(bf16[256,2,1024]{2,1,0:T(2,128)(2,1)} %broadcast_in_dim.5) | data formatting | bytes 2097152 | tf_op jit(solution)/shard_map/reshape | solution.py:29
  13.1 4.8 %scatter_custom_fusion.1 = bf16[1024,1024]{1,0:T(8,128)(2,1)} fusion(s32[512]{0:T(512)S(1)} %bitcast.31, bf16[512,1024]{1,0:T(8,128)(2,1)} %reshape.87, bf16[]{:T(256)} %constant.5.clone.1), kind=kCustom, calls=%fused_computation.16 | custom fusion | bytes 2097664 | tf_op jit(solution)/shard_map/scatter | solution.py:31
  17.9 5.2 %all-to-all-start.1 = ((bf16[8,128,1024]{2,1,0:T(8,128)(2,1)}), bf16[8,128,1024]{2,1,0:T(8,128)(2,1)}, u32[]{:S(2)}, u32[]{:S(2)}) async-start(bf16[8,128,1024]{2,1,0:T(8,128)(2,1)} %bitcast.25), calls=%async_computation.1 | async-start | bytes 4194304 | tf_op jit(solution)/shard_map/all_to_all | solution.py:36
  23.1 0.0 copy-done.4
  23.1 0.1 copy.21
  23.3 0.1 mul.47
  23.4 2.9 %mul.49 = f32[256,2,1024]{2,1,0:T(2,128)} broadcast(bf16[256,1024]{1,0:T(8,128)(2,1)} %param.8), dimensions={0,2} | broadcast | bytes 2621440 | tf_op jit(solution)/shard_map/mul | solution.py:27
  26.3 3.7 %mul.50 = f32[512,1024]{1,0:T(8,128)} reshape(f32[256,2,1024]{2,1,0:T(2,128)} %mul.49) | data formatting | bytes 4194304 | tf_op jit(solution)/shard_map/mul | solution.py:27
  30.0 5.2 %scatter_custom_fusion = bf16[1024,1024]{1,0:T(8,128)(2,1)} fusion(s32[512]{0:T(512)S(1)} %bitcast.32, f32[512,1024]{1,0:T(8,128)} %mul.50, f32[512]{0:T(512)S(1)} %mul.47, bf16[]{:T(256)} %constant.5.clone.1), kind=kCustom, calls=%fused_computation.14 | custom fusion | flops 1048576 | bytes 4196354 | tf_op jit(solution)/shard_map/scatter | solution.py:33
  35.2 13.6 %all-to-all-done.1 = bf16[8,128,1024]{2,1,0:T(8,128)(2,1)} async-done(((bf16[8,128,1024]{2,1,0:T(8,128)(2,1)}), bf16[8,128,1024]{2,1,0:T(8,128)(2,1)}, u32[]{:S(2)}, u32[]{:S(2)}) %all-to-all-start.1) | async-done | bytes 2097184 | tf_op jit(solution)/shard_map/all_to_all | solution.py:36
  48.8 4.5 %all-to-all-start = ((bf16[8,128,1024]{2,1,0:T(8,128)(2,1)}), bf16[8,128,1024]{2,1,0:T(8,128)(2,1)}, u32[]{:S(2)}, u32[]{:S(2)}) async-start(bf16[8,128,1024]{2,1,0:T(8,128)(2,1)} %bitcast.26), calls=%async_computation | async-start | bytes 4194304 | tf_op jit(solution)/shard_map/all_to_all | solution.py:37
  53.3 0.2 reduce-scatter.5.cloned.1.call-start
  53.5 3.1 %copy.23 = bf16[2,4,128,1024]{3,2,1,0:T(8,128)(2,1)} copy(bf16[2,4,128,1024]{3,2,0,1:T(8,128)(2,1)} %bitcast.7) | data formatting | bytes 4194304 | tf_op jit(solution)/shard_map/all_to_all | solution.py:36
  56.6 21.4 %all-to-all-done = bf16[8,128,1024]{2,1,0:T(8,128)(2,1)} async-done(((bf16[8,128,1024]{2,1,0:T(8,128)(2,1)}), bf16[8,128,1024]{2,1,0:T(8,128)(2,1)}, u32[]{:S(2)}, u32[]{:S(2)}) %all-to-all-start) | async-done | bytes 2097184 | tf_op jit(solution)/shard_map/all_to_all | solution.py:37
  77.9 2.0 copy.22
  79.9 0.0 copy-start.3
  79.9 0.2 copy-done.1
  80.2 6.0 %fusion.12 = f32[2,512,1536]{2,1,0:T(8,128)S(1)} fusion(bf16[2,512,1024]{2,1,0:T(8,128)(2,1)S(1)} %bitcast.27, bf16[2,1024,1536]{2,1,0:T(8,128)(2,1)} %param.12), kind=kOutput, calls=%fused_computation.28 | convolution fusion | flops 3221225472 | bytes 14680064 | tf_op jit(solution)/shard_map/ksd,kdf->ksf/dot_general | solution.py:10
  86.2 0.0 copy-start.5
  86.2 0.0 copy-done.3
  86.2 2.6 %copy-done.5 = f32[2,512,1536]{2,1,0:T(8,128)} copy-done((f32[2,512,1536]{2,1,0:T(8,128)}, f32[2,512,1536]{2,1,0:T(8,128)S(1)}, u32[]{:S(2)}) %copy-start.5) | copy-done | bytes 6291480
  88.9 3.7 %convolution_convert_fusion.1 = bf16[2,768,1024]{2,1,0:T(8,128)(2,1)} fusion(bf16[2,512,1024]{2,1,0:T(8,128)(2,1)S(1)} %bitcast.29, f32[2,512,1536]{2,1,0:T(8,128)S(1)} %fusion.12), kind=kOutput, calls=%fused_computation.10 | convolution fusion | flops 1616904192 | bytes 11534336 | tf_op jit(solution)/shard_map/ksf,ksd->kfd/dot_general | solution.py:43
  92.6 0.0 reduce-scatter.5.cloned.1.call-update
  92.6 0.0 reduce-scatter.3.cloned.1.call-start
  92.7 0.0 copy-done
  92.7 0.0 copy-start.2
  92.7 5.9 %multiply_convert_fusion.2 = (bf16[2,512,768]{2,1,0:T(8,128)(2,1)S(1)}, bf16[2,512,768]{2,1,0:T(8,128)(2,1)S(1)}) fusion(f32[2,512,1536]{2,1,0:T(8,128)} %copy-done.5, bf16[2,512,1024]{2,1,0:T(8,128)(2,1)} %bitcast.30, bf16[2,768,1024]{2,1,0:T(8,128)(2,1)S(1)} %copy-done), kind=kOutput, calls=%fused_computation.7 | convolution fusion | flops 1620836352 | bytes 14680064 | tf_op jit(solution)/shard_map/ksd,kfd->ksf/dot_general | solution.py:40
  98.6 0.0 copy-start.7
  98.6 1.2 copy-done.6
  99.8 0.5 copy-done.7
  100.2 5.4 %convolution_convert_fusion = bf16[2,1024,1536]{2,1,0:T(8,128)(2,1)} fusion(bf16[2,512,1024]{2,1,0:T(8,128)(2,1)S(1)} %bitcast.28, bf16[2,512,768]{2,1,0:T(8,128)(2,1)S(1)} %get-tuple-element.6, bf16[2,512,768]{2,1,0:T(8,128)(2,1)S(1)} %get-tuple-element.5), kind=kOutput, calls=%fused_computation.3 | convolution fusion | flops 3230662656 | bytes 11534336 | tf_op jit(solution)/shard_map/ksd,ksf->kdf/dot_general | solution.py:49
  105.7 0.0 reduce-scatter.3.cloned.1.call-update
  105.7 7.3 %fusion.2 = bf16[2,512,1024]{2,1,0:T(8,128)(2,1)S(1)} fusion(bf16[2,1024,1536]{2,1,0:T(8,128)(2,1)} %param.12, bf16[2,512,768]{2,1,0:T(8,128)(2,1)} %copy-done.7, bf16[2,512,768]{2,1,0:T(8,128)(2,1)} %copy-done.6), kind=kOutput, calls=%fused_computation.13 | convolution fusion | flops 3228565504 | bytes 11534336 | tf_op jit(solution)/shard_map/ksf,kdf->ksd/dot_general | solution.py:50
  113.0 3.6 %copy.24 = bf16[2,512,1024]{2,0,1:T(2,128)(2,1)} copy(bf16[2,512,1024]{2,1,0:T(8,128)(2,1)S(1)} %fusion.2) | data formatting | bytes 4194304 | tf_op jit(solution)/shard_map/convert_element_type | solution.py:52
  116.6 4.7 %all-to-all-start.2 = ((bf16[2,512,1024]{2,0,1:T(2,128)(2,1)}), bf16[2,512,1024]{2,0,1:T(2,128)(2,1)}, u32[]{:S(2)}, u32[]{:S(2)}) async-start(bf16[2,512,1024]{2,0,1:T(2,128)(2,1)} %copy.24), calls=%async_computation.2 | async-start | bytes 4194304 | tf_op jit(solution)/shard_map/all_to_all | solution.py:53
  121.3 24.1 %all-to-all-done.2 = bf16[2,512,1024]{2,0,1:T(2,128)(2,1)} async-done(((bf16[2,512,1024]{2,0,1:T(2,128)(2,1)}), bf16[2,512,1024]{2,0,1:T(2,128)(2,1)}, u32[]{:S(2)}, u32[]{:S(2)}) %all-to-all-start.2) | async-done | bytes 2097184 | tf_op jit(solution)/shard_map/all_to_all | solution.py:53
  145.4 3.6 %copy.25 = bf16[2,4,128,1024]{3,2,0,1:T(8,128)(2,1)} copy(bf16[2,4,128,1024]{3,0,2,1:T(2,128)(2,1)} %bitcast.9) | data formatting | bytes 4194304 | tf_op jit(solution)/shard_map/all_to_all | solution.py:53
  149.1 5.4 %gather_fusion = bf16[512,1024]{1,0:T(8,128)(2,1)} fusion(bf16[1024,1024]{1,0:T(8,128)(2,1)} %bitcast.24, s32[1024]{0:T(1024)S(1)} %pad_clamp_fusion), kind=kCustom, calls=%fused_computation | custom fusion | bytes 2099200 | tf_op jit(solution)/shard_map/gather | solution.py:54
  154.5 2.2 %reshape.66 = bf16[256,2,1024]{2,1,0:T(2,128)(2,1)} reshape(bf16[512,1024]{1,0:T(8,128)(2,1)} %gather_fusion) | data formatting | bytes 2097152 | tf_op jit(solution)/shard_map/reshape | solution.py:54
  156.7 4.6 %reduce_sum.12 = bf16[256,1024]{1,0:T(8,128)(2,1)} reduce(bf16[256,2,1024]{2,1,0:T(2,128)(2,1)} %reshape.66, bf16[]{:T(256)} %constant.5.clone.1), dimensions={1}, to_apply=%region_2.0 | reduce | flops 262144 | bytes 1572866 | tf_op jit(solution)/shard_map/reduce_sum | solution.py:55
  161.3 2.0 convert_element_type.36
  163.2 41.3 %reduce-scatter.3.cloned.1.call-done = bf16[2,128,1536]{2,1,0:T(8,128)(2,1)} async-done(((bf16[2,1024,1536]{2,1,0:T(8,128)(2,1)}), bf16[2,128,1536]{2,1,0:T(8,128)(2,1)}) %reduce-scatter.3.cloned.1.call-update) | async-done | bytes 786448 | tf_op jit(solution)/shard_map/reduce_scatter | solution.py:57
  204.6 2.5 %convert_element_type.33 = f32[2,128,1536]{2,1,0:T(8,128)} convert(bf16[2,128,1536]{2,1,0:T(8,128)(2,1)} %reduce-scatter.3.cloned.1.call-done) | non-fusion elementwise | flops 393216 | bytes 2359296 | tf_op jit(solution)/shard_map/convert_element_type | solution.py:59
  (9 shorter events, 0.0 us)
Async XLA Ops:
  7.2 85.5 %copy-start = (bf16[2,768,1024]{2,1,0:T(8,128)(2,1)S(1)}, bf16[2,768,1024]{2,1,0:T(8,128)(2,1)}, u32[]{:S(2)}) copy-start(bf16[2,768,1024]{2,1,0:T(8,128)(2,1)} %param.13) | copy-start | bytes 9437188
  13.1 10.0 %copy-start.4 = (f32[256,2]{0,1:T(2,128)S(1)}, f32[256,2]{0,1:T(2,128)}, u32[]{:S(2)}) copy-start(f32[256,2]{0,1:T(2,128)} %param.9) | copy-start | bytes 6148
  17.9 30.9 %all-to-all-start.1 = ((bf16[8,128,1024]{2,1,0:T(8,128)(2,1)}), bf16[8,128,1024]{2,1,0:T(8,128)(2,1)}, u32[]{:S(2)}, u32[]{:S(2)}) async-start(bf16[8,128,1024]{2,1,0:T(8,128)(2,1)} %bitcast.25), calls=%async_computation.1 | async-start | bytes 4194304 | tf_op jit(solution)/shard_map/all_to_all | solution.py:36
  48.8 29.1 %all-to-all-start = ((bf16[8,128,1024]{2,1,0:T(8,128)(2,1)}), bf16[8,128,1024]{2,1,0:T(8,128)(2,1)}, u32[]{:S(2)}, u32[]{:S(2)}) async-start(bf16[8,128,1024]{2,1,0:T(8,128)(2,1)} %bitcast.26), calls=%async_computation | async-start | bytes 4194304 | tf_op jit(solution)/shard_map/all_to_all | solution.py:37
  53.3 108.0 %reduce-scatter.5.cloned.1.call-start = ((), (), s32[]{:S(2)}) async-start(), calls=%async_computation.6 | async-start | bytes 3538944 | tf_op jit(solution)/shard_map/reduce_scatter | solution.py:60
  77.9 2.2 %copy-start.1 = (bf16[2,4,128,1024]{3,2,1,0:T(8,128)(2,1)S(1)}, bf16[2,4,128,1024]{3,2,1,0:T(8,128)(2,1)}, u32[]{:S(2)}) copy-start(bf16[2,4,128,1024]{3,2,1,0:T(8,128)(2,1)} %copy.23) | copy-start | bytes 6291460
  79.9 6.3 %copy-start.3 = (bf16[2,4,128,1024]{3,2,1,0:T(8,128)(2,1)}, bf16[2,4,128,1024]{3,2,1,0:T(8,128)(2,1)S(1)}, u32[]{:S(2)}) copy-start(bf16[2,4,128,1024]{3,2,1,0:T(8,128)(2,1)S(1)} %copy.22) | copy-start | bytes 6291460
  86.2 2.7 %copy-start.5 = (f32[2,512,1536]{2,1,0:T(8,128)}, f32[2,512,1536]{2,1,0:T(8,128)S(1)}, u32[]{:S(2)}) copy-start(f32[2,512,1536]{2,1,0:T(8,128)S(1)} %fusion.12) | copy-start | bytes 18874372
  92.6 112.0 %reduce-scatter.3.cloned.1.call-start = ((), (), s32[]{:S(2)}) async-start(), calls=%async_computation.5 | async-start | bytes 7077888 | tf_op jit(solution)/shard_map/reduce_scatter | solution.py:57
  92.7 7.6 %copy-start.2 = (bf16[2,4,128,1024]{3,2,1,0:T(8,128)(2,1)S(1)}, bf16[2,4,128,1024]{3,2,1,0:T(8,128)(2,1)}, u32[]{:S(2)}) copy-start(bf16[2,4,128,1024]{3,2,1,0:T(8,128)(2,1)} %copy.23) | copy-start | bytes 6291460
  98.6 1.2 copy-start.6
  98.6 1.7 copy-start.7
  116.6 28.8 %all-to-all-start.2 = ((bf16[2,512,1024]{2,0,1:T(2,128)(2,1)}), bf16[2,512,1024]{2,0,1:T(2,128)(2,1)}, u32[]{:S(2)}, u32[]{:S(2)}) async-start(bf16[2,512,1024]{2,0,1:T(2,128)(2,1)} %copy.24), calls=%async_computation.2 | async-start | bytes 4194304 | tf_op jit(solution)/shard_map/all_to_all | solution.py:53
Sparse Core Ops, SparseCore 0:
  92.7 40.5 reduce-scatter.4
  135.7 68.8 reduce-scatter.2
where the time goes:
time: 215 us; the launch traced here: 214 us
  waiting for transfers between devices  100 us (47%)
  local copies, waits for them, and re-layouts  41.2 us (19%)
  matrix products  28.4 us (13%)
  other arithmetic  15.1 us (7%)
  starting transfers between devices  14.6 us (7%)
  between operations  14.2 us (7%)
    reduce_scatter x1, waiting for transfers between devices, per_device(): lax.psum_scatter(term_in.astype(jnp.bfloat16), 'dp', scatter_dimension=1,...  41.3 us
    all_to_all x1, waiting for transfers between devices, per_device(): lax.all_to_all(returned, 'expert', split_axis=1, concat_axis=0, tiled=True)  24.1 us
    all_to_all x1, waiting for transfers between devices, per_device(): lax.all_to_all(send_scaled, 'expert', split_axis=0, concat_axis=1, tiled=...  21.4 us
    all_to_all x1, waiting for transfers between devices, per_device(): lax.all_to_all(send_inputs, 'expert', split_axis=0, concat_axis=1, tiled=...  13.6 us
    dot_general x1, matrix products, per_device(): jnp.einsum('ksf,kdf->ksd', grad_pair, w_in, preferred_element_type=jnp.fl...  7.3 us
    mul x3, local copies, waits for them, and re-layouts, per_device(): combine[:, :, None] * cotangent[:, None, :].astype(jnp.float32)  6.75 us
    dot_general x1, matrix products, recompute(): jnp.einsum('ksd,kdf->ksf', input_slots, w_in, preferred_element_type=jnp....  6.02 us
    dot_general x1, matrix products, per_device(): jnp.einsum('ksd,kfd->ksf', cotangent_slots, w_down, preferred_element_typ...  5.89 us
  transfers between devices with their start and end apart: 5, of which 4 were waited for; matrix products, arithmetic and copies ran while one was open for 26% of the time, Pallas kernels for 0%

commit v1 on v0

v1 whole, which is shorter than its diff:
```python
import functools

import jax
import jax.numpy as jnp
from jax import lax
from jax.experimental import pallas as pl
from jax.experimental.pallas import tpu as pltpu
from jax.sharding import PartitionSpec as P

TOP = 2
BF = jnp.bfloat16
F32 = jnp.float32
VMEM_BYTES = 40 * 1024 * 1024


def dot(a, b):
    return jnp.dot(a, b, preferred_element_type=F32)


def dot_nt(a, b):
    return lax.dot_general(a, b, (((1,), (1,)), ((), ())), preferred_element_type=F32)


def call(body, grid, in_specs, out_specs, out_shape, scratch, flops, moved, *args):
    return pl.pallas_call(
        body,
        out_shape=out_shape,
        grid_spec=pltpu.PrefetchScalarGridSpec(
            num_scalar_prefetch=1,
            grid=grid,
            in_specs=in_specs,
            out_specs=out_specs,
            scratch_shapes=scratch,
        ),
        compiler_params=pltpu.CompilerParams(vmem_limit_bytes=VMEM_BYTES),
        cost_estimate=pl.CostEstimate(flops=flops, bytes_accessed=moved, transcendentals=0),
    )(*args)


def whole(array):
    return pl.BlockSpec(array.shape, lambda e, scal: (0,) * array.ndim)


def per_expert(shape):
    return pl.BlockSpec((1,) + tuple(shape), lambda e, scal: (e,) + (0,) * len(shape))


def load_source(refs, parts, rows):
    blocks = [refs[ref][pl.ds(first, count), :] for ref, first, count in parts]
    return blocks[0] if len(blocks) == 1 else jnp.concatenate(blocks, axis=0)


def forward_body(layout, cap, tile, scal, route, *refs):
    pieces = refs[: layout["pieces"]]
    w_in = refs[layout["pieces"]]
    rows_t, hidden_t, scale_gate, scale_up, onehot, onehot_t, weight = refs[layout["pieces"] + 1 :]
    width = w_in.shape[1]
    ff = w_in.shape[2] // 2
    expert = pl.program_id(0)
    base = (scal[0] + expert * cap).astype(F32)
    tokens = route.shape[2]
    slot = lax.broadcasted_iota(jnp.int32, (cap, tokens), 0).astype(F32) + base
    gathered = []
    for s, parts in enumerate(layout["sources"]):
        first = slot == route[s, 0:1, :]
        second = slot == route[s, 1:2, :]
        hit = jnp.where(jnp.logical_or(first, second), 1.0, 0.0)
        factor = jnp.where(first, route[s, 2:3, :], 0.0) + jnp.where(second, route[s, 3:4, :], 0.0)
        factor = jnp.sum(factor, axis=1, keepdims=True)
        place = pl.ds(s * cap, cap)
        onehot[0, place, :] = hit.astype(BF)
        onehot_t[0, s] = jnp.transpose(hit).astype(BF)
        weight[0, place, :] = jnp.broadcast_to(factor, (cap, 128))
        gathered.append(dot(hit.astype(BF), load_source(pieces, parts, tokens)).astype(BF))
    rows = jnp.concatenate(gathered, axis=0)
    rows_t[0] = jnp.transpose(rows)
    for f in range(0, ff, tile):
        gate = dot(rows, w_in[0, :, pl.ds(f, tile)])
        upper = dot(rows, w_in[0, :, pl.ds(ff + f, tile)])
        sg = jax.nn.sigmoid(gate)
        activated = gate * sg
        hidden_t[0, pl.ds(f, tile), :] = jnp.transpose((activated * upper).astype(BF))
        scale_gate[0, :, pl.ds(f, tile)] = (upper * sg * (1.0 + gate * (1.0 - sg))).astype(BF)
        scale_up[0, :, pl.ds(f, tile)] = activated.astype(BF)


def cotangent_body(layout, cap, nz, start, last, scal, onehot, weight, hidden_t, *refs):
    refs = list(refs)
    pieces = [refs.pop(0) for _ in range(layout["pieces"])]
    w_down = refs.pop(0)
    if not start:
        before = refs.pop(0)
    if last:
        scale_gate, scale_up = refs.pop(0), refs.pop(0)
    give, keep, after = refs
    expert = pl.program_id(0)
    slots = []
    for s, parts in enumerate(layout["sources"]):
        place = pl.ds(s * cap, cap)
        block = load_source(pieces, parts, onehot.shape[2])
        factor = weight[0, place, 0:1]
        slots.append((dot(onehot[0, place, :], block) * factor).astype(BF))
    slots = jnp.concatenate(slots, axis=0)
    part = give.shape[2]
    for out, offset in ((give, scal[2]), (keep, scal[1])):
        left = []
        for t in range(nz):
            shard = scal[3 + t + nz * expert]
            left.append(hidden_t[0, pl.ds(pl.multiple_of((2 * shard + offset) * part, 16), part), :])
        result = dot(jnp.concatenate(left, axis=0), slots).astype(BF)
        for t in range(nz):
            out[t, 0] = result[t * part : (t + 1) * part]
    grad_hidden = dot_nt(slots, w_down[0])
    if not start:
        grad_hidden = grad_hidden + before[0]
    if last:
        ff = scale_gate.shape[2]
        after[0, :, pl.ds(0, ff)] = (grad_hidden * scale_gate[0].astype(F32)).astype(BF)
        after[0, :, pl.ds(ff, ff)] = (grad_hidden * scale_up[0].astype(F32)).astype(BF)
    else:
        after[0] = grad_hidden


def input_weight_body(nz, steps, scal, rows_t, pair, give, keep):
    expert = pl.program_id(0)
    part = give.shape[2]
    left = []
    for t in steps:
        shard = scal[3 + t + nz * expert]
        for offset in (scal[2], scal[1]):
            left.append(rows_t[0, pl.ds(pl.multiple_of((2 * shard + offset) * part, 16), part), :])
    left = jnp.concatenate(left, axis=0)
    for f in range(0, pair.shape[2], 256):
        result = dot(left, pair[0, :, pl.ds(f, 256)]).astype(BF)
        for t in range(len(steps)):
            give[t, 0, :, pl.ds(f, 256)] = result[2 * t * part : (2 * t + 1) * part]
            keep[t, 0, :, pl.ds(f, 256)] = result[(2 * t + 1) * part : (2 * t + 2) * part]


def returned_body(outputs, cap, experts, scal, pair, w_in, onehot_t, *refs):
    outs, total = refs[:-1], refs[-1]
    expert = pl.program_id(0)
    sources = onehot_t.shape[1]
    width = w_in.shape[1]
    for n in range(0, width, 256):
        returned = dot_nt(pair[0], w_in[0, pl.ds(n, 256), :]).astype(BF)
        for s in range(sources):
            share = dot(onehot_t[0, s], returned[s * cap : (s + 1) * cap])

            @pl.when(expert == 0)
            def _():
                total[s, :, pl.ds(n, 256)] = share

            @pl.when(expert > 0)
            def _():
                total[s, :, pl.ds(n, 256)] += share

    @pl.when(expert == experts - 1)
    def _():
        for out, index, s, first, count in outputs:
            outs[out][index] = total[s, pl.ds(first, count), :].astype(BF)


def gather_blocks(block, n):
    rows = block.shape[0]
    if n != 4:
        everything = lax.all_gather(block, "expert", tiled=True)
        return [everything], [[(0, s * rows, rows)] for s in range(n)]
    half = rows // 2
    low, high = block[:half], block[half:]
    across_x = functools.partial(lax.ppermute, axis_name="expert", perm=[(i, i ^ 1) for i in range(4)])
    across_y = functools.partial(lax.ppermute, axis_name="expert", perm=[(i, i ^ 2) for i in range(4)])
    x_low, y_high = across_x(low), across_y(high)
    x_high, y_low = across_x(high), across_y(low)
    d_low, d_high = across_y(x_low), across_x(y_high)
    pieces = [block, x_low, x_high, y_low, y_high, d_low, d_high]
    sources = [[(0, 0, rows)]] + [[(k, 0, half), (k + 1, 0, half)] for k in (1, 3, 5)]
    return pieces, sources


def gather_routes(route, n):
    if n != 4:
        return lax.all_gather(route, "expert")
    others = [lax.ppermute(route, "expert", [(i, i ^ k) for i in range(4)]) for k in (1, 2, 3)]
    return jnp.stack([route] + others)


def add(*terms):
    return functools.reduce(jnp.add, [t.astype(F32) for t in terms])


def ring_sum(own, nz, experts):
    half = experts // 2
    up = [(i, (i + 2) % (2 * nz)) for i in range(2 * nz)]
    down = [(j, i) for i, j in up]
    held = [None, None]
    for t in range(nz):
        sums = []
        for way, chosen in enumerate((slice(0, half), slice(half, experts))):
            terms = [x[chosen] for x in own(t)]
            if held[way] is not None:
                terms.append(held[way])
            sums.append(add(*terms))
        if t == nz - 1:
            return jnp.concatenate(sums, axis=0)
        held = [
            lax.ppermute(total.astype(BF), "dp", perm) for total, perm in zip(sums, (up, down))
        ]


def per_device(column_parts, tokens, cotangent, route_logits, expert_ids, slot_pos, w_in, w_down):
    token_count, width = tokens.shape
    experts, ff = w_down.shape[:2]
    n = lax.axis_size("expert")
    ndp = lax.axis_size("dp")
    nz = ndp // 2
    cap = 2 * TOP * token_count // (experts * n)
    slots = n * cap
    place = lax.axis_index("dp")
    z, core = place // 2, place % 2
    swap = functools.partial(
        lax.ppermute, axis_name="dp", perm=[(i, i ^ 1) for i in range(ndp)]
    )

    token_pieces, token_sources = gather_blocks(tokens, n)
    first = jax.nn.sigmoid(route_logits[:, 0] - route_logits[:, 1])
    destination = (expert_ids * cap + slot_pos).astype(F32)
    route = jnp.stack([destination[:, 0], destination[:, 1], first, 1.0 - first])
    route = gather_routes(jnp.concatenate([route, jnp.zeros_like(route)]), n)
    columns = width // column_parts
    cot_parts = [
        gather_blocks(cotangent[:, k * columns : (k + 1) * columns], n) for k in range(column_parts)
    ]

    steps = jnp.arange(1, nz + 1)
    ups = (z - steps) % nz
    downs = (z + steps) % nz
    scal = jnp.concatenate(
        [jnp.stack([lax.axis_index("expert") * experts * cap, core, 1 - core])]
        + [ups] * (experts // 2)
        + [downs] * (experts - experts // 2)
    ).astype(jnp.int32)

    s3 = lambda *shape: jax.ShapeDtypeStruct(shape, BF)
    layout = dict(pieces=len(token_pieces), sources=token_sources)
    macs = experts * slots * width * ff
    rows_t, hidden_t, scale_gate, scale_up, onehot, onehot_t, weight = call(
        functools.partial(forward_body, layout, cap, 256),
        (experts,),
        [whole(route)] + [whole(p) for p in token_pieces] + [per_expert(w_in.shape[1:])],
        [
            per_expert((width, slots)),
            per_expert((ff, slots)),
            per_expert((slots, ff)),
            per_expert((slots, ff)),
            per_expert((slots, token_count)),
            per_expert((n, token_count, cap)),
            per_expert((slots, 128)),
        ],
        [
            s3(experts, width, slots),
            s3(experts, ff, slots),
            s3(experts, slots, ff),
            s3(experts, slots, ff),
            s3(experts, slots, token_count),
            s3(experts, n, token_count, cap),
            jax.ShapeDtypeStruct((experts, slots, 128), F32),
        ],
        [],
        4 * macs,
        16 << 20,
        scal,
        route,
        *token_pieces,
        w_in,
    )

    down_rows = ff // ndp
    in_rows = width // ndp
    after = None
    downs_given = []
    for k, (pieces, sources) in enumerate(cot_parts):
        start, last = k == 0, k == column_parts - 1
        layout = dict(pieces=len(pieces), sources=sources)
        piece_of = pl.BlockSpec((1, ff, columns), functools.partial(lambda k, e, scal: (e, 0, k), k))
        stepwise = pl.BlockSpec((nz, 1, down_rows, columns), lambda e, scal: (0, e, 0, 0))
        extra = [] if start else [after]
        if last:
            extra += [scale_gate, scale_up]
        after_shape = (experts, slots, 2 * ff) if last else (experts, slots, ff)
        give, keep, after = call(
            functools.partial(cotangent_body, layout, cap, nz, start, last),
            (experts,),
            [per_expert(onehot.shape[1:]), per_expert(weight.shape[1:]), per_expert(hidden_t.shape[1:])]
            + [whole(p) for p in pieces]
            + [piece_of]
            + [per_expert(x.shape[1:]) for x in extra],
            [stepwise, stepwise, per_expert(after_shape[1:])],
            [s3(nz, experts, down_rows, columns)] * 2
            + [jax.ShapeDtypeStruct(after_shape, BF if last else F32)],
            [],
            4 * macs // column_parts,
            8 << 20,
            scal,
            onehot,
            weight,
            hidden_t,
            *pieces,
            w_down,
            *extra,
        )
        downs_given.append((keep, swap(give)))
    pair = after

    ins_given = []
    for chosen in ((0,), tuple(range(1, nz))):
        stepwise = pl.BlockSpec((len(chosen), 1, in_rows, 2 * ff), lambda e, scal: (0, e, 0, 0))
        give, keep = call(
            functools.partial(input_weight_body, nz, chosen),
            (experts,),
            [per_expert(rows_t.shape[1:]), per_expert(pair.shape[1:])],
            [stepwise, stepwise],
            [s3(len(chosen), experts, in_rows, 2 * ff)] * 2,
            [],
            4 * macs * len(chosen) // nz,
            8 << 20,
            scal,
            rows_t,
            pair,
        )
        other = swap(give)
        ins_given += [(keep[t], other[t]) for t in range(len(chosen))]

    if n == 4:
        half = token_count // 2
        outputs = [
            (0, 0, 2, 0, half),
            (0, 1, 3, 0, half),
            (1, 0, 1, half, half),
            (1, 1, 3, half, half),
            (2, 0, 0, 0, half),
            (2, 1, 1, 0, half),
            (3, 0, 0, half, half),
            (3, 1, 2, half, half),
        ]
        out_shapes = [s3(2, half, width)] * 4
    else:
        outputs = [(0, s, s, 0, token_count) for s in range(n)]
        out_shapes = [s3(n, token_count, width)]
    shares = call(
        functools.partial(returned_body, outputs, cap, experts),
        (experts,),
        [per_expert(pair.shape[1:]), per_expert(w_in.shape[1:]), per_expert(onehot_t.shape[1:])],
        [whole(x) for x in out_shapes],
        out_shapes,
        [pltpu.VMEM((n, token_count, width), F32)],
        4 * macs,
        16 << 20,
        scal,
        pair,
        w_in,
        onehot_t,
    )
    if n == 4:
        across_x = functools.partial(lax.ppermute, axis_name="expert", perm=[(i, i ^ 1) for i in range(4)])
        across_y = functools.partial(lax.ppermute, axis_name="expert", perm=[(i, i ^ 2) for i in range(4)])
        to_y, to_x, low, high = shares
        from_y, from_x = across_y(to_y), across_x(to_x)
        low_x = across_x(add(low[1], from_y[1]).astype(BF))
        high_y = across_y(add(high[1], from_x[1]).astype(BF))
        input_grad = jnp.concatenate(
            [add(low[0], from_y[0], low_x), add(high[0], from_x[0], high_y)], axis=0
        ).astype(BF)
    else:
        input_grad = lax.psum_scatter(shares[0], "expert", scatter_dimension=0)

    grad_down = jnp.concatenate(
        [ring_sum(lambda t: (keep[t], other[t]), nz, experts) for keep, other in downs_given], axis=2
    )
    grad_in = ring_sum(lambda t: ins_given[t], nz, experts)
    return (input_grad, grad_in, grad_down)


def solution(mesh):
    in_specs = (
        P(("dp", "expert"), None),
        P(("dp", "expert"), None),
        P(("dp", "expert"), None),
        P(("dp", "expert"), None),
        P(("dp", "expert"), None),
        P("expert", None, None),
        P("expert", None, None),
    )
    out_specs = (P(("dp", "expert"), None), P("expert", "dp", None), P("expert", "dp", None))
    return jax.shard_map(
        functools.partial(per_device, 2),
        mesh=mesh,
        in_specs=in_specs,
        out_specs=out_specs,
        check_vma=False,
    )
```

time: 215 us -> 202 us (0.940)
  starting transfers between devices: 14.6 us -> 66.5 us
  Pallas kernels: 0 us -> 36.2 us
  waiting for transfers between devices: 100 us -> 70.1 us
  matrix products: 28.4 us -> 0 us
  local copies, waits for them, and re-layouts: 41.2 us -> 21.1 us
  between operations: 14.2 us -> 1.06 us
  other arithmetic: 15.1 us -> 6.46 us
    ppermute x0 -> x47, waiting for transfers between devices: none -> 70.1 us  [the longest x18 49.3 us: ring_sum(): lax.ppermute(total.astype(BF), 'dp', perm)]
    ppermute x0 -> x47, starting transfers between devices: none -> 66.5 us  [the longest x18 32.6 us: ring_sum(): lax.ppermute(total.astype(BF), 'dp', perm)]
    all_to_all x3 -> x0, waiting for transfers between devices: 59.1 us -> none  [the longest x1 24.1 us: per_device(): lax.all_to_all(returned, 'expert', split_axis=1, concat_axis=0, tiled=True)]
    reduce_scatter x2 -> x0, waiting for transfers between devices: 41.3 us -> none  [the longest x1 41.3 us: per_device(): lax.psum_scatter(term_in.astype(jnp.bfloat16), 'dp', scatter_dimension=1,...]
    pallas_call x0 -> x6, Pallas kernels: none -> 36.2 us  [call(): pl.pallas_call(body, out_shape=out_shape, grid_spec=pltpu.PrefetchScalarG...]
    dot_general x5 -> x0, matrix products: 28.4 us -> none  [the longest x1 7.3 us: per_device(): jnp.einsum('ksf,kdf->ksd', grad_pair, w_in, preferred_element_type=jnp.fl...]
    all_to_all x3 -> x0, starting transfers between devices: 14.3 us -> none  [the longest x1 5.16 us: per_device(): lax.all_to_all(send_inputs, 'expert', split_axis=0, concat_axis=1, tiled=...]
    unnamed x16 -> x52, local copies, waits for them, and re-layouts: 4.54 us -> 17.2 us
  transfers between devices with their start and end apart: 5 -> 47, of which waited for: 4 -> 17; matrix products, arithmetic and copies ran while one was open for 26% -> 4% of each run, Pallas kernels for 0% -> 8%
where the time goes in v1:
time: 202 us; the launch traced here: 201 us
  waiting for transfers between devices  70.1 us (35%)
  starting transfers between devices  66.5 us (33%)
  Pallas kernels  36.2 us (18%)
  local copies, waits for them, and re-layouts  21.1 us (10%)
  other arithmetic  6.46 us (3%)
    ppermute x18, waiting for transfers between devices, ring_sum(): lax.ppermute(total.astype(BF), 'dp', perm)  49.3 us
    pallas_call x6, Pallas kernels, call(): pl.pallas_call(body, out_shape=out_shape, grid_spec=pltpu.PrefetchScalarG...  36.2 us
    ppermute x18, starting transfers between devices, ring_sum(): lax.ppermute(total.astype(BF), 'dp', perm)  32.6 us
    unnamed x52, local copies, waits for them, and re-layouts  17.2 us
    ppermute x6, starting transfers between devices, gather_blocks(): x_high, y_low = (across_x(high), across_y(low))  7.97 us
    ppermute x6, starting transfers between devices, gather_blocks(): d_low, d_high = (across_y(x_low), across_x(y_high))  7.94 us
    ppermute x6, starting transfers between devices, gather_blocks(): x_low, y_high = (across_x(low), across_y(high))  7.06 us
    ppermute x2, waiting for transfers between devices, per_device(): from_y, from_x = (across_y(to_y), across_x(to_x))  6.62 us
  transfers between devices with their start and end apart: 47, of which 17 were waited for; matrix products, arithmetic and copies ran while one was open for 4% of the time, Pallas kernels for 8%

profile of v1, /device:TPU:0, one launch (start us, length us, event | category | flops | bytes accessed | tf_op | source)
XLA Modules:
  0.0 201.3 jit_solution(10635987193686795525)
XLA Ops:
  1.8 3.0 %collective-permute-start.3 = (bf16[128,1024]{1,0:T(8,128)(2,1)S(1)}, bf16[128,1024]{1,0:T(8,128)(2,1)S(1)}, u32[]{:S(2)}, u32[]{:S(2)}) collective-permute-start(bf16[128,1024]{1,0:T(8,128)(2,1)S(1)} %get-tuple-element.66), channel_id=1, source_target_pairs={{0,1},{1,0},{2,3},{3,2},{4,5},{5,4},{6,7},{7,6},{8,9},{9,8},{10,11... | collective-permute-start | bytes 786440 | tf_op jit(solution)/shard_map/ppermute | solution.py:173
  4.8 1.5 collective-permute-start.6
  6.3 1.9 fusion.24
  10.2 1.6 collective-permute-start
  12.3 1.8 collective-permute-done
  14.1 2.7 %collective-permute-start.2 = (f32[8,256]{1,0:T(8,128)S(1)}, f32[8,256]{1,0:T(8,128)S(1)}, u32[]{:S(2)}, u32[]{:S(2)}) collective-permute-start(f32[8,256]{1,0:T(8,128)S(1)} %concatenate.23), channel_id=1, source_target_pairs={{0,3},{1,2},{2,1},{3,0},{4,7},{5,6},{6,5},{7,4},{8,11},{9,10},{10,... | collective-permute-start | bytes 24584 | tf_op jit(solution)/shard_map/ppermute | solution.py:184
  17.3 1.3 collective-permute-done.2
  18.6 1.8 collective-permute-start.5
  20.7 1.8 collective-permute-start.7
  22.5 1.6 collective-permute-start.8
  24.8 5.7 %collective-permute-done.18.refs_4_ = bf16[128,512]{1,0:T(8,128)(2,1)} collective-permute-done((bf16[128,512]{1,0:T(8,128)(2,1)S(1)}, bf16[128,512]{1,0:T(8,128)(2,1)}, u32[]{:S(2)}, u32[]{:S(2)}) %collective-permute-start.18) | collective-permute-done | bytes 131104 | tf_op jit(solution)/shard_map/ppermute | solution.py:173
  30.6 1.5 collective-permute-start.16
  32.2 3.4 %collective-permute-done.16.refs_2_ = bf16[128,512]{1,0:T(8,128)(2,1)S(1)} collective-permute-done((bf16[128,512]{1,0:T(8,128)(2,1)S(1)}, bf16[128,512]{1,0:T(8,128)(2,1)S(1)}, u32[]{:S(2)}, u32[]{:S(2)}) %collective-permute-start.16) | collective-permute-done | bytes 131104 | tf_op jit(solution)/shard_map/ppermute | solution.py:174
  36.3 2.3 %collective-permute-start.17 = (bf16[128,512]{1,0:T(8,128)(2,1)}, bf16[128,512]{1,0:T(8,128)(2,1)S(1)}, u32[]{:S(2)}, u32[]{:S(2)}) collective-permute-start(bf16[128,512]{1,0:T(8,128)(2,1)} %get-tuple-element.62), channel_id=1, source_target_pairs={{0,2},{1,3},{2,0},{3,1},{4,6},{5,7},{6,4},{7,5},{8,10},{9,11},{10,... | collective-permute-start | bytes 393224 | tf_op jit(solution)/shard_map/ppermute | solution.py:174
  39.3 1.8 collective-permute-start.9
  42.5 2.0 %collective-permute-start.19 = (bf16[128,512]{1,0:T(8,128)(2,1)S(1)}, bf16[128,512]{1,0:T(8,128)(2,1)S(1)}, u32[]{:S(2)}, u32[]{:S(2)}) collective-permute-start(bf16[128,512]{1,0:T(8,128)(2,1)S(1)} %collective-permute-done.15.refs_1_), channel_id=1, source_target_pairs={{0,2},{1,3},{2,0},{3,1},{4,6},{5,7},{6,4},{7,5},{8,10},{9,11},{10,... | collective-permute-start | bytes 393224 | tf_op jit(solution)/shard_map/ppermute | solution.py:175
  52.3 7.2 %shard_map.94 = (bf16[2,1024,512]{2,1,0:T(8,128)(2,1)S(1)}, bf16[2,768,512]{2,1,0:T(8,128)(2,1)S(1)}, bf16[2,512,768]{2,1,0:T(8,128)(2,1)S(1)}, bf16[2,512,768]{...) custom-call(s32[11]{0:T(128)S(1)} %concatenate.22.scal, ...), custom_call_target="tpu_custom_call" | custom-call | flops 3221225472 | bytes 16777216 | tf_op jit(solution)/shard_map/pallas_call | solution.py:25
  60.3 1.8 collective-permute-start.10
  62.1 2.0 %collective-permute-start.13 = (bf16[128,512]{1,0:T(8,128)(2,1)S(1)}, bf16[128,512]{1,0:T(8,128)(2,1)S(1)}, u32[]{:S(2)}, u32[]{:S(2)}) collective-permute-start(bf16[128,512]{1,0:T(8,128)(2,1)S(1)} %collective-permute-done.9.refs_1_), channel_id=1, source_target_pairs={{0,2},{1,3},{2,0},{3,1},{4,6},{5,7},{6,4},{7,5},{8,10},{9,11},{10,... | collective-permute-start | bytes 393224 | tf_op jit(solution)/shard_map/ppermute | solution.py:175
  64.4 4.1 %shard_map.95 = (bf16[4,2,96,512]{3,2,1,0:T(8,128)(2,1)S(1)}, bf16[4,2,96,512]{3,2,1,0:T(8,128)(2,1)S(1)}, f32[2,512,768]{2,1,0:T(8,128)S(1)}) custom-call(s32[11]{0:T(128)S(1)} %concatenate.22.scal, bf16[2,512,256]{2,1,0:T(8,128)(2,1)S(1)} %get-tuple-element.24.onehot, f32[2,512,128]{2,1,0:T(8,128)S(1)} %get-tuple-element.25.weight, ...), custom_call_target="tpu_custom_call" | custom-call | flops 1610612736 | bytes 8388608 | tf_op jit(solution)/shard_map/pallas_call | solution.py:25
  68.4 1.6 copy-done.1
  71.9 5.0 %shard_map.96 = (bf16[4,2,96,512]{3,2,1,0:T(8,128)(2,1)S(1)}, bf16[4,2,96,512]{3,2,1,0:T(8,128)(2,1)S(1)}, bf16[2,512,1536]{2,1,0:T(8,128)(2,1)S(1)}) custom-call(s32[11]{0:T(128)S(1)} %concatenate.22.scal, bf16[2,512,256]{2,1,0:T(8,128)(2,1)S(1)} %get-tuple-element.24.onehot, f32[2,512,128]{2,1,0:T(8,128)S(1)} %get-tuple-element.25.weight, ...), custom_call_target="tpu_custom_call" | custom-call | flops 1610612736 | bytes 8388608 | tf_op jit(solution)/shard_map/pallas_call | solution.py:25
  76.9 2.8 %copy-done.8 = bf16[2,1024,1536]{2,1,0:T(8,128)(2,1)S(1)} copy-done((bf16[2,1024,1536]{2,1,0:T(8,128)(2,1)S(1)}, bf16[2,1024,1536]{2,1,0:T(8,128)(2,1)}, u32[]{:S(2)}) %copy-start.8) | copy-done | bytes 6291480
  79.7 14.6 %shard_map.97 = (bf16[2,128,1024]{2,1,0:T(8,128)(2,1)S(1)}, bf16[2,128,1024]{2,1,0:T(8,128)(2,1)S(1)}, bf16[2,128,1024]{2,1,0:T(8,128)(2,1)S(1)}, bf16[2,128,1024]{2,1,0:T(8,128)(2,1)S(1)}) custom-call(s32[11]{0:T(128)S(1)} %concatenate.22.scal, bf16[2,512,1536]{2,1,0:T(8,128)(2,1)S(1)} %get-tuple-element.30.pair, bf16[2,1024,1536]{2,1,0:T(8,128)(2,1)S(1)} %copy-done.8, ...), custom_call_target="tpu_custom_call" | custom-call | flops 3221225472 | bytes 16777216 | tf_op jit(solution)/shard_map/pallas_call | solution.py:25
  94.9 1.8 collective-permute-start.23
  96.7 3.6 %shard_map.98 = (bf16[3,2,128,1536]{3,2,1,0:T(8,128)(2,1)S(1)}, bf16[3,2,128,1536]{3,2,1,0:T(8,128)(2,1)S(1)}) custom-call(s32[11]{0:T(128)S(1)} %concatenate.22.scal, bf16[2,1024,512]{2,1,0:T(8,128)(2,1)S(1)} %get-tuple-element.36.rows_t, bf16[2,512,1536]{2,1,0:T(8,128)(2,1)S(1)} %get-tuple-element.30.pair), custom_call_target="tpu_custom_call" | custom-call | flops 2415919104 | bytes 8388608 | tf_op jit(solution)/shard_map/pallas_call | solution.py:25
  100.4 1.7 shard_map.99
  102.1 1.3 collective-permute-done.21
  103.6 5.3 %collective-permute-done.23 = bf16[2,128,1024]{2,1,0:T(8,128)(2,1)S(1)} collective-permute-done((bf16[2,128,1024]{2,1,0:T(8,128)(2,1)S(1)}, bf16[2,128,1024]{2,1,0:T(8,128)(2,1)S(1)}, u32[]{:S(2)}, u32[]{:S(2)}) %collective-permute-start.23) | collective-permute-done | bytes 524320 | tf_op jit(solution)/shard_map/ppermute | solution.py:368
  108.8 1.7 collective-permute-start.22
  110.7 1.9 collective-permute-start.24
  112.7 1.8 collective-permute-start.34
  114.5 1.8 collective-permute-done.22
  116.3 3.6 %collective-permute-start.37 = (bf16[1,96,512]{2,1,0:T(8,128)(2,1)S(1)}, bf16[1,96,512]{2,1,0:T(8,128)(2,1)S(1)}, u32[]{:S(2)}, u32[]{:S(2)}) collective-permute-start(bf16[1,96,512]{2,1,0:T(8,128)(2,1)S(1)} %get-tuple-element.52), channel_id=1, source_target_pairs={{8,0},{12,4},{16,8},{20,12},{24,16},{28,20},{0,24},{4,28},{9,1},{1... | collective-permute-start | bytes 294920 | tf_op jit(solution)/shard_map/ppermute | solution.py:207
  120.2 3.9 %collective-permute-start.44 = (bf16[1,96,512]{2,1,0:T(8,128)(2,1)S(1)}, bf16[1,96,512]{2,1,0:T(8,128)(2,1)S(1)}, u32[]{:S(2)}, u32[]{:S(2)}) collective-permute-start(bf16[1,96,512]{2,1,0:T(8,128)(2,1)S(1)} %get-tuple-element.56), channel_id=1, source_target_pairs={{8,0},{12,4},{16,8},{20,12},{24,16},{28,20},{0,24},{4,28},{9,1},{1... | collective-permute-start | bytes 294920 | tf_op jit(solution)/shard_map/ppermute | solution.py:207
  125.2 1.4 collective-permute-done.41
  126.6 2.4 %collective-permute-start.30 = (bf16[1,128,1536]{2,1,0:T(8,128)(2,1)S(1)}, bf16[1,128,1536]{2,1,0:T(8,128)(2,1)S(1)}, u32[]{:S(2)}, u32[]{:S(2)}) collective-permute-start(bf16[1,128,1536]{2,1,0:T(8,128)(2,1)S(1)} %get-tuple-element.58), channel_id=1, source_target_pairs={{8,0},{12,4},{16,8},{20,12},{24,16},{28,20},{0,24},{4,28},{9,1},{1... | collective-permute-start | bytes 1179656 | tf_op jit(solution)/shard_map/ppermute | solution.py:207
  129.1 9.9 %collective-permute-done.27 = bf16[1,128,1536]{2,1,0:T(8,128)(2,1)S(1)} collective-permute-done((bf16[1,128,1536]{2,1,0:T(8,128)(2,1)S(1)}, bf16[1,128,1536]{2,1,0:T(8,128)(2,1)S(1)}, u32[]{:S(2)}, u32[]{:S(2)}) %collective-permute-start.27) | collective-permute-done | bytes 393248 | tf_op jit(solution)/shard_map/ppermute | solution.py:207
  139.1 8.5 %collective-permute-done.35 = bf16[1,96,512]{2,1,0:T(8,128)(2,1)S(1)} collective-permute-done((bf16[1,96,512]{2,1,0:T(8,128)(2,1)S(1)}, bf16[1,96,512]{2,1,0:T(8,128)(2,1)S(1)}, u32[]{:S(2)}, u32[]{:S(2)}) %collective-permute-start.35) | collective-permute-done | bytes 98336 | tf_op jit(solution)/shard_map/ppermute | solution.py:207
  148.7 1.6 collective-permute-start.36
  150.4 8.4 %collective-permute-done.28 = bf16[1,128,1536]{2,1,0:T(8,128)(2,1)S(1)} collective-permute-done((bf16[1,128,1536]{2,1,0:T(8,128)(2,1)S(1)}, bf16[1,128,1536]{2,1,0:T(8,128)(2,1)S(1)}, u32[]{:S(2)}, u32[]{:S(2)}) %collective-permute-start.28) | collective-permute-done | bytes 393248 | tf_op jit(solution)/shard_map/ppermute | solution.py:207
  160.5 3.1 %collective-permute-start.38 = (bf16[1,96,512]{2,1,0:T(8,128)(2,1)S(1)}, bf16[1,96,512]{2,1,0:T(8,128)(2,1)S(1)}, u32[]{:S(2)}, u32[]{:S(2)}) collective-permute-start(bf16[1,96,512]{2,1,0:T(8,128)(2,1)S(1)} %get-tuple-element.50), channel_id=1, source_target_pairs={{8,0},{12,4},{16,8},{20,12},{24,16},{28,20},{0,24},{4,28},{9,1},{1... | collective-permute-start | bytes 294920 | tf_op jit(solution)/shard_map/ppermute | solution.py:207
  163.6 2.8 %collective-permute-done.43 = bf16[1,96,512]{2,1,0:T(8,128)(2,1)S(1)} collective-permute-done((bf16[1,96,512]{2,1,0:T(8,128)(2,1)S(1)}, bf16[1,96,512]{2,1,0:T(8,128)(2,1)S(1)}, u32[]{:S(2)}, u32[]{:S(2)}) %collective-permute-start.43) | collective-permute-done | bytes 98336 | tf_op jit(solution)/shard_map/ppermute | solution.py:207
  166.5 6.2 %collective-permute-done.29 = bf16[1,128,1536]{2,1,0:T(8,128)(2,1)S(1)} collective-permute-done((bf16[1,128,1536]{2,1,0:T(8,128)(2,1)S(1)}, bf16[1,128,1536]{2,1,0:T(8,128)(2,1)S(1)}, u32[]{:S(2)}, u32[]{:S(2)}) %collective-permute-start.29) | collective-permute-done | bytes 393248 | tf_op jit(solution)/shard_map/ppermute | solution.py:207
  172.9 10.1 %collective-permute-start.31 = (bf16[1,128,1536]{2,1,0:T(8,128)(2,1)S(1)}, bf16[1,128,1536]{2,1,0:T(8,128)(2,1)S(1)}, u32[]{:S(2)}, u32[]{:S(2)}) collective-permute-start(bf16[1,128,1536]{2,1,0:T(8,128)(2,1)S(1)} %get-tuple-element.48), channel_id=1, source_target_pairs={{8,0},{12,4},{16,8},{20,12},{24,16},{28,20},{0,24},{4,28},{9,1},{1... | collective-permute-start | bytes 1179656 | tf_op jit(solution)/shard_map/ppermute | solution.py:207
  183.5 6.6 %collective-permute-done.31 = bf16[1,128,1536]{2,1,0:T(8,128)(2,1)S(1)} collective-permute-done((bf16[1,128,1536]{2,1,0:T(8,128)(2,1)S(1)}, bf16[1,128,1536]{2,1,0:T(8,128)(2,1)S(1)}, u32[]{:S(2)}, u32[]{:S(2)}) %collective-permute-start.31) | collective-permute-done | bytes 393248 | tf_op jit(solution)/shard_map/ppermute | solution.py:207
  190.3 4.3 %collective-permute-start.32 = (bf16[1,128,1536]{2,1,0:T(8,128)(2,1)S(1)}, bf16[1,128,1536]{2,1,0:T(8,128)(2,1)S(1)}, u32[]{:S(2)}, u32[]{:S(2)}) collective-permute-start(bf16[1,128,1536]{2,1,0:T(8,128)(2,1)S(1)} %fusion.1), channel_id=1, source_target_pairs={{8,0},{12,4},{16,8},{20,12},{24,16},{28,20},{0,24},{4,28},{9,1},{1... | collective-permute-start | bytes 1179656 | tf_op jit(solution)/shard_map/ppermute | solution.py:207
  195.7 4.3 %collective-permute-done.32 = bf16[1,128,1536]{2,1,0:T(8,128)(2,1)S(1)} collective-permute-done((bf16[1,128,1536]{2,1,0:T(8,128)(2,1)S(1)}, bf16[1,128,1536]{2,1,0:T(8,128)(2,1)S(1)}, u32[]{:S(2)}, u32[]{:S(2)}) %collective-permute-start.32) | collective-permute-done | bytes 393248 | tf_op jit(solution)/shard_map/ppermute | solution.py:207
  (140 shorter events, 27.4 us)
Async XLA Ops:
  1.8 18.9 %collective-permute-start.3 = (bf16[128,1024]{1,0:T(8,128)(2,1)S(1)}, bf16[128,1024]{1,0:T(8,128)(2,1)S(1)}, u32[]{:S(2)}, u32[]{:S(2)}) collective-permute-start(bf16[128,1024]{1,0:T(8,128)(2,1)S(1)} %get-tuple-element.66), channel_id=1, source_target_pairs={{0,1},{1,0},{2,3},{3,2},{4,5},{5,4},{6,7},{7,6},{8,9},{9,8},{10,11... | collective-permute-start | bytes 786440 | tf_op jit(solution)/shard_map/ppermute | solution.py:173
  4.8 17.7 %collective-permute-start.6 = (bf16[128,1024]{1,0:T(8,128)(2,1)S(1)}, bf16[128,1024]{1,0:T(8,128)(2,1)S(1)}, u32[]{:S(2)}, u32[]{:S(2)}) collective-permute-start(bf16[128,1024]{1,0:T(8,128)(2,1)S(1)} %get-tuple-element.65), channel_id=1, source_target_pairs={{0,2},{1,3},{2,0},{3,1},{4,6},{5,7},{6,4},{7,5},{8,10},{9,11},{10,... | collective-permute-start | bytes 786440 | tf_op jit(solution)/shard_map/ppermute | solution.py:173
  8.2 12.3 %collective-permute-start.15 = (bf16[128,512]{1,0:T(8,128)(2,1)}, bf16[128,512]{1,0:T(8,128)(2,1)S(1)}, u32[]{:S(2)}, u32[]{:S(2)}) collective-permute-start(bf16[128,512]{1,0:T(8,128)(2,1)} %get-tuple-element.62), channel_id=1, source_target_pairs={{0,1},{1,0},{2,3},{3,2},{4,5},{5,4},{6,7},{7,6},{8,9},{9,8},{10,11... | collective-permute-start | bytes 393224 | tf_op jit(solution)/shard_map/ppermute | solution.py:173
  10.2 3.8 %collective-permute-start = (f32[8,256]{1,0:T(8,128)S(1)}, f32[8,256]{1,0:T(8,128)S(1)}, u32[]{:S(2)}, u32[]{:S(2)}) collective-permute-start(f32[8,256]{1,0:T(8,128)S(1)} %concatenate.23), channel_id=1, source_target_pairs={{0,1},{1,0},{2,3},{3,2},{4,5},{5,4},{6,7},{7,6},{8,9},{9,8},{10,11... | collective-permute-start | bytes 24584 | tf_op jit(solution)/shard_map/ppermute | solution.py:184
  11.8 5.0 %collective-permute-start.1 = (f32[8,256]{1,0:T(8,128)S(1)}, f32[8,256]{1,0:T(8,128)S(1)}, u32[]{:S(2)}, u32[]{:S(2)}) collective-permute-start(f32[8,256]{1,0:T(8,128)S(1)} %concatenate.23), channel_id=1, source_target_pairs={{0,2},{1,3},{2,0},{3,1},{4,6},{5,7},{6,4},{7,5},{8,10},{9,11},{10,... | collective-permute-start | bytes 24584 | tf_op jit(solution)/shard_map/ppermute | solution.py:184
  14.1 4.6 %collective-permute-start.2 = (f32[8,256]{1,0:T(8,128)S(1)}, f32[8,256]{1,0:T(8,128)S(1)}, u32[]{:S(2)}, u32[]{:S(2)}) collective-permute-start(f32[8,256]{1,0:T(8,128)S(1)} %concatenate.23), channel_id=1, source_target_pairs={{0,3},{1,2},{2,1},{3,0},{4,7},{5,6},{6,5},{7,4},{8,11},{9,10},{10,... | collective-permute-start | bytes 24584 | tf_op jit(solution)/shard_map/ppermute | solution.py:184
  16.8 21.9 %collective-permute-start.4 = (bf16[128,1024]{1,0:T(8,128)(2,1)S(1)}, bf16[128,1024]{1,0:T(8,128)(2,1)S(1)}, u32[]{:S(2)}, u32[]{:S(2)}) collective-permute-start(bf16[128,1024]{1,0:T(8,128)(2,1)S(1)} %get-tuple-element.65), channel_id=1, source_target_pairs={{0,1},{1,0},{2,3},{3,2},{4,5},{5,4},{6,7},{7,6},{8,9},{9,8},{10,11... | collective-permute-start | bytes 786440 | tf_op jit(solution)/shard_map/ppermute | solution.py:174
  18.6 22.5 %collective-permute-start.5 = (bf16[128,1024]{1,0:T(8,128)(2,1)S(1)}, bf16[128,1024]{1,0:T(8,128)(2,1)S(1)}, u32[]{:S(2)}, u32[]{:S(2)}) collective-permute-start(bf16[128,1024]{1,0:T(8,128)(2,1)S(1)} %get-tuple-element.66), channel_id=1, source_target_pairs={{0,2},{1,3},{2,0},{3,1},{4,6},{5,7},{6,4},{7,5},{8,10},{9,11},{10,... | collective-permute-start | bytes 786440 | tf_op jit(solution)/shard_map/ppermute | solution.py:174
  20.4 10.1 %collective-permute-start.18 = (bf16[128,512]{1,0:T(8,128)(2,1)S(1)}, bf16[128,512]{1,0:T(8,128)(2,1)}, u32[]{:S(2)}, u32[]{:S(2)}) collective-permute-start(bf16[128,512]{1,0:T(8,128)(2,1)S(1)} %get-tuple-element.59), channel_id=1, source_target_pairs={{0,2},{1,3},{2,0},{3,1},{4,6},{5,7},{6,4},{7,5},{8,10},{9,11},{10,... | collective-permute-start | bytes 393224 | tf_op jit(solution)/shard_map/ppermute | solution.py:173
  20.7 23.9 %copy-start.11 = (bf16[128,1024]{1,0:T(8,128)(2,1)}, bf16[128,1024]{1,0:T(8,128)(2,1)S(1)}, u32[]{:S(2)}) copy-start(bf16[128,1024]{1,0:T(8,128)(2,1)S(1)} %collective-permute-done.3.refs_1_) | copy-start | bytes 786436
  20.7 21.2 %collective-permute-start.7 = (bf16[128,1024]{1,0:T(8,128)(2,1)S(1)}, bf16[128,1024]{1,0:T(8,128)(2,1)S(1)}, u32[]{:S(2)}, u32[]{:S(2)}) collective-permute-start(bf16[128,1024]{1,0:T(8,128)(2,1)S(1)} %collective-permute-done.3.refs_1_), channel_id=1, source_target_pairs={{0,2},{1,3},{2,0},{3,1},{4,6},{5,7},{6,4},{7,5},{8,10},{9,11},{10,... | collective-permute-start | bytes 786440 | tf_op jit(solution)/shard_map/ppermute | solution.py:175
  22.5 22.1 %collective-permute-start.8 = (bf16[128,1024]{1,0:T(8,128)(2,1)S(1)}, bf16[128,1024]{1,0:T(8,128)(2,1)S(1)}, u32[]{:S(2)}, u32[]{:S(2)}) collective-permute-start(bf16[128,1024]{1,0:T(8,128)(2,1)S(1)} %collective-permute-done.6.refs_4_), channel_id=1, source_target_pairs={{0,1},{1,0},{2,3},{3,2},{4,5},{5,4},{6,7},{7,6},{8,9},{9,8},{10,11... | collective-permute-start | bytes 786440 | tf_op jit(solution)/shard_map/ppermute | solution.py:175
  30.6 5.1 %collective-permute-start.16 = (bf16[128,512]{1,0:T(8,128)(2,1)S(1)}, bf16[128,512]{1,0:T(8,128)(2,1)S(1)}, u32[]{:S(2)}, u32[]{:S(2)}) collective-permute-start(bf16[128,512]{1,0:T(8,128)(2,1)S(1)} %get-tuple-element.59), channel_id=1, source_target_pairs={{0,1},{1,0},{2,3},{3,2},{4,5},{5,4},{6,7},{7,6},{8,9},{9,8},{10,11... | collective-permute-start | bytes 393224 | tf_op jit(solution)/shard_map/ppermute | solution.py:174
  36.3 24.0 %collective-permute-start.17 = (bf16[128,512]{1,0:T(8,128)(2,1)}, bf16[128,512]{1,0:T(8,128)(2,1)S(1)}, u32[]{:S(2)}, u32[]{:S(2)}) collective-permute-start(bf16[128,512]{1,0:T(8,128)(2,1)} %get-tuple-element.62), channel_id=1, source_target_pairs={{0,2},{1,3},{2,0},{3,1},{4,6},{5,7},{6,4},{7,5},{8,10},{9,11},{10,... | collective-permute-start | bytes 393224 | tf_op jit(solution)/shard_map/ppermute | solution.py:174
  39.3 22.7 %collective-permute-start.9 = (bf16[128,512]{1,0:T(8,128)(2,1)}, bf16[128,512]{1,0:T(8,128)(2,1)S(1)}, u32[]{:S(2)}, u32[]{:S(2)}) collective-permute-start(bf16[128,512]{1,0:T(8,128)(2,1)} %get-tuple-element.61), channel_id=1, source_target_pairs={{0,1},{1,0},{2,3},{3,2},{4,5},{5,4},{6,7},{7,6},{8,9},{9,8},{10,11... | collective-permute-start | bytes 393224 | tf_op jit(solution)/shard_map/ppermute | solution.py:173
  41.8 20.3 %collective-permute-start.12 = (bf16[128,512]{1,0:T(8,128)(2,1)}, bf16[128,512]{1,0:T(8,128)(2,1)S(1)}, u32[]{:S(2)}, u32[]{:S(2)}) collective-permute-start(bf16[128,512]{1,0:T(8,128)(2,1)} %get-tuple-element.60), channel_id=1, source_target_pairs={{0,2},{1,3},{2,0},{3,1},{4,6},{5,7},{6,4},{7,5},{8,10},{9,11},{10,... | collective-permute-start | bytes 393224 | tf_op jit(solution)/shard_map/ppermute | solution.py:173
  42.5 21.5 %collective-permute-start.19 = (bf16[128,512]{1,0:T(8,128)(2,1)S(1)}, bf16[128,512]{1,0:T(8,128)(2,1)S(1)}, u32[]{:S(2)}, u32[]{:S(2)}) collective-permute-start(bf16[128,512]{1,0:T(8,128)(2,1)S(1)} %collective-permute-done.15.refs_1_), channel_id=1, source_target_pairs={{0,2},{1,3},{2,0},{3,1},{4,6},{5,7},{6,4},{7,5},{8,10},{9,11},{10,... | collective-permute-start | bytes 393224 | tf_op jit(solution)/shard_map/ppermute | solution.py:175
  45.3 19.1 %collective-permute-start.20 = (bf16[128,512]{1,0:T(8,128)(2,1)}, bf16[128,512]{1,0:T(8,128)(2,1)S(1)}, u32[]{:S(2)}, u32[]{:S(2)}) collective-permute-start(bf16[128,512]{1,0:T(8,128)(2,1)} %collective-permute-done.18.refs_4_), channel_id=1, source_target_pairs={{0,1},{1,0},{2,3},{3,2},{4,5},{5,4},{6,7},{7,6},{8,9},{9,8},{10,11... | collective-permute-start | bytes 393224 | tf_op jit(solution)/shard_map/ppermute | solution.py:175
  60.3 11.5 %collective-permute-start.10 = (bf16[128,512]{1,0:T(8,128)(2,1)}, bf16[128,512]{1,0:T(8,128)(2,1)S(1)}, u32[]{:S(2)}, u32[]{:S(2)}) collective-permute-start(bf16[128,512]{1,0:T(8,128)(2,1)} %get-tuple-element.60), channel_id=1, source_target_pairs={{0,1},{1,0},{2,3},{3,2},{4,5},{5,4},{6,7},{7,6},{8,9},{9,8},{10,11... | collective-permute-start | bytes 393224 | tf_op jit(solution)/shard_map/ppermute | solution.py:174
  62.1 9.8 %collective-permute-start.11 = (bf16[128,512]{1,0:T(8,128)(2,1)}, bf16[128,512]{1,0:T(8,128)(2,1)S(1)}, u32[]{:S(2)}, u32[]{:S(2)}) collective-permute-start(bf16[128,512]{1,0:T(8,128)(2,1)} %get-tuple-element.61), channel_id=1, source_target_pairs={{0,2},{1,3},{2,0},{3,1},{4,6},{5,7},{6,4},{7,5},{8,10},{9,11},{10,... | collective-permute-start | bytes 393224 | tf_op jit(solution)/shard_map/ppermute | solution.py:174
  62.1 9.8 %collective-permute-start.13 = (bf16[128,512]{1,0:T(8,128)(2,1)S(1)}, bf16[128,512]{1,0:T(8,128)(2,1)S(1)}, u32[]{:S(2)}, u32[]{:S(2)}) collective-permute-start(bf16[128,512]{1,0:T(8,128)(2,1)S(1)} %collective-permute-done.9.refs_1_), channel_id=1, source_target_pairs={{0,2},{1,3},{2,0},{3,1},{4,6},{5,7},{6,4},{7,5},{8,10},{9,11},{10,... | collective-permute-start | bytes 393224 | tf_op jit(solution)/shard_map/ppermute | solution.py:175
  64.1 7.7 %collective-permute-start.14 = (bf16[128,512]{1,0:T(8,128)(2,1)S(1)}, bf16[128,512]{1,0:T(8,128)(2,1)S(1)}, u32[]{:S(2)}, u32[]{:S(2)}) collective-permute-start(bf16[128,512]{1,0:T(8,128)(2,1)S(1)} %collective-permute-done.12.refs_4_), channel_id=1, source_target_pairs={{0,1},{1,0},{2,3},{3,2},{4,5},{5,4},{6,7},{7,6},{8,9},{9,8},{10,11... | collective-permute-start | bytes 393224 | tf_op jit(solution)/shard_map/ppermute | solution.py:175
  94.2 9.2 %collective-permute-start.21 = (bf16[2,128,1024]{2,1,0:T(8,128)(2,1)S(1)}, bf16[2,128,1024]{2,1,0:T(8,128)(2,1)S(1)}, u32[]{:S(2)}, u32[]{:S(2)}) collective-permute-start(bf16[2,128,1024]{2,1,0:T(8,128)(2,1)S(1)} %get-tuple-element.33), channel_id=1, source_target_pairs={{0,2},{1,3},{2,0},{3,1},{4,6},{5,7},{6,4},{7,5},{8,10},{9,11},{10,... | collective-permute-start | bytes 1572872 | tf_op jit(solution)/shard_map/ppermute | solution.py:368
  94.4 16.3 %collective-permute-start.33 = (bf16[4,2,96,512]{3,2,1,0:T(8,128)(2,1)S(1)}, bf16[4,2,96,512]{3,2,1,0:T(8,128)(2,1)S(1)}, u32[]{:S(2)}, u32[]{:S(2)}) collective-permute-start(bf16[4,2,96,512]{3,2,1,0:T(8,128)(2,1)S(1)} %copy-done.10), channel_id=1, source_target_pairs={{0,4},{4,0},{8,12},{12,8},{16,20},{20,16},{24,28},{28,24},{1,5},{5... | collective-permute-start | bytes 2359304 | tf_op jit(solution)/shard_map/ppermute | solution.py:312
  94.4 18.2 %collective-permute-start.40 = (bf16[4,2,96,512]{3,2,1,0:T(8,128)(2,1)S(1)}, bf16[4,2,96,512]{3,2,1,0:T(8,128)(2,1)S(1)}, u32[]{:S(2)}, u32[]{:S(2)}) collective-permute-start(bf16[4,2,96,512]{3,2,1,0:T(8,128)(2,1)S(1)} %get-tuple-element.44), channel_id=1, source_target_pairs={{0,4},{4,0},{8,12},{12,8},{16,20},{20,16},{24,28},{28,24},{1,5},{5... | collective-permute-start | bytes 2359304 | tf_op jit(solution)/shard_map/ppermute | solution.py:312
  94.9 13.9 %collective-permute-start.23 = (bf16[2,128,1024]{2,1,0:T(8,128)(2,1)S(1)}, bf16[2,128,1024]{2,1,0:T(8,128)(2,1)S(1)}, u32[]{:S(2)}, u32[]{:S(2)}) collective-permute-start(bf16[2,128,1024]{2,1,0:T(8,128)(2,1)S(1)} %get-tuple-element.35), channel_id=1, source_target_pairs={{0,1},{1,0},{2,3},{3,2},{4,5},{5,4},{6,7},{7,6},{8,9},{9,8},{10,11... | collective-permute-start | bytes 1572872 | tf_op jit(solution)/shard_map/ppermute | solution.py:368
  100.3 38.7 %collective-permute-start.25 = (bf16[3,2,128,1536]{3,2,1,0:T(8,128)(2,1)S(1)}, bf16[3,2,128,1536]{3,2,1,0:T(8,128)(2,1)S(1)}, u32[]{:S(2)}, u32[]{:S(2)}) collective-permute-start(bf16[3,2,128,1536]{3,2,1,0:T(8,128)(2,1)S(1)} %get-tuple-element.38), channel_id=1, source_target_pairs={{0,4},{4,0},{8,12},{12,8},{16,20},{20,16},{24,28},{28,24},{1,5},{5... | collective-permute-start | bytes 7077896 | tf_op jit(solution)/shard_map/ppermute | solution.py:331
  103.5 16.7 %collective-permute-start.26 = (bf16[1,2,128,1536]{3,2,1,0:T(8,128)(2,1)S(1)}, bf16[1,2,128,1536]{3,2,1,0:T(8,128)(2,1)S(1)}, u32[]{:S(2)}, u32[]{:S(2)}) collective-permute-start(bf16[1,2,128,1536]{3,2,1,0:T(8,128)(2,1)S(1)} %get-tuple-element.40), channel_id=1, source_target_pairs={{0,4},{4,0},{8,12},{12,8},{16,20},{20,16},{24,28},{28,24},{1,5},{5... | collective-permute-start | bytes 2359304 | tf_op jit(solution)/shard_map/ppermute | solution.py:331
  108.8 7.5 %collective-permute-start.22 = (bf16[128,1024]{1,0:T(8,128)(2,1)S(1)}, bf16[128,1024]{1,0:T(8,128)(2,1)S(1)}, u32[]{:S(2)}, u32[]{:S(2)}) collective-permute-start(bf16[128,1024]{1,0:T(8,128)(2,1)S(1)} %fusion.8), channel_id=1, source_target_pairs={{0,1},{1,0},{2,3},{3,2},{4,5},{5,4},{6,7},{7,6},{8,9},{9,8},{10,11... | collective-permute-start | bytes 786440 | tf_op jit(solution)/shard_map/ppermute | solution.py:369
  110.7 9.4 %collective-permute-start.24 = (bf16[128,1024]{1,0:T(8,128)(2,1)S(1)}, bf16[128,1024]{1,0:T(8,128)(2,1)S(1)}, u32[]{:S(2)}, u32[]{:S(2)}) collective-permute-start(bf16[128,1024]{1,0:T(8,128)(2,1)S(1)} %fusion.9), channel_id=1, source_target_pairs={{0,2},{1,3},{2,0},{3,1},{4,6},{5,7},{6,4},{7,5},{8,10},{9,11},{10,... | collective-permute-start | bytes 786440 | tf_op jit(solution)/shard_map/ppermute | solution.py:370
  112.7 12.5 %collective-permute-start.34 = (bf16[1,96,512]{2,1,0:T(8,128)(2,1)S(1)}, bf16[1,96,512]{2,1,0:T(8,128)(2,1)S(1)}, u32[]{:S(2)}, u32[]{:S(2)}) collective-permute-start(bf16[1,96,512]{2,1,0:T(8,128)(2,1)S(1)} %get-tuple-element.51), channel_id=1, source_target_pairs={{0,8},{4,12},{8,16},{12,20},{16,24},{20,28},{24,0},{28,4},{1,9},{5... | collective-permute-start | bytes 294920 | tf_op jit(solution)/shard_map/ppermute | solution.py:207
  116.3 43.2 %collective-permute-start.37 = (bf16[1,96,512]{2,1,0:T(8,128)(2,1)S(1)}, bf16[1,96,512]{2,1,0:T(8,128)(2,1)S(1)}, u32[]{:S(2)}, u32[]{:S(2)}) collective-permute-start(bf16[1,96,512]{2,1,0:T(8,128)(2,1)S(1)} %get-tuple-element.52), channel_id=1, source_target_pairs={{8,0},{12,4},{16,8},{20,12},{24,16},{28,20},{0,24},{4,28},{9,1},{1... | collective-permute-start | bytes 294920 | tf_op jit(solution)/shard_map/ppermute | solution.py:207
  120.0 6.6 %collective-permute-start.41 = (bf16[1,96,512]{2,1,0:T(8,128)(2,1)S(1)}, bf16[1,96,512]{2,1,0:T(8,128)(2,1)S(1)}, u32[]{:S(2)}, u32[]{:S(2)}) collective-permute-start(bf16[1,96,512]{2,1,0:T(8,128)(2,1)S(1)} %get-tuple-element.55), channel_id=1, source_target_pairs={{0,8},{4,12},{8,16},{12,20},{16,24},{20,28},{24,0},{28,4},{1,9},{5... | collective-permute-start | bytes 294920 | tf_op jit(solution)/shard_map/ppermute | solution.py:207
  120.2 43.3 %collective-permute-start.44 = (bf16[1,96,512]{2,1,0:T(8,128)(2,1)S(1)}, bf16[1,96,512]{2,1,0:T(8,128)(2,1)S(1)}, u32[]{:S(2)}, u32[]{:S(2)}) collective-permute-start(bf16[1,96,512]{2,1,0:T(8,128)(2,1)S(1)} %get-tuple-element.56), channel_id=1, source_target_pairs={{8,0},{12,4},{16,8},{20,12},{24,16},{28,20},{0,24},{4,28},{9,1},{1... | collective-permute-start | bytes 294920 | tf_op jit(solution)/shard_map/ppermute | solution.py:207
  125.1 13.9 %collective-permute-start.27 = (bf16[1,128,1536]{2,1,0:T(8,128)(2,1)S(1)}, bf16[1,128,1536]{2,1,0:T(8,128)(2,1)S(1)}, u32[]{:S(2)}, u32[]{:S(2)}) collective-permute-start(bf16[1,128,1536]{2,1,0:T(8,128)(2,1)S(1)} %get-tuple-element.57), channel_id=1, source_target_pairs={{0,8},{4,12},{8,16},{12,20},{16,24},{20,28},{24,0},{28,4},{1,9},{5... | collective-permute-start | bytes 1179656 | tf_op jit(solution)/shard_map/ppermute | solution.py:207
  126.6 39.9 %collective-permute-start.30 = (bf16[1,128,1536]{2,1,0:T(8,128)(2,1)S(1)}, bf16[1,128,1536]{2,1,0:T(8,128)(2,1)S(1)}, u32[]{:S(2)}, u32[]{:S(2)}) collective-permute-start(bf16[1,128,1536]{2,1,0:T(8,128)(2,1)S(1)} %get-tuple-element.58), channel_id=1, source_target_pairs={{8,0},{12,4},{16,8},{20,12},{24,16},{28,20},{0,24},{4,28},{9,1},{1... | collective-permute-start | bytes 1179656 | tf_op jit(solution)/shard_map/ppermute | solution.py:207
  139.0 8.7 %collective-permute-start.35 = (bf16[1,96,512]{2,1,0:T(8,128)(2,1)S(1)}, bf16[1,96,512]{2,1,0:T(8,128)(2,1)S(1)}, u32[]{:S(2)}, u32[]{:S(2)}) collective-permute-start(bf16[1,96,512]{2,1,0:T(8,128)(2,1)S(1)} %fusion.16), channel_id=1, source_target_pairs={{0,8},{4,12},{8,16},{12,20},{16,24},{20,28},{24,0},{28,4},{1,9},{5... | collective-permute-start | bytes 294920 | tf_op jit(solution)/shard_map/ppermute | solution.py:207
  139.0 9.7 %collective-permute-start.42 = (bf16[1,96,512]{2,1,0:T(8,128)(2,1)S(1)}, bf16[1,96,512]{2,1,0:T(8,128)(2,1)S(1)}, u32[]{:S(2)}, u32[]{:S(2)}) collective-permute-start(bf16[1,96,512]{2,1,0:T(8,128)(2,1)S(1)} %fusion.12), channel_id=1, source_target_pairs={{0,8},{4,12},{8,16},{12,20},{16,24},{20,28},{24,0},{28,4},{1,9},{5... | collective-permute-start | bytes 294920 | tf_op jit(solution)/shard_map/ppermute | solution.py:207
  147.6 11.2 %collective-permute-start.28 = (bf16[1,128,1536]{2,1,0:T(8,128)(2,1)S(1)}, bf16[1,128,1536]{2,1,0:T(8,128)(2,1)S(1)}, u32[]{:S(2)}, u32[]{:S(2)}) collective-permute-start(bf16[1,128,1536]{2,1,0:T(8,128)(2,1)S(1)} %fusion.2), channel_id=1, source_target_pairs={{0,8},{4,12},{8,16},{12,20},{16,24},{20,28},{24,0},{28,4},{1,9},{5... | collective-permute-start | bytes 1179656 | tf_op jit(solution)/shard_map/ppermute | solution.py:207
  148.7 11.7 %collective-permute-start.36 = (bf16[1,96,512]{2,1,0:T(8,128)(2,1)S(1)}, bf16[1,96,512]{2,1,0:T(8,128)(2,1)S(1)}, u32[]{:S(2)}, u32[]{:S(2)}) collective-permute-start(bf16[1,96,512]{2,1,0:T(8,128)(2,1)S(1)} %fusion.17), channel_id=1, source_target_pairs={{0,8},{4,12},{8,16},{12,20},{16,24},{20,28},{24,0},{28,4},{1,9},{5... | collective-permute-start | bytes 294920 | tf_op jit(solution)/shard_map/ppermute | solution.py:207
  158.8 7.5 %collective-permute-start.43 = (bf16[1,96,512]{2,1,0:T(8,128)(2,1)S(1)}, bf16[1,96,512]{2,1,0:T(8,128)(2,1)S(1)}, u32[]{:S(2)}, u32[]{:S(2)}) collective-permute-start(bf16[1,96,512]{2,1,0:T(8,128)(2,1)S(1)} %fusion.13), channel_id=1, source_target_pairs={{0,8},{4,12},{8,16},{12,20},{16,24},{20,28},{24,0},{28,4},{1,9},{5... | collective-permute-start | bytes 294920 | tf_op jit(solution)/shard_map/ppermute | solution.py:207
  159.6 13.1 %collective-permute-start.29 = (bf16[1,128,1536]{2,1,0:T(8,128)(2,1)S(1)}, bf16[1,128,1536]{2,1,0:T(8,128)(2,1)S(1)}, u32[]{:S(2)}, u32[]{:S(2)}) collective-permute-start(bf16[1,128,1536]{2,1,0:T(8,128)(2,1)S(1)} %fusion.3), channel_id=1, source_target_pairs={{0,8},{4,12},{8,16},{12,20},{16,24},{20,28},{24,0},{28,4},{1,9},{5... | collective-permute-start | bytes 1179656 | tf_op jit(solution)/shard_map/ppermute | solution.py:207
  160.5 22.5 %collective-permute-start.38 = (bf16[1,96,512]{2,1,0:T(8,128)(2,1)S(1)}, bf16[1,96,512]{2,1,0:T(8,128)(2,1)S(1)}, u32[]{:S(2)}, u32[]{:S(2)}) collective-permute-start(bf16[1,96,512]{2,1,0:T(8,128)(2,1)S(1)} %get-tuple-element.50), channel_id=1, source_target_pairs={{8,0},{12,4},{16,8},{20,12},{24,16},{28,20},{0,24},{4,28},{9,1},{1... | collective-permute-start | bytes 294920 | tf_op jit(solution)/shard_map/ppermute | solution.py:207
  166.4 17.0 %collective-permute-start.45 = (bf16[1,96,512]{2,1,0:T(8,128)(2,1)S(1)}, bf16[1,96,512]{2,1,0:T(8,128)(2,1)S(1)}, u32[]{:S(2)}, u32[]{:S(2)}) collective-permute-start(bf16[1,96,512]{2,1,0:T(8,128)(2,1)S(1)} %get-tuple-element.54), channel_id=1, source_target_pairs={{8,0},{12,4},{16,8},{20,12},{24,16},{28,20},{0,24},{4,28},{9,1},{1... | collective-permute-start | bytes 294920 | tf_op jit(solution)/shard_map/ppermute | solution.py:207
  172.9 17.2 %collective-permute-start.31 = (bf16[1,128,1536]{2,1,0:T(8,128)(2,1)S(1)}, bf16[1,128,1536]{2,1,0:T(8,128)(2,1)S(1)}, u32[]{:S(2)}, u32[]{:S(2)}) collective-permute-start(bf16[1,128,1536]{2,1,0:T(8,128)(2,1)S(1)} %get-tuple-element.48), channel_id=1, source_target_pairs={{8,0},{12,4},{16,8},{20,12},{24,16},{28,20},{0,24},{4,28},{9,1},{1... | collective-permute-start | bytes 1179656 | tf_op jit(solution)/shard_map/ppermute | solution.py:207
  183.0 11.6 %collective-permute-start.39 = (bf16[1,96,512]{2,1,0:T(8,128)(2,1)S(1)}, bf16[1,96,512]{2,1,0:T(8,128)(2,1)S(1)}, u32[]{:S(2)}, u32[]{:S(2)}) collective-permute-start(bf16[1,96,512]{2,1,0:T(8,128)(2,1)S(1)} %fusion.15), channel_id=1, source_target_pairs={{8,0},{12,4},{16,8},{20,12},{24,16},{28,20},{0,24},{4,28},{9,1},{1... | collective-permute-start | bytes 294920 | tf_op jit(solution)/shard_map/ppermute | solution.py:207
  183.5 11.2 %collective-permute-start.46 = (bf16[1,96,512]{2,1,0:T(8,128)(2,1)S(1)}, bf16[1,96,512]{2,1,0:T(8,128)(2,1)S(1)}, u32[]{:S(2)}, u32[]{:S(2)}) collective-permute-start(bf16[1,96,512]{2,1,0:T(8,128)(2,1)S(1)} %fusion.11), channel_id=1, source_target_pairs={{8,0},{12,4},{16,8},{20,12},{24,16},{28,20},{0,24},{4,28},{9,1},{1... | collective-permute-start | bytes 294920 | tf_op jit(solution)/shard_map/ppermute | solution.py:207
  190.3 9.6 %collective-permute-start.32 = (bf16[1,128,1536]{2,1,0:T(8,128)(2,1)S(1)}, bf16[1,128,1536]{2,1,0:T(8,128)(2,1)S(1)}, u32[]{:S(2)}, u32[]{:S(2)}) collective-permute-start(bf16[1,128,1536]{2,1,0:T(8,128)(2,1)S(1)} %fusion.1), channel_id=1, source_target_pairs={{8,0},{12,4},{16,8},{20,12},{24,16},{28,20},{0,24},{4,28},{9,1},{1... | collective-permute-start | bytes 1179656 | tf_op jit(solution)/shard_map/ppermute | solution.py:207
  (25 other events, 151.9 us)

commit v2 on v0

v2 whole, which is shorter than its diff:
```python
import functools

import jax
import jax.numpy as jnp
from jax import lax
from jax.experimental import pallas as pl
from jax.experimental.pallas import tpu as pltpu
from jax.sharding import PartitionSpec as P

TOP = 2
BF = jnp.bfloat16
F32 = jnp.float32
IN_PARTS = 1


def dot(a, b):
    return jnp.dot(a, b, preferred_element_type=F32)


def dot_nt(a, b):
    return lax.dot_general(a, b, (((1,), (1,)), ((), ())), preferred_element_type=F32)


def bf(*shape):
    return jax.ShapeDtypeStruct(shape, BF)


def whole(array):
    return pl.BlockSpec(array.shape, lambda step, scal: (0,) * len(array.shape))


def of_expert(weights, columns=None, index=0):
    shape = (1, weights.shape[1], columns or weights.shape[2])
    return pl.BlockSpec(shape, lambda step, scal: (scal[0], 0, index))


def call(body, out_shape, flops, limit, scal, *args, specs=None):
    return pl.pallas_call(
        body,
        out_shape=out_shape,
        grid_spec=pltpu.PrefetchScalarGridSpec(
            num_scalar_prefetch=1,
            grid=(1,),
            in_specs=specs or [whole(x) for x in args],
            out_specs=[whole(x) for x in out_shape],
        ),
        compiler_params=pltpu.CompilerParams(vmem_limit_bytes=limit << 20),
        cost_estimate=pl.CostEstimate(flops=flops, bytes_accessed=flops // 1000, transcendentals=0),
    )(scal, *args)


def stack_rows(refs, index):
    return jnp.concatenate([ref[index] for ref in refs], axis=0)


def after(value, *others):
    return lax.optimization_barrier((value, *others))[0]


ROUTE_ROWS = 16


def route_rows(route_logits, expert_ids, slot_pos, width):
    share = jax.nn.sigmoid(route_logits[:, 0] - route_logits[:, 1])
    high = lax.reduce_precision(share, 8, 7)
    middle = lax.reduce_precision(share - high, 8, 7)
    low = share - high - middle
    places = jnp.concatenate(
        [x.astype(BF) for x in (expert_ids[:, 0], expert_ids[:, 1], slot_pos[:, 0], slot_pos[:, 1])]
    )
    shares = jnp.concatenate([x.astype(BF) for x in (high, middle, low)])
    rows = [jnp.pad(x, (0, width - x.shape[0])) for x in (places, shares)]
    return jnp.pad(jnp.stack(rows), ((0, ROUTE_ROWS - 2), (0, 0)))


def slots_body(cap, n, scal, block, *refs):
    outs, back = refs[:-1], refs[-1]
    tokens = back.shape[0]
    route = block[0:2, :].astype(F32)
    row = lambda r, k: route[r : r + 1, k * tokens : (k + 1) * tokens]
    slot = lax.broadcasted_iota(jnp.int32, (cap, tokens), 0)
    slot = jnp.concatenate([slot + scal[2 + j] for j in range(n)], axis=0).astype(F32)
    first = slot == row(0, 0) * cap + row(0, 2)
    second = slot == row(0, 1) * cap + row(0, 3)
    share = row(1, 0) + row(1, 1) + row(1, 2)
    hit = jnp.where(jnp.logical_or(first, second), 1.0, 0.0)
    factor = jnp.where(first, share, 0.0) + jnp.where(second, 1.0 - share, 0.0)
    factor = jnp.sum(factor, axis=1, keepdims=True)
    back[...] = jnp.transpose(hit).astype(BF)
    hit = hit.astype(BF)
    rows = dot(hit, block[pl.ds(ROUTE_ROWS, tokens), :]).astype(BF)
    scaled = (dot(hit, block[pl.ds(ROUTE_ROWS + tokens, tokens), :]) * factor).astype(BF)
    for j, out in enumerate(outs):
        out[0] = rows[j * cap : (j + 1) * cap]
        out[1] = scaled[j * cap : (j + 1) * cap]


def forward_body(tile, scal, *refs):
    *arrived, w_in, rows_t, hidden_t, scale_gate, scale_up = refs
    ff = w_in.shape[2] // 2
    rows = stack_rows(arrived, 0)
    rows_t[...] = jnp.transpose(rows)
    for f in range(0, ff, tile):
        gate = dot(rows, w_in[0, :, pl.ds(f, tile)])
        upper = dot(rows, w_in[0, :, pl.ds(ff + f, tile)])
        sg = jax.nn.sigmoid(gate)
        activated = gate * sg
        hidden_t[pl.ds(f, tile), :] = jnp.transpose((activated * upper).astype(BF))
        scale_gate[:, pl.ds(f, tile)] = (upper * sg * (1.0 + gate * (1.0 - sg))).astype(BF)
        scale_up[:, pl.ds(f, tile)] = activated.astype(BF)


def shard_rows(sources, scal, shards, part):
    taken = []
    for offset in (1 - scal[1], scal[1]):
        for shard in shards:
            start = pl.multiple_of((2 * shard + offset) * part, 16)
            taken.append(jnp.concatenate([x[pl.ds(start, part), :] for x in sources], axis=1))
    return jnp.concatenate(taken, axis=0)


def down_body(n, nz, scal, *refs):
    arrived, (w_down, hidden_a, hidden_b, *scales), outs = refs[: 2 * n], refs[2 * n : 2 * n + 7], refs[2 * n + 7 :]
    give, keep, *pairs = outs
    part = give.shape[1]
    slots = [stack_rows(arrived[:n], 1), stack_rows(arrived[n:], 1)]
    shards = [scal[scal.shape[0] - nz + k] for k in range(nz)]
    left = shard_rows((hidden_a, hidden_b), scal, shards, part)
    result = dot(left, jnp.concatenate(slots, axis=0)).astype(BF)
    for k in range(nz):
        give[k] = result[k * part : (k + 1) * part]
        keep[k] = result[(nz + k) * part : (nz + k + 1) * part]
    for g in range(2):
        grad_hidden = dot_nt(slots[g], w_down[0])
        scale_gate, scale_up = scales[2 * g : 2 * g + 2]
        ff = scale_gate.shape[1]
        pairs[g][:, pl.ds(0, ff)] = (grad_hidden * scale_gate[...].astype(F32)).astype(BF)
        pairs[g][:, pl.ds(ff, ff)] = (grad_hidden * scale_up[...].astype(F32)).astype(BF)


def input_weight_body(first, nz, scal, rows_a, rows_b, pair_a, pair_b, give, keep):
    part, columns = give.shape[1:]
    pair = jnp.concatenate(
        [pair_a[:, pl.ds(first, columns)], pair_b[:, pl.ds(first, columns)]], axis=0
    )
    result = dot(shard_rows((rows_a, rows_b), scal, range(nz), part), pair).astype(BF)
    for k in range(nz):
        give[k] = result[k * part : (k + 1) * part]
        keep[k] = result[(nz + k) * part : (nz + k + 1) * part]


def returned_body(cap, scal, pair_a, pair_b, w_in, *outs):
    for g, pair in enumerate((pair_a, pair_b)):
        returned = dot_nt(pair[...], w_in[0]).astype(BF)
        for j, out in enumerate(outs):
            out[pl.ds(g * cap, cap), :] = returned[j * cap : (j + 1) * cap]


def combine_body(cap, scal, back_a, back_b, *refs):
    arrived, outs = refs[:-2], refs[-2:]
    for g, (back, out) in enumerate(zip((back_a, back_b), outs)):
        rows = jnp.concatenate([x[pl.ds(g * cap, cap), :] for x in arrived], axis=0)
        out[...] = dot(back[...], rows).astype(BF)


def per_device(tokens, cotangent, route_logits, expert_ids, slot_pos, w_in, w_down):
    token_count, width = tokens.shape
    experts, ff = w_down.shape[:2]
    n = lax.axis_size("expert")
    ndp = lax.axis_size("dp")
    nz = ndp // 2
    cap = 2 * TOP * token_count // (experts * n)
    slots = n * cap
    column, place = lax.axis_index("expert"), lax.axis_index("dp")
    z, core = place // 2, place % 2
    expert_of = lambda k: (k ^ (k >> 1)) & 1
    mine = expert_of(z)
    scal = [mine, core]
    scal += [((column ^ j) * experts + mine) * cap for j in range(n)]
    scal += [z ^ k for k in range(nz)]
    scal = jnp.stack(scal).astype(jnp.int32)
    swap_core = lambda x: lax.ppermute(x, "dp", [(i, i ^ 1) for i in range(ndp)])
    along_z = lambda x, k: lax.ppermute(x, "dp", [(i, i ^ (2 * k)) for i in range(ndp)]) if k else x
    across = lambda x, j: lax.ppermute(x, "expert", [(i, i ^ j) for i in range(n)]) if j else x
    macs = 2 * slots * width * ff

    block = jnp.concatenate(
        [route_rows(route_logits, expert_ids, slot_pos, width), tokens, cotangent], axis=0
    )
    arrived, backs = [], []
    for block in (block, along_z(block, 1)):
        *sent, back = call(
            functools.partial(slots_body, cap, n),
            [bf(2, cap, width)] * n + [bf(token_count, slots)],
            macs // 4,
            LIMITS[0],
            scal,
            block,
        )
        arrived += [across(x, j) for j, x in enumerate(sent)]
        backs.append(back)

    forwards = []
    for g in range(2):
        pieces = arrived[g * n : (g + 1) * n]
        forwards.append(
            call(
                functools.partial(forward_body, 256),
                [bf(width, slots), bf(ff, slots), bf(slots, ff), bf(slots, ff)],
                2 * macs,
                LIMITS[1],
                scal,
                *pieces,
                w_in,
                specs=[whole(x) for x in pieces] + [of_expert(w_in)],
            )
        )
    (rows_a, hidden_a, *scales_a), (rows_b, hidden_b, *scales_b) = forwards

    args = arrived + [w_down, hidden_a, hidden_b] + scales_a + scales_b
    specs = [whole(x) for x in args]
    specs[2 * n] = of_expert(w_down)
    *down, pair_a, pair_b = call(
        functools.partial(down_body, n, nz),
        [bf(nz, ff // ndp, width)] * 2 + [bf(slots, 2 * ff)] * 2,
        4 * macs,
        LIMITS[2],
        scal,
        *args,
        specs=specs,
    )
    pairs = (pair_a, pair_b)

    columns = 2 * ff // IN_PARTS
    ins = [
        call(
            functools.partial(input_weight_body, k * columns, nz),
            [bf(nz, width // ndp, columns)] * 2,
            4 * macs // IN_PARTS,
            LIMITS[3],
            scal,
            rows_a,
            rows_b,
            *pairs,
        )
        for k in range(IN_PARTS)
    ]

    def core_sum(give, keep):
        other = swap_core(give)
        return [(keep[k].astype(F32) + other[k].astype(F32)).astype(BF) for k in range(nz)]

    def gather_z(terms):
        return [along_z(x, k) for k, x in enumerate(terms)]

    def over_z(terms):
        same, different = (
            sum(terms[k].astype(F32) for k in range(nz) if expert_of(k) == e) for e in range(2)
        )
        return jnp.where(mine == 0, jnp.stack([same, different]), jnp.stack([different, same]))

    down_terms = gather_z(core_sum(*down))
    grad_down = over_z(down_terms)
    (give, keep) = ins[0]
    total = (keep.astype(F32) + swap_core(give).astype(F32)).astype(BF)
    terms = lax.all_to_all(
        total, "dp", 0, 0, tiled=True, axis_index_groups=[list(range(c, ndp, 2)) for c in range(2)]
    )
    grad_in = jnp.stack(
        [sum(terms[k].astype(F32) for k in range(nz) if expert_of(k) == e) for e in range(experts)]
    )
    sent = call(
        functools.partial(returned_body, cap),
        [bf(2 * cap, width)] * n,
        4 * macs,
        LIMITS[4],
        scal,
        after(pairs[0], total),
        pairs[1],
        w_in,
        specs=[whole(x) for x in pairs] + [of_expert(w_in)],
    )
    mine_sum, beside_sum = call(
        functools.partial(combine_body, cap),
        [bf(token_count, width)] * 2,
        macs // 4,
        LIMITS[5],
        scal,
        *backs,
        *[across(x, j) for j, x in enumerate(sent)],
    )
    input_grad = (mine_sum.astype(F32) + along_z(beside_sum, 1).astype(F32)).astype(BF)
    return (input_grad, grad_in, grad_down)


LIMITS = (24, 28, 28, 24, 24, 16)


def solution(mesh):
    in_specs = (
        P(("dp", "expert"), None),
        P(("dp", "expert"), None),
        P(("dp", "expert"), None),
        P(("dp", "expert"), None),
        P(("dp", "expert"), None),
        P("expert", None, None),
        P("expert", None, None),
    )
    out_specs = (P(("dp", "expert"), None), P("expert", "dp", None), P("expert", "dp", None))
    return jax.shard_map(
        per_device, mesh=mesh, in_specs=in_specs, out_specs=out_specs, check_vma=False
    )
```

time: 215 us -> 145 us (0.67)
  local copies, waits for them, and re-layouts: 41.2 us -> 8 us
  waiting for transfers between devices: 100 us -> 71 us
  matrix products: 28.4 us -> 0 us
  Pallas kernels: 0 us -> 23.2 us
  starting transfers between devices: 14.6 us -> 28.9 us
  between operations: 14.2 us -> 0.86 us
    ppermute x0 -> x16, waiting for transfers between devices: none -> 71 us  [the longest x5 37.8 us: per_device(): lax.ppermute(x, 'dp', [(i, i ^ 2 * k) for i in range(ndp)])]
    all_to_all x3 -> x1, waiting for transfers between devices: 59.1 us -> 0.01 us  [per_device(): lax.all_to_all(total, 'dp', 0, 0, tiled=True, axis_index_groups=[list(ran...]
    reduce_scatter x2 -> x0, waiting for transfers between devices: 41.3 us -> none  [the longest x1 41.3 us: per_device(): lax.psum_scatter(term_in.astype(jnp.bfloat16), 'dp', scatter_dimension=1,...]
    dot_general x5 -> x0, matrix products: 28.4 us -> none  [the longest x1 7.3 us: per_device(): jnp.einsum('ksf,kdf->ksd', grad_pair, w_in, preferred_element_type=jnp.fl...]
    ppermute x0 -> x16, starting transfers between devices: none -> 24.1 us  [the longest x5 13.4 us: per_device(): lax.ppermute(x, 'dp', [(i, i ^ 2 * k) for i in range(ndp)])]
    pallas_call x0 -> x8, Pallas kernels: none -> 23.2 us  [call(): pl.pallas_call(body, out_shape=out_shape, grid_spec=pltpu.PrefetchScalarG...]
    all_to_all x3 -> x1, starting transfers between devices: 14.3 us -> 4.88 us  [per_device(): lax.all_to_all(total, 'dp', 0, 0, tiled=True, axis_index_groups=[list(ran...]
    all_to_all x3 -> x0, local copies, waits for them, and re-layouts: 8.69 us -> none  [the longest x1 3.65 us: per_device(): lax.all_to_all(returned, 'expert', split_axis=1, concat_axis=0, tiled=True)]
  transfers between devices with their start and end apart: 5 -> 17, of which waited for: 4 -> 9; matrix products, arithmetic and copies ran while one was open for 26% -> 3% of each run, Pallas kernels for 0% -> 9%
where the time goes in v2:
time: 145 us
  waiting for transfers between devices  71 us (49%)
  starting transfers between devices  28.9 us (20%)
  Pallas kernels  23.2 us (16%)
  other arithmetic  13 us (9%)
  local copies, waits for them, and re-layouts  8 us (6%)
    ppermute x5, waiting for transfers between devices, per_device(): lax.ppermute(x, 'dp', [(i, i ^ 2 * k) for i in range(ndp)])  37.8 us
    ppermute x9, waiting for transfers between devices, per_device(): lax.ppermute(x, 'expert', [(i, i ^ j) for i in range(n)])  29.8 us
    pallas_call x8, Pallas kernels, call(): pl.pallas_call(body, out_shape=out_shape, grid_spec=pltpu.PrefetchScalarG...  23.2 us
    ppermute x5, starting transfers between devices, per_device(): lax.ppermute(x, 'dp', [(i, i ^ 2 * k) for i in range(ndp)])  13.4 us
    ppermute x9, starting transfers between devices, per_device(): lax.ppermute(x, 'expert', [(i, i ^ j) for i in range(n)])  10.6 us
    unnamed x18, local copies, waits for them, and re-layouts  7.88 us
    all_to_all x1, starting transfers between devices, per_device(): lax.all_to_all(total, 'dp', 0, 0, tiled=True, axis_index_groups=[list(ran...  4.88 us
    ppermute x2, waiting for transfers between devices, per_device(): lax.ppermute(x, 'dp', [(i, i ^ 1) for i in range(ndp)])  3.4 us
  transfers between devices with their start and end apart: 17, of which 9 were waited for; matrix products, arithmetic and copies ran while one was open for 3% of the time, Pallas kernels for 9%

profile of v2, /device:TPU:0, one launch (start us, length us, event | category | flops | bytes accessed | tf_op | source)
XLA Modules:
  0.0 145.0 jit_solution(9960710539885084160)
XLA Ops:
  0.6 0.8 add_divide_fusion
  1.4 0.7 convert.9
  2.1 0.7 convert.10
  2.9 1.4 pad_maximum_fusion.1.block
  4.3 3.1 %collective-permute-start = (bf16[528,1024]{1,0:T(8,128)(2,1)S(1)}, bf16[528,1024]{1,0:T(8,128)(2,1)}, u32[]{:S(2)}, u32[]{:S(2)}) collective-permute-start(bf16[528,1024]{1,0:T(8,128)(2,1)S(1)} %pad_maximum_fusion.1.block), channel_id=1, source_target_pairs={{0,8},{4,12},{8,0},{12,4},{16,24},{20,28},{24,16},{28,20},{1,9},{5... | collective-permute-start | bytes 3244040 | tf_op jit(solution)/shard_map/ppermute | solution.py:183
  7.5 1.3 shard_map.94
  8.8 1.6 %collective-permute-start.1 = (bf16[2,128,1024]{2,1,0:T(8,128)(2,1)S(1)}, bf16[2,128,1024]{2,1,0:T(8,128)(2,1)S(1)}, u32[]{:S(2)}, u32[]{:S(2)}) collective-permute-start(bf16[2,128,1024]{2,1,0:T(8,128)(2,1)S(1)} %get-tuple-element.37), channel_id=1, source_target_pairs={{0,1},{1,0},{2,3},{3,2},{4,5},{5,4},{6,7},{7,6},{8,9},{9,8},{10,11... | collective-permute-start | bytes 1572872 | tf_op jit(solution)/shard_map/ppermute | solution.py:184
  10.4 1.5 %collective-permute-start.2 = (bf16[2,128,1024]{2,1,0:T(8,128)(2,1)S(1)}, bf16[2,128,1024]{2,1,0:T(8,128)(2,1)S(1)}, u32[]{:S(2)}, u32[]{:S(2)}) collective-permute-start(bf16[2,128,1024]{2,1,0:T(8,128)(2,1)S(1)} %get-tuple-element.38), channel_id=1, source_target_pairs={{0,2},{1,3},{2,0},{3,1},{4,6},{5,7},{6,4},{7,5},{8,10},{9,11},{10,... | collective-permute-start | bytes 1572872 | tf_op jit(solution)/shard_map/ppermute | solution.py:184
  11.9 0.5 collective-permute-start.3
  12.4 19.0 %collective-permute-done.block = bf16[528,1024]{1,0:T(8,128)(2,1)} collective-permute-done((bf16[528,1024]{1,0:T(8,128)(2,1)S(1)}, bf16[528,1024]{1,0:T(8,128)(2,1)}, u32[]{:S(2)}, u32[]{:S(2)}) %collective-permute-start) | collective-permute-done | bytes 1081376 | tf_op jit(solution)/shard_map/ppermute | solution.py:183
  31.4 2.5 %shard_map.95 = (bf16[2,128,1024]{2,1,0:T(8,128)(2,1)S(1)}, bf16[2,128,1024]{2,1,0:T(8,128)(2,1)S(1)}, bf16[2,128,1024]{2,1,0:T(8,128)(2,1)S(1)}, bf16[2,128,1024]{2,1,0:T(8,128)(2,1)S(1)}, bf16[256,512]{1,0:T(8,128)(2,1)S(1)}) custom-call(s32[10]{0:T(128)S(1)} %stack.71.scal, bf16[528,1024]{1,0:T(8,128)(2,1)} %collective-permute-done.block), custom_call_target="tpu_custom_call" | custom-call | flops 201326592 | bytes 201326 | tf_op jit(solution)/shard_map/pallas_call | solution.py:38
  33.9 1.7 %collective-permute-start.4 = (bf16[2,128,1024]{2,1,0:T(8,128)(2,1)S(1)}, bf16[2,128,1024]{2,1,0:T(8,128)(2,1)S(1)}, u32[]{:S(2)}, u32[]{:S(2)}) collective-permute-start(bf16[2,128,1024]{2,1,0:T(8,128)(2,1)S(1)} %get-tuple-element.41), channel_id=1, source_target_pairs={{0,1},{1,0},{2,3},{3,2},{4,5},{5,4},{6,7},{7,6},{8,9},{9,8},{10,11... | collective-permute-start | bytes 1572872 | tf_op jit(solution)/shard_map/ppermute | solution.py:184
  35.6 1.5 %collective-permute-start.5 = (bf16[2,128,1024]{2,1,0:T(8,128)(2,1)S(1)}, bf16[2,128,1024]{2,1,0:T(8,128)(2,1)S(1)}, u32[]{:S(2)}, u32[]{:S(2)}) collective-permute-start(bf16[2,128,1024]{2,1,0:T(8,128)(2,1)S(1)} %get-tuple-element.42), channel_id=1, source_target_pairs={{0,2},{1,3},{2,0},{3,1},{4,6},{5,7},{6,4},{7,5},{8,10},{9,11},{10,... | collective-permute-start | bytes 1572872 | tf_op jit(solution)/shard_map/ppermute | solution.py:184
  37.2 0.3 collective-permute-start.6
  37.5 2.8 %copy-done = bf16[2,1024,1536]{2,1,0:T(8,128)(2,1)S(1)} copy-done((bf16[2,1024,1536]{2,1,0:T(8,128)(2,1)S(1)}, bf16[2,1024,1536]{2,1,0:T(8,128)(2,1)}, u32[]{:S(2)}) %copy-start) | copy-done | bytes 6291480
  40.3 2.5 %shard_map.96 = (bf16[1024,512]{1,0:T(8,128)(2,1)S(1)}, bf16[768,512]{1,0:T(8,128)(2,1)S(1)}, bf16[512,768]{1,0:T(8,128)(2,1)S(1)}, bf16[512,768]{1,0:T(8,128)(2,1)S(1)}) custom-call(s32[10]{0:T(128)S(1)} %stack.71.scal, bf16[2,128,1024]{2,1,0:T(8,128)(2,1)S(1)} %get-tuple-element.36.refs_0_, bf16[2,128,1024]{2,1,0:T(8,128)(2,1)S(1)} %collective-permute-done.1.refs_1_, ...), custom_call_target="tpu_custom_call" | custom-call | flops 1610612736 | bytes 1610612 | tf_op jit(solution)/shard_map/pallas_call | solution.py:38
  42.8 6.0 %collective-permute-done.4.refs_1_.refs_5_ = bf16[2,128,1024]{2,1,0:T(8,128)(2,1)S(1)} collective-permute-done((bf16[2,128,1024]{2,1,0:T(8,128)(2,1)S(1)}, bf16[2,128,1024]{2,1,0:T(8,128)(2,1)S(1)}, u32[]{:S(2)}, u32[]{:S(2)}) %collective-permute-start.4) | collective-permute-done | bytes 524320 | tf_op jit(solution)/shard_map/ppermute | solution.py:184
  48.8 10.5 %collective-permute-done.5.refs_2_.refs_6_ = bf16[2,128,1024]{2,1,0:T(8,128)(2,1)S(1)} collective-permute-done((bf16[2,128,1024]{2,1,0:T(8,128)(2,1)S(1)}, bf16[2,128,1024]{2,1,0:T(8,128)(2,1)S(1)}, u32[]{:S(2)}, u32[]{:S(2)}) %collective-permute-start.5) | collective-permute-done | bytes 524320 | tf_op jit(solution)/shard_map/ppermute | solution.py:184
  59.4 2.5 %shard_map.97 = (bf16[1024,512]{1,0:T(8,128)(2,1)S(1)}, bf16[768,512]{1,0:T(8,128)(2,1)S(1)}, bf16[512,768]{1,0:T(8,128)(2,1)S(1)}, bf16[512,768]{1,0:T(8,128)(2,1)S(1)}) custom-call(s32[10]{0:T(128)S(1)} %stack.71.scal, bf16[2,128,1024]{2,1,0:T(8,128)(2,1)S(1)} %get-tuple-element.40.refs_0_.refs_4_, ...), custom_call_target="tpu_custom_call" | custom-call | flops 1610612736 | bytes 1610612 | tf_op jit(solution)/shard_map/pallas_call | solution.py:38
  61.9 4.1 %shard_map.98 = (bf16[4,96,1024]{2,1,0:T(8,128)(2,1)S(1)}, bf16[4,96,1024]{2,1,0:T(8,128)(2,1)S(1)}, bf16[512,1536]{1,0:T(8,128)(2,1)S(1)}, bf16[512,1536]{1,0:T(8,128)(2,1)S(1)}) custom-call(s32[10]{0:T(128)S(1)} %stack.71.scal, bf16[2,128,1024]{2,1,0:T(8,128)(2,1)S(1)} %get-tuple-element.36.refs_0_, ...), custom_call_target="tpu_custom_call" | custom-call | flops 3221225472 | bytes 3221225 | tf_op jit(solution)/shard_map/pallas_call | solution.py:38
  66.1 4.0 %shard_map.99 = (bf16[4,128,1536]{2,1,0:T(8,128)(2,1)S(1)}, bf16[4,128,1536]{2,1,0:T(8,128)(2,1)S(1)}) custom-call(s32[10]{0:T(128)S(1)} %stack.71.scal, bf16[1024,512]{1,0:T(8,128)(2,1)S(1)} %get-tuple-element.51.rows_a, bf16[1024,512]{1,0:T(8,128)(2,1)S(1)} %get-tuple-element.52.rows_b, bf16[512,1536]{1,0:T(8,128)(2,1)S(1)} %get-tuple-element.56.pair_a, ...), custom_call_target="tpu_custom_call" | custom-call | flops 3221225472 | bytes 3221225 | tf_op jit(solution)/shard_map/pallas_call | solution.py:38
  70.2 3.4 %collective-permute-done.7 = bf16[4,128,1536]{2,1,0:T(8,128)(2,1)S(1)} collective-permute-done((bf16[4,128,1536]{2,1,0:T(8,128)(2,1)S(1)}, bf16[4,128,1536]{2,1,0:T(8,128)(2,1)S(1)}, u32[]{:S(2)}, u32[]{:S(2)}) %collective-permute-start.7) | collective-permute-done | bytes 1572896 | tf_op jit(solution)/shard_map/ppermute | solution.py:182
  73.5 1.6 %add_convert_fusion = bf16[4,128,1536]{2,1,0:T(8,128)(2,1)} fusion(bf16[4,128,1536]{2,1,0:T(8,128)(2,1)S(1)} %collective-permute-done.7, bf16[4,128,1536]{2,1,0:T(8,128)(2,1)S(1)} %get-tuple-element.54), kind=kLoop, calls=%fused_computation | loop fusion | flops 3145728 | bytes 4718592 | tf_op jit(solution)/shard_map/convert_element_type | solution.py:265
  75.1 4.9 %all-to-all-start = ((bf16[4,128,1536]{2,1,0:T(8,128)(2,1)}), bf16[4,128,1536]{2,1,0:T(8,128)(2,1)}, u32[]{:S(2)}, u32[]{:S(2)}) async-start(bf16[4,128,1536]{2,1,0:T(8,128)(2,1)} %add_convert_fusion), calls=%async_computation | async-start | bytes 3145728 | tf_op jit(solution)/shard_map/all_to_all | solution.py:266
  80.0 2.8 %copy-done.1 = bf16[2,1024,1536]{2,1,0:T(8,128)(2,1)S(1)} copy-done((bf16[2,1024,1536]{2,1,0:T(8,128)(2,1)S(1)}, bf16[2,1024,1536]{2,1,0:T(8,128)(2,1)}, u32[]{:S(2)}) %copy-start.1) | copy-done | bytes 6291480
  82.8 1.4 copy-done.4
  84.2 5.1 %shard_map.100 = (bf16[256,1024]{1,0:T(8,128)(2,1)S(1)}, bf16[256,1024]{1,0:T(8,128)(2,1)}, bf16[256,1024]{1,0:T(8,128)(2,1)}, bf16[256,1024]{1,0:T(8,128)(2,1)}) custom-call(s32[10]{0:T(128)S(1)} %stack.71.scal, bf16[512,1536]{1,0:T(8,128)(2,1)S(1)} %get-tuple-element.56.pair_a, bf16[512,1536]{1,0:T(8,128)(2,1)S(1)} %copy-done.4, ...), custom_call_target="tpu_custom_call" | custom-call | flops 3221225472 | bytes 3221225 | tf_op jit(solution)/shard_map/pallas_call | solution.py:38
  89.3 1.2 collective-permute-start.8
  90.5 0.8 collective-permute-start.9
  91.3 1.4 collective-permute-start.10
  92.8 0.9 copy-done.6
  93.7 0.9 fusion.2
  94.6 2.9 %collective-permute-start.15 = (bf16[96,1024]{1,0:T(8,128)(2,1)}, bf16[96,1024]{1,0:T(8,128)(2,1)}, u32[]{:S(2)}, u32[]{:S(2)}) collective-permute-start(bf16[96,1024]{1,0:T(8,128)(2,1)} %get-tuple-element.70), channel_id=1, source_target_pairs={{0,16},{4,20},{8,24},{12,28},{16,0},{20,4},{24,8},{28,12},{1,17},{... | collective-permute-start | bytes 589832 | tf_op jit(solution)/shard_map/ppermute | solution.py:183
  97.5 1.5 %collective-permute-start.14 = (bf16[96,1024]{1,0:T(8,128)(2,1)}, bf16[96,1024]{1,0:T(8,128)(2,1)}, u32[]{:S(2)}, u32[]{:S(2)}) collective-permute-start(bf16[96,1024]{1,0:T(8,128)(2,1)} %get-tuple-element.71), channel_id=1, source_target_pairs={{0,8},{4,12},{8,0},{12,4},{16,24},{20,28},{24,16},{28,20},{1,9},{5... | collective-permute-start | bytes 589832 | tf_op jit(solution)/shard_map/ppermute | solution.py:183
  99.0 5.2 %collective-permute-done.8.refs_1_ = bf16[256,1024]{1,0:T(8,128)(2,1)S(1)} collective-permute-done((bf16[256,1024]{1,0:T(8,128)(2,1)}, bf16[256,1024]{1,0:T(8,128)(2,1)S(1)}, u32[]{:S(2)}, u32[]{:S(2)}) %collective-permute-start.8) | collective-permute-done | bytes 524320 | tf_op jit(solution)/shard_map/ppermute | solution.py:184
  104.2 3.8 %collective-permute-start.13 = (bf16[96,1024]{1,0:T(8,128)(2,1)}, bf16[96,1024]{1,0:T(8,128)(2,1)S(1)}, u32[]{:S(2)}, u32[]{:S(2)}) collective-permute-start(bf16[96,1024]{1,0:T(8,128)(2,1)} %get-tuple-element.69), channel_id=1, source_target_pairs={{0,24},{4,28},{8,16},{12,20},{16,8},{20,12},{24,0},{28,4},{1,25},{... | collective-permute-start | bytes 589832 | tf_op jit(solution)/shard_map/ppermute | solution.py:183
  108.0 6.4 %collective-permute-done.9.refs_2_ = bf16[256,1024]{1,0:T(8,128)(2,1)S(1)} collective-permute-done((bf16[256,1024]{1,0:T(8,128)(2,1)}, bf16[256,1024]{1,0:T(8,128)(2,1)S(1)}, u32[]{:S(2)}, u32[]{:S(2)}) %collective-permute-start.9) | collective-permute-done | bytes 524320 | tf_op jit(solution)/shard_map/ppermute | solution.py:184
  114.5 1.5 %collective-permute-done.10.refs_3_ = bf16[256,1024]{1,0:T(8,128)(2,1)S(1)} collective-permute-done((bf16[256,1024]{1,0:T(8,128)(2,1)}, bf16[256,1024]{1,0:T(8,128)(2,1)S(1)}, u32[]{:S(2)}, u32[]{:S(2)}) %collective-permute-start.10) | collective-permute-done | bytes 524320 | tf_op jit(solution)/shard_map/ppermute | solution.py:184
  116.0 1.2 shard_map.101
  117.3 2.1 %collective-permute-start.11 = (bf16[256,1024]{1,0:T(8,128)(2,1)S(1)}, bf16[256,1024]{1,0:T(8,128)(2,1)S(1)}, u32[]{:S(2)}, u32[]{:S(2)}) collective-permute-start(bf16[256,1024]{1,0:T(8,128)(2,1)S(1)} %get-tuple-element.62), channel_id=1, source_target_pairs={{0,8},{4,12},{8,0},{12,4},{16,24},{20,28},{24,16},{28,20},{1,9},{5... | collective-permute-start | bytes 1572872 | tf_op jit(solution)/shard_map/ppermute | solution.py:183
  119.4 11.7 %collective-permute-done.15 = bf16[96,1024]{1,0:T(8,128)(2,1)} collective-permute-done((bf16[96,1024]{1,0:T(8,128)(2,1)}, bf16[96,1024]{1,0:T(8,128)(2,1)}, u32[]{:S(2)}, u32[]{:S(2)}) %collective-permute-start.15) | collective-permute-done | bytes 196640 | tf_op jit(solution)/shard_map/ppermute | solution.py:183
  131.0 1.1 add_bitcast_fusion
  132.1 1.0 fusion
  133.1 1.0 maximum_select_fusion
  134.1 7.0 %collective-permute-done.11 = bf16[256,1024]{1,0:T(8,128)(2,1)S(1)} collective-permute-done((bf16[256,1024]{1,0:T(8,128)(2,1)S(1)}, bf16[256,1024]{1,0:T(8,128)(2,1)S(1)}, u32[]{:S(2)}, u32[]{:S(2)}) %collective-permute-start.11) | collective-permute-done | bytes 524320 | tf_op jit(solution)/shard_map/ppermute | solution.py:183
  141.1 1.0 add_convert_fusion.1
  142.1 1.6 %convert_add_fusion.1 = (f32[1,128,1536]{2,1,0:T(8,128)S(1)}, f32[1,128,1536]{2,1,0:T(8,128)S(1)}) fusion(bf16[4,128,1536]{2,1,0:T(8,128)(2,1)} %all-to-all-done), kind=kLoop, calls=%fused_computation.6 | loop fusion | flops 1179648 | bytes 3145728 | tf_op jit(solution)/shard_map/add | solution.py:270
  143.7 1.3 pad_maximum_fusion
  (33 shorter events, 0.3 us)
Async XLA Ops:
  2.9 56.5 %slice-start = ((s8[6291456]{0:T(1024)(128)(4,1)}), s8[2097152]{0:T(1024)(128)(4,1)S(1)}, s32[]{:S(2)}) async-start(s8[6291456]{0:T(1024)(128)(4,1)} %bitcast.26), calls=%async_computation.1 | async-start | bytes 4194304
  4.3 27.1 %collective-permute-start = (bf16[528,1024]{1,0:T(8,128)(2,1)S(1)}, bf16[528,1024]{1,0:T(8,128)(2,1)}, u32[]{:S(2)}, u32[]{:S(2)}) collective-permute-start(bf16[528,1024]{1,0:T(8,128)(2,1)S(1)} %pad_maximum_fusion.1.block), channel_id=1, source_target_pairs={{0,8},{4,12},{8,0},{12,4},{16,24},{20,28},{24,16},{28,20},{1,9},{5... | collective-permute-start | bytes 3244040 | tf_op jit(solution)/shard_map/ppermute | solution.py:183
  8.8 28.4 %collective-permute-start.1 = (bf16[2,128,1024]{2,1,0:T(8,128)(2,1)S(1)}, bf16[2,128,1024]{2,1,0:T(8,128)(2,1)S(1)}, u32[]{:S(2)}, u32[]{:S(2)}) collective-permute-start(bf16[2,128,1024]{2,1,0:T(8,128)(2,1)S(1)} %get-tuple-element.37), channel_id=1, source_target_pairs={{0,1},{1,0},{2,3},{3,2},{4,5},{5,4},{6,7},{7,6},{8,9},{9,8},{10,11... | collective-permute-start | bytes 1572872 | tf_op jit(solution)/shard_map/ppermute | solution.py:184
  10.4 27.1 %collective-permute-start.2 = (bf16[2,128,1024]{2,1,0:T(8,128)(2,1)S(1)}, bf16[2,128,1024]{2,1,0:T(8,128)(2,1)S(1)}, u32[]{:S(2)}, u32[]{:S(2)}) collective-permute-start(bf16[2,128,1024]{2,1,0:T(8,128)(2,1)S(1)} %get-tuple-element.38), channel_id=1, source_target_pairs={{0,2},{1,3},{2,0},{3,1},{4,6},{5,7},{6,4},{7,5},{8,10},{9,11},{10,... | collective-permute-start | bytes 1572872 | tf_op jit(solution)/shard_map/ppermute | solution.py:184
  11.9 25.6 %collective-permute-start.3 = (bf16[2,128,1024]{2,1,0:T(8,128)(2,1)S(1)}, bf16[2,128,1024]{2,1,0:T(8,128)(2,1)S(1)}, u32[]{:S(2)}, u32[]{:S(2)}) collective-permute-start(bf16[2,128,1024]{2,1,0:T(8,128)(2,1)S(1)} %get-tuple-element.39), channel_id=1, source_target_pairs={{0,3},{1,2},{2,1},{3,0},{4,7},{5,6},{6,5},{7,4},{8,11},{9,10},{10,... | collective-permute-start | bytes 1572872 | tf_op jit(solution)/shard_map/ppermute | solution.py:184
  33.9 14.9 %collective-permute-start.4 = (bf16[2,128,1024]{2,1,0:T(8,128)(2,1)S(1)}, bf16[2,128,1024]{2,1,0:T(8,128)(2,1)S(1)}, u32[]{:S(2)}, u32[]{:S(2)}) collective-permute-start(bf16[2,128,1024]{2,1,0:T(8,128)(2,1)S(1)} %get-tuple-element.41), channel_id=1, source_target_pairs={{0,1},{1,0},{2,3},{3,2},{4,5},{5,4},{6,7},{7,6},{8,9},{9,8},{10,11... | collective-permute-start | bytes 1572872 | tf_op jit(solution)/shard_map/ppermute | solution.py:184
  35.6 23.7 %collective-permute-start.5 = (bf16[2,128,1024]{2,1,0:T(8,128)(2,1)S(1)}, bf16[2,128,1024]{2,1,0:T(8,128)(2,1)S(1)}, u32[]{:S(2)}, u32[]{:S(2)}) collective-permute-start(bf16[2,128,1024]{2,1,0:T(8,128)(2,1)S(1)} %get-tuple-element.42), channel_id=1, source_target_pairs={{0,2},{1,3},{2,0},{3,1},{4,6},{5,7},{6,4},{7,5},{8,10},{9,11},{10,... | collective-permute-start | bytes 1572872 | tf_op jit(solution)/shard_map/ppermute | solution.py:184
  37.2 22.2 %collective-permute-start.6 = (bf16[2,128,1024]{2,1,0:T(8,128)(2,1)S(1)}, bf16[2,128,1024]{2,1,0:T(8,128)(2,1)S(1)}, u32[]{:S(2)}, u32[]{:S(2)}) collective-permute-start(bf16[2,128,1024]{2,1,0:T(8,128)(2,1)S(1)} %get-tuple-element.43), channel_id=1, source_target_pairs={{0,3},{1,2},{2,1},{3,0},{4,7},{5,6},{6,5},{7,4},{8,11},{9,10},{10,... | collective-permute-start | bytes 1572872 | tf_op jit(solution)/shard_map/ppermute | solution.py:184
  37.5 2.8 %copy-start = (bf16[2,1024,1536]{2,1,0:T(8,128)(2,1)S(1)}, bf16[2,1024,1536]{2,1,0:T(8,128)(2,1)}, u32[]{:S(2)}) copy-start(bf16[2,1024,1536]{2,1,0:T(8,128)(2,1)} %w_in.1) | copy-start | bytes 18874372
  40.3 19.1 %slice-start.1 = ((s8[6291456]{0:T(1024)(128)(4,1)}), s8[4194304]{0:T(1024)(128)(4,1)S(1)}, s32[]{:S(2)}) async-start(s8[6291456]{0:T(1024)(128)(4,1)} %bitcast.26), calls=%async_computation.2 | async-start | bytes 8388608
  59.4 2.5 %copy-start.2 = (bf16[2,768,1024]{2,1,0:T(8,128)(2,1)S(1)}, bf16[2,768,1024]{2,1,0:T(8,128)(2,1)}, u32[]{:S(2)}) copy-start(bf16[2,768,1024]{2,1,0:T(8,128)(2,1)} %refs_8_.1) | copy-start | bytes 9437188
  66.1 4.0 %copy-start.3 = (bf16[512,1536]{1,0:T(8,128)(2,1)}, bf16[512,1536]{1,0:T(8,128)(2,1)S(1)}, u32[]{:S(2)}) copy-start(bf16[512,1536]{1,0:T(8,128)(2,1)S(1)} %get-tuple-element.53.pair_b) | copy-start | bytes 4718596
  66.1 4.0 %copy-start.5 = (bf16[4,96,1024]{2,1,0:T(8,128)(2,1)}, bf16[4,96,1024]{2,1,0:T(8,128)(2,1)S(1)}, u32[]{:S(2)}) copy-start(bf16[4,96,1024]{2,1,0:T(8,128)(2,1)S(1)} %get-tuple-element.64) | copy-start | bytes 2359300
  70.1 3.5 %collective-permute-start.7 = (bf16[4,128,1536]{2,1,0:T(8,128)(2,1)S(1)}, bf16[4,128,1536]{2,1,0:T(8,128)(2,1)S(1)}, u32[]{:S(2)}, u32[]{:S(2)}) collective-permute-start(bf16[4,128,1536]{2,1,0:T(8,128)(2,1)S(1)} %get-tuple-element.55), channel_id=1, source_target_pairs={{0,4},{4,0},{8,12},{12,8},{16,20},{20,16},{24,28},{28,24},{1,5},{5... | collective-permute-start | bytes 4718600 | tf_op jit(solution)/shard_map/ppermute | solution.py:182
  75.1 67.0 %all-to-all-start = ((bf16[4,128,1536]{2,1,0:T(8,128)(2,1)}), bf16[4,128,1536]{2,1,0:T(8,128)(2,1)}, u32[]{:S(2)}, u32[]{:S(2)}) async-start(bf16[4,128,1536]{2,1,0:T(8,128)(2,1)} %add_convert_fusion), calls=%async_computation | async-start | bytes 3145728 | tf_op jit(solution)/shard_map/all_to_all | solution.py:266
  80.0 12.8 %collective-permute-start.12 = (bf16[4,96,1024]{2,1,0:T(8,128)(2,1)}, bf16[4,96,1024]{2,1,0:T(8,128)(2,1)S(1)}, u32[]{:S(2)}, u32[]{:S(2)}) collective-permute-start(bf16[4,96,1024]{2,1,0:T(8,128)(2,1)} %copy-done.5), channel_id=1, source_target_pairs={{0,4},{4,0},{8,12},{12,8},{16,20},{20,16},{24,28},{28,24},{1,5},{5... | collective-permute-start | bytes 2359304 | tf_op jit(solution)/shard_map/ppermute | solution.py:182
  80.0 2.8 %copy-start.1 = (bf16[2,1024,1536]{2,1,0:T(8,128)(2,1)S(1)}, bf16[2,1024,1536]{2,1,0:T(8,128)(2,1)}, u32[]{:S(2)}) copy-start(bf16[2,1024,1536]{2,1,0:T(8,128)(2,1)} %w_in.1) | copy-start | bytes 18874372
  82.8 1.4 copy-start.4
  89.3 14.9 %collective-permute-start.8 = (bf16[256,1024]{1,0:T(8,128)(2,1)}, bf16[256,1024]{1,0:T(8,128)(2,1)S(1)}, u32[]{:S(2)}, u32[]{:S(2)}) collective-permute-start(bf16[256,1024]{1,0:T(8,128)(2,1)} %get-tuple-element.58), channel_id=1, source_target_pairs={{0,1},{1,0},{2,3},{3,2},{4,5},{5,4},{6,7},{7,6},{8,9},{9,8},{10,11... | collective-permute-start | bytes 1572872 | tf_op jit(solution)/shard_map/ppermute | solution.py:184
  90.5 24.0 %collective-permute-start.9 = (bf16[256,1024]{1,0:T(8,128)(2,1)}, bf16[256,1024]{1,0:T(8,128)(2,1)S(1)}, u32[]{:S(2)}, u32[]{:S(2)}) collective-permute-start(bf16[256,1024]{1,0:T(8,128)(2,1)} %get-tuple-element.59), channel_id=1, source_target_pairs={{0,2},{1,3},{2,0},{3,1},{4,6},{5,7},{6,4},{7,5},{8,10},{9,11},{10,... | collective-permute-start | bytes 1572872 | tf_op jit(solution)/shard_map/ppermute | solution.py:184
  91.3 24.7 %collective-permute-start.10 = (bf16[256,1024]{1,0:T(8,128)(2,1)}, bf16[256,1024]{1,0:T(8,128)(2,1)S(1)}, u32[]{:S(2)}, u32[]{:S(2)}) collective-permute-start(bf16[256,1024]{1,0:T(8,128)(2,1)} %get-tuple-element.60), channel_id=1, source_target_pairs={{0,3},{1,2},{2,1},{3,0},{4,7},{5,6},{6,5},{7,4},{8,11},{9,10},{10,... | collective-permute-start | bytes 1572872 | tf_op jit(solution)/shard_map/ppermute | solution.py:184
  92.8 0.9 copy-start.6
  94.6 36.5 %collective-permute-start.15 = (bf16[96,1024]{1,0:T(8,128)(2,1)}, bf16[96,1024]{1,0:T(8,128)(2,1)}, u32[]{:S(2)}, u32[]{:S(2)}) collective-permute-start(bf16[96,1024]{1,0:T(8,128)(2,1)} %get-tuple-element.70), channel_id=1, source_target_pairs={{0,16},{4,20},{8,24},{12,28},{16,0},{20,4},{24,8},{28,12},{1,17},{... | collective-permute-start | bytes 589832 | tf_op jit(solution)/shard_map/ppermute | solution.py:183
  97.5 33.5 %collective-permute-start.14 = (bf16[96,1024]{1,0:T(8,128)(2,1)}, bf16[96,1024]{1,0:T(8,128)(2,1)}, u32[]{:S(2)}, u32[]{:S(2)}) collective-permute-start(bf16[96,1024]{1,0:T(8,128)(2,1)} %get-tuple-element.71), channel_id=1, source_target_pairs={{0,8},{4,12},{8,0},{12,4},{16,24},{20,28},{24,16},{28,20},{1,9},{5... | collective-permute-start | bytes 589832 | tf_op jit(solution)/shard_map/ppermute | solution.py:183
  104.2 27.9 %collective-permute-start.13 = (bf16[96,1024]{1,0:T(8,128)(2,1)}, bf16[96,1024]{1,0:T(8,128)(2,1)S(1)}, u32[]{:S(2)}, u32[]{:S(2)}) collective-permute-start(bf16[96,1024]{1,0:T(8,128)(2,1)} %get-tuple-element.69), channel_id=1, source_target_pairs={{0,24},{4,28},{8,16},{12,20},{16,8},{20,12},{24,0},{28,4},{1,25},{... | collective-permute-start | bytes 589832 | tf_op jit(solution)/shard_map/ppermute | solution.py:183
  117.3 23.9 %collective-permute-start.11 = (bf16[256,1024]{1,0:T(8,128)(2,1)S(1)}, bf16[256,1024]{1,0:T(8,128)(2,1)S(1)}, u32[]{:S(2)}, u32[]{:S(2)}) collective-permute-start(bf16[256,1024]{1,0:T(8,128)(2,1)S(1)} %get-tuple-element.62), channel_id=1, source_target_pairs={{0,8},{4,12},{8,0},{12,4},{16,24},{20,28},{24,16},{28,20},{1,9},{5... | collective-permute-start | bytes 1572872 | tf_op jit(solution)/shard_map/ppermute | solution.py:183

commit v3 on v2

--- a/solution.py
+++ b/solution.py
@@ -49,8 +49,8 @@
     )(scal, *args)
 
 
-def stack_rows(refs, index):
-    return jnp.concatenate([ref[index] for ref in refs], axis=0)
+def stack_rows(refs, column, columns):
+    return jnp.concatenate([ref[:, pl.ds(column, columns)] for ref in refs], axis=0)
 
 
 def after(value, *others):
@@ -90,15 +90,19 @@
     hit = hit.astype(BF)
     rows = dot(hit, block[pl.ds(ROUTE_ROWS, tokens), :]).astype(BF)
     scaled = (dot(hit, block[pl.ds(ROUTE_ROWS + tokens, tokens), :]) * factor).astype(BF)
-    for j, out in enumerate(outs):
-        out[0] = rows[j * cap : (j + 1) * cap]
-        out[1] = scaled[j * cap : (j + 1) * cap]
+    rows = jnp.concatenate([rows, scaled], axis=1)
+    column = 0
+    for k in range(0, len(outs), n):
+        columns = outs[k].shape[1]
+        for j in range(n):
+            outs[k + j][...] = rows[j * cap : (j + 1) * cap, column : column + columns]
+        column += columns
 
 
 def forward_body(tile, scal, *refs):
     *arrived, w_in, rows_t, hidden_t, scale_gate, scale_up = refs
     ff = w_in.shape[2] // 2
-    rows = stack_rows(arrived, 0)
+    rows = stack_rows(arrived, 0, w_in.shape[1])
     rows_t[...] = jnp.transpose(rows)
     for f in range(0, ff, tile):
         gate = dot(rows, w_in[0, :, pl.ds(f, tile)])
@@ -110,22 +114,25 @@
         scale_up[:, pl.ds(f, tile)] = activated.astype(BF)
 
 
-def shard_rows(sources, scal, shards, part):
+def shard_rows(sources, scal, nz, part):
     taken = []
     for offset in (1 - scal[1], scal[1]):
-        for shard in shards:
+        for shard in range(nz):
             start = pl.multiple_of((2 * shard + offset) * part, 16)
             taken.append(jnp.concatenate([x[pl.ds(start, part), :] for x in sources], axis=1))
     return jnp.concatenate(taken, axis=0)
 
 
 def down_body(n, nz, scal, *refs):
-    arrived, (w_down, hidden_a, hidden_b, *scales), outs = refs[: 2 * n], refs[2 * n : 2 * n + 7], refs[2 * n + 7 :]
+    arrived, (w_down, hidden_a, hidden_b, *scales), outs = (
+        refs[: 2 * n],
+        refs[2 * n : 2 * n + 7],
+        refs[2 * n + 7 :],
+    )
     give, keep, *pairs = outs
-    part = give.shape[1]
-    slots = [stack_rows(arrived[:n], 1), stack_rows(arrived[n:], 1)]
-    shards = [scal[scal.shape[0] - nz + k] for k in range(nz)]
-    left = shard_rows((hidden_a, hidden_b), scal, shards, part)
+    part, width = give.shape[1:]
+    slots = [stack_rows(arrived[:n], width, width), stack_rows(arrived[n:], 0, width)]
+    left = shard_rows((hidden_a, hidden_b), scal, nz, part)
     result = dot(left, jnp.concatenate(slots, axis=0)).astype(BF)
     for k in range(nz):
         give[k] = result[k * part : (k + 1) * part]
@@ -143,10 +150,46 @@
     pair = jnp.concatenate(
         [pair_a[:, pl.ds(first, columns)], pair_b[:, pl.ds(first, columns)]], axis=0
     )
-    result = dot(shard_rows((rows_a, rows_b), scal, range(nz), part), pair).astype(BF)
+    result = dot(shard_rows((rows_a, rows_b), scal, nz, part), pair).astype(BF)
     for k in range(nz):
         give[k] = result[k * part : (k + 1) * part]
         keep[k] = result[(nz + k) * part : (nz + k + 1) * part]
+
+
+def in_blocks(rows, width, columns):
+    blocks = [(c, width, 0, rows, c // width * rows, 0) for c in range(0, columns - width + 1, width)]
+    rest = columns % width
+    first = columns - rest
+    count = rest * rows // width
+    for k in range(width // rest if rest else 0):
+        blocks.append((first, rest, k * count, count, first // width * rows, k * rest))
+    return blocks
+
+
+def pack_body(nz, scal, keep_down, other_down, *refs):
+    ins, out = refs[:-1], refs[-1]
+    width = keep_down.shape[2]
+    top = keep_down.shape[1]
+    rows = ins[0].shape[1]
+    for k in range(nz):
+        out[k, pl.ds(0, top), :] = keep_down[k] + other_down[k]
+        total = jnp.concatenate([x[k] + y[k] for x, y in zip(ins[::2], ins[1::2])], axis=1)
+        for c, columns, r, count, place, column in in_blocks(rows, width, total.shape[1]):
+            out[k, pl.ds(top + place, count), pl.ds(column, columns)] = total[
+                r : r + count, c : c + columns
+            ]
+
+
+def unpack_body(sets, scal, terms, grad_in, grad_down):
+    top, width = grad_down.shape[1:]
+    rows, columns = grad_in.shape[1:]
+    for e, members in enumerate(sets):
+        total = functools.reduce(jnp.add, [terms[k].astype(F32) for k in members])
+        grad_down[e] = total[:top]
+        for c, some, r, count, place, column in in_blocks(rows, width, columns):
+            grad_in[e, pl.ds(r, count), pl.ds(c, some)] = total[
+                top + place : top + place + count, column : column + some
+            ]
 
 
 def returned_body(cap, scal, pair_a, pair_b, w_in, *outs):
@@ -182,27 +225,29 @@
     swap_core = lambda x: lax.ppermute(x, "dp", [(i, i ^ 1) for i in range(ndp)])
     along_z = lambda x, k: lax.ppermute(x, "dp", [(i, i ^ (2 * k)) for i in range(ndp)]) if k else x
     across = lambda x, j: lax.ppermute(x, "expert", [(i, i ^ j) for i in range(n)]) if j else x
+    same_core = [list(range(c, ndp, 2)) for c in range(2)]
     macs = 2 * slots * width * ff
 
     block = jnp.concatenate(
         [route_rows(route_logits, expert_ids, slot_pos, width), tokens, cotangent], axis=0
     )
+    messages = ([2 * width], [width, width])
     arrived, backs = [], []
-    for block in (block, along_z(block, 1)):
+    for parts, block in zip(messages, (block, along_z(block, 1))):
         *sent, back = call(
             functools.partial(slots_body, cap, n),
-            [bf(2, cap, width)] * n + [bf(token_count, slots)],
+            [bf(cap, c) for c in parts for _ in range(n)] + [bf(token_count, slots)],
             macs // 4,
             LIMITS[0],
             scal,
             block,
         )
-        arrived += [across(x, j) for j, x in enumerate(sent)]
+        arrived.append([across(x, k % n) for k, x in enumerate(sent)])
         backs.append(back)
 
     forwards = []
     for g in range(2):
-        pieces = arrived[g * n : (g + 1) * n]
+        pieces = arrived[g][:n]
         forwards.append(
             call(
                 functools.partial(forward_body, 256),
@@ -217,10 +262,10 @@
         )
     (rows_a, hidden_a, *scales_a), (rows_b, hidden_b, *scales_b) = forwards
 
-    args = arrived + [w_down, hidden_a, hidden_b] + scales_a + scales_b
+    args = arrived[0] + arrived[1][n:] + [w_down, hidden_a, hidden_b] + scales_a + scales_b
     specs = [whole(x) for x in args]
     specs[2 * n] = of_expert(w_down)
-    *down, pair_a, pair_b = call(
+    give, keep, *pairs = call(
         functools.partial(down_body, n, nz),
         [bf(nz, ff // ndp, width)] * 2 + [bf(slots, 2 * ff)] * 2,
         4 * macs,
@@ -229,11 +274,11 @@
         *args,
         specs=specs,
     )
-    pairs = (pair_a, pair_b)
+    terms = [keep, swap_core(give)]
 
     columns = 2 * ff // IN_PARTS
-    ins = [
-        call(
+    for k in range(IN_PARTS):
+        give, keep = call(
             functools.partial(input_weight_body, k * columns, nz),
             [bf(nz, width // ndp, columns)] * 2,
             4 * macs // IN_PARTS,
@@ -243,42 +288,35 @@
             rows_b,
             *pairs,
         )
-        for k in range(IN_PARTS)
-    ]
-
-    def core_sum(give, keep):
-        other = swap_core(give)
-        return [(keep[k].astype(F32) + other[k].astype(F32)).astype(BF) for k in range(nz)]
-
-    def gather_z(terms):
-        return [along_z(x, k) for k, x in enumerate(terms)]
-
-    def over_z(terms):
-        same, different = (
-            sum(terms[k].astype(F32) for k in range(nz) if expert_of(k) == e) for e in range(2)
-        )
-        return jnp.where(mine == 0, jnp.stack([same, different]), jnp.stack([different, same]))
-
-    down_terms = gather_z(core_sum(*down))
-    grad_down = over_z(down_terms)
-    (give, keep) = ins[0]
-    total = (keep.astype(F32) + swap_core(give).astype(F32)).astype(BF)
-    terms = lax.all_to_all(
-        total, "dp", 0, 0, tiled=True, axis_index_groups=[list(range(c, ndp, 2)) for c in range(2)]
-    )
-    grad_in = jnp.stack(
-        [sum(terms[k].astype(F32) for k in range(nz) if expert_of(k) == e) for e in range(experts)]
-    )
+        terms += [keep, swap_core(give)]
     sent = call(
         functools.partial(returned_body, cap),
         [bf(2 * cap, width)] * n,
         4 * macs,
         LIMITS[4],
         scal,
-        after(pairs[0], total),
+        pairs[0],
         pairs[1],
         w_in,
         specs=[whole(x) for x in pairs] + [of_expert(w_in)],
+    )
+    terms[-1] = after(terms[-1], *sent)
+    rows = ff // ndp + width // ndp * 2 * ff // width
+    (total,) = call(
+        functools.partial(pack_body, nz), [bf(nz, rows, width)], 1, LIMITS[6], scal, *terms
+    )
+    total = lax.all_to_all(total, "dp", 0, 0, tiled=True, axis_index_groups=same_core)
+    sets = [[k for k in range(nz) if expert_of(k) == e] for e in range(experts)]
+    grad_in, grad_down = call(
+        functools.partial(unpack_body, sets),
+        [
+            jax.ShapeDtypeStruct((experts, width // ndp, 2 * ff), F32),
+            jax.ShapeDtypeStruct((experts, ff // ndp, width), F32),
+        ],
+        1,
+        LIMITS[6],
+        scal,
+        total,
     )
     mine_sum, beside_sum = call(
         functools.partial(combine_body, cap),
@@ -293,7 +331,7 @@
     return (input_grad, grad_in, grad_down)
 
 
-LIMITS = (24, 28, 28, 24, 24, 16)
+LIMITS = (16, 20, 20, 20, 20, 12, 20)
 
 
 def solution(mesh):

time: 145 us -> 137 us (0.945)
  other arithmetic: 13 us -> 4.6 us
  local copies, waits for them, and re-layouts: 8 us -> 4.02 us
  Pallas kernels: 23.2 us -> 26.5 us
  waiting for transfers between devices: 71 us -> 73.8 us
  starting transfers between devices: 28.9 us -> 26.7 us
    ppermute x5 -> x2, starting transfers between devices: 13.4 us -> 4.9 us  [per_device(): lax.ppermute(x, 'dp', [(i, i ^ 2 * k) for i in range(ndp)])]
    ppermute x9 -> x12, starting transfers between devices: 10.6 us -> 16.4 us  [per_device(): lax.ppermute(x, 'expert', [(i, i ^ j) for i in range(n)])]
    unnamed x18 -> x14, local copies, waits for them, and re-layouts: 7.88 us -> 3.9 us
    all_to_all x1, waiting for transfers between devices: 0.01 us -> 3.47 us  [per_device(): lax.all_to_all(total, 'dp', 0, 0, tiled=True, axis_index_groups=same_core)]
    ppermute x2, waiting for transfers between devices: 3.4 us -> 0.01 us  [per_device(): lax.ppermute(x, 'dp', [(i, i ^ 1) for i in range(ndp)])]
    another operation x5 -> x2, other arithmetic: 4.69 us -> 1.37 us  [the longest x2 2.07 us: over_z(): jnp.stack([same, different])]
    pallas_call x8 -> x10, Pallas kernels: 23.2 us -> 26.5 us  [call(): pl.pallas_call(body, out_shape=out_shape, grid_spec=pltpu.PrefetchScalarG...]
    convert_element_type x2 -> x0, other arithmetic: 2.5 us -> none  [the longest x1 1.56 us: per_device(): total = (keep.astype(F32) + swap_core(give).astype(F32)).astype(BF)]
  transfers between devices with their start and end apart: 17 -> 17, of which waited for: 9 -> 9; matrix products, arithmetic and copies ran while one was open for 3% -> 1% of each run, Pallas kernels for 9% -> 10%
where the time goes in v3:
time: 137 us; the launch traced here: 136 us
  waiting for transfers between devices  73.8 us (54%)
  starting transfers between devices  26.7 us (19%)
  Pallas kernels  26.5 us (19%)
  other arithmetic  4.6 us (3%)
  local copies, waits for them, and re-layouts  4.02 us (3%)
    ppermute x2, waiting for transfers between devices, per_device(): lax.ppermute(x, 'dp', [(i, i ^ 2 * k) for i in range(ndp)])  39.5 us
    ppermute x12, waiting for transfers between devices, per_device(): lax.ppermute(x, 'expert', [(i, i ^ j) for i in range(n)])  30.8 us
    pallas_call x10, Pallas kernels, call(): pl.pallas_call(body, out_shape=out_shape, grid_spec=pltpu.PrefetchScalarG...  26.5 us
    ppermute x12, starting transfers between devices, per_device(): lax.ppermute(x, 'expert', [(i, i ^ j) for i in range(n)])  16.4 us
    ppermute x2, starting transfers between devices, per_device(): lax.ppermute(x, 'dp', [(i, i ^ 2 * k) for i in range(ndp)])  4.9 us
    all_to_all x1, starting transfers between devices, per_device(): lax.all_to_all(total, 'dp', 0, 0, tiled=True, axis_index_groups=same_core)  4.87 us
    unnamed x14, local copies, waits for them, and re-layouts  3.9 us
    all_to_all x1, waiting for transfers between devices, per_device(): lax.all_to_all(total, 'dp', 0, 0, tiled=True, axis_index_groups=same_core)  3.47 us
  transfers between devices with their start and end apart: 17, of which 9 were waited for; matrix products, arithmetic and copies ran while one was open for 1% of the time, Pallas kernels for 10%

profile of v3, /device:TPU:0, one launch (start us, length us, event | category | flops | bytes accessed | tf_op | source)
XLA Modules:
  0.0 136.5 jit_solution(5621585977887605136)
XLA Ops:
  0.6 0.8 add_divide_fusion
  1.4 0.7 convert.8
  2.1 0.7 convert.9
  2.9 0.0 slice-start
  2.9 1.4 %pad_maximum_fusion.block = bf16[528,1024]{1,0:T(8,128)(2,1)S(1)} fusion(bf16[256,1024]{1,0:T(8,128)(2,1)} %param.8, bf16[256,1024]{1,0:T(8,128)(2,1)} %param.7, bf16[16,1024]{1,0:T(8,128)(2,1)S(1)} %fusion.2), kind=kLoop, calls=%fused_computation | loop fusion | flops 3244032 | bytes 2162688 | tf_op jit(solution)/shard_map/concatenate | solution.py:231
  4.3 3.1 %collective-permute-start = (bf16[528,1024]{1,0:T(8,128)(2,1)S(1)}, bf16[528,1024]{1,0:T(8,128)(2,1)}, u32[]{:S(2)}, u32[]{:S(2)}) collective-permute-start(bf16[528,1024]{1,0:T(8,128)(2,1)S(1)} %pad_maximum_fusion.block), channel_id=1, source_target_pairs={{0,8},{4,12},{8,0},{12,4},{16,24},{20,28},{24,16},{28,20},{1,9},{5... | collective-permute-start | bytes 3244040 | tf_op jit(solution)/shard_map/ppermute | solution.py:226
  7.4 0.1 stack.52.scal
  7.5 1.3 shard_map.94
  8.8 1.6 %collective-permute-start.1 = (bf16[128,2048]{1,0:T(8,128)(2,1)S(1)}, bf16[128,2048]{1,0:T(8,128)(2,1)S(1)}, u32[]{:S(2)}, u32[]{:S(2)}) collective-permute-start(bf16[128,2048]{1,0:T(8,128)(2,1)S(1)} %get-tuple-element.43), channel_id=1, source_target_pairs={{0,1},{1,0},{2,3},{3,2},{4,5},{5,4},{6,7},{7,6},{8,9},{9,8},{10,11... | collective-permute-start | bytes 1572872 | tf_op jit(solution)/shard_map/ppermute | solution.py:227
  10.4 1.5 %collective-permute-start.2 = (bf16[128,2048]{1,0:T(8,128)(2,1)S(1)}, bf16[128,2048]{1,0:T(8,128)(2,1)S(1)}, u32[]{:S(2)}, u32[]{:S(2)}) collective-permute-start(bf16[128,2048]{1,0:T(8,128)(2,1)S(1)} %get-tuple-element.44), channel_id=1, source_target_pairs={{0,2},{1,3},{2,0},{3,1},{4,6},{5,7},{6,4},{7,5},{8,10},{9,11},{10,... | collective-permute-start | bytes 1572872 | tf_op jit(solution)/shard_map/ppermute | solution.py:227
  11.9 0.5 collective-permute-start.3
  12.4 19.0 %collective-permute-done.block = bf16[528,1024]{1,0:T(8,128)(2,1)} collective-permute-done((bf16[528,1024]{1,0:T(8,128)(2,1)S(1)}, bf16[528,1024]{1,0:T(8,128)(2,1)}, u32[]{:S(2)}, u32[]{:S(2)}) %collective-permute-start) | collective-permute-done | bytes 1081376 | tf_op jit(solution)/shard_map/ppermute | solution.py:226
  31.4 2.5 %shard_map.95 = (bf16[128,1024]{1,0:T(8,128)(2,1)S(1)}, bf16[128,1024]{1,0:T(8,128)(2,1)S(1)}, bf16[128,1024]{1,0:T(8,128)(2,1)S(1)}, bf16[128,1024]{1,0:T(8,128...) custom-call(s32[10]{0:T(128)S(1)} %stack.52.scal, ...), custom_call_target="tpu_custom_call" | custom-call | flops 201326592 | bytes 201326 | tf_op jit(solution)/shard_map/pallas_call | solution.py:38
  33.9 1.7 %collective-permute-start.7 = (bf16[128,1024]{1,0:T(8,128)(2,1)S(1)}, bf16[128,1024]{1,0:T(8,128)(2,1)S(1)}, u32[]{:S(2)}, u32[]{:S(2)}) collective-permute-start(bf16[128,1024]{1,0:T(8,128)(2,1)S(1)} %get-tuple-element.52), channel_id=1, source_target_pairs={{0,1},{1,0},{2,3},{3,2},{4,5},{5,4},{6,7},{7,6},{8,9},{9,8},{10,11... | collective-permute-start | bytes 786440 | tf_op jit(solution)/shard_map/ppermute | solution.py:227
  35.6 1.5 %collective-permute-start.8 = (bf16[128,1024]{1,0:T(8,128)(2,1)S(1)}, bf16[128,1024]{1,0:T(8,128)(2,1)S(1)}, u32[]{:S(2)}, u32[]{:S(2)}) collective-permute-start(bf16[128,1024]{1,0:T(8,128)(2,1)S(1)} %get-tuple-element.53), channel_id=1, source_target_pairs={{0,2},{1,3},{2,0},{3,1},{4,6},{5,7},{6,4},{7,5},{8,10},{9,11},{10,... | collective-permute-start | bytes 786440 | tf_op jit(solution)/shard_map/ppermute | solution.py:227
  37.2 0.3 collective-permute-start.9
  37.5 1.7 %collective-permute-start.4 = (bf16[128,1024]{1,0:T(8,128)(2,1)S(1)}, bf16[128,1024]{1,0:T(8,128)(2,1)S(1)}, u32[]{:S(2)}, u32[]{:S(2)}) collective-permute-start(bf16[128,1024]{1,0:T(8,128)(2,1)S(1)} %get-tuple-element.47), channel_id=1, source_target_pairs={{0,1},{1,0},{2,3},{3,2},{4,5},{5,4},{6,7},{7,6},{8,9},{9,8},{10,11... | collective-permute-start | bytes 786440 | tf_op jit(solution)/shard_map/ppermute | solution.py:227
  39.1 1.5 %collective-permute-start.5 = (bf16[128,1024]{1,0:T(8,128)(2,1)S(1)}, bf16[128,1024]{1,0:T(8,128)(2,1)S(1)}, u32[]{:S(2)}, u32[]{:S(2)}) collective-permute-start(bf16[128,1024]{1,0:T(8,128)(2,1)S(1)} %get-tuple-element.48), channel_id=1, source_target_pairs={{0,2},{1,3},{2,0},{3,1},{4,6},{5,7},{6,4},{7,5},{8,10},{9,11},{10,... | collective-permute-start | bytes 786440 | tf_op jit(solution)/shard_map/ppermute | solution.py:227
  40.7 2.6 %collective-permute-done.7.refs_1_ = bf16[128,1024]{1,0:T(8,128)(2,1)S(1)} collective-permute-done((bf16[128,1024]{1,0:T(8,128)(2,1)S(1)}, bf16[128,1024]{1,0:T(8,128)(2,1)S(1)}, u32[]{:S(2)}, u32[]{:S(2)}) %collective-permute-start.7) | collective-permute-done | bytes 262176 | tf_op jit(solution)/shard_map/ppermute | solution.py:227
  43.2 2.6 %collective-permute-start.6 = (bf16[128,1024]{1,0:T(8,128)(2,1)S(1)}, bf16[128,1024]{1,0:T(8,128)(2,1)S(1)}, u32[]{:S(2)}, u32[]{:S(2)}) collective-permute-start(bf16[128,1024]{1,0:T(8,128)(2,1)S(1)} %get-tuple-element.49), channel_id=1, source_target_pairs={{0,3},{1,2},{2,1},{3,0},{4,7},{5,6},{6,5},{7,4},{8,11},{9,10},{10,... | collective-permute-start | bytes 786440 | tf_op jit(solution)/shard_map/ppermute | solution.py:227
  45.8 2.8 %copy-done = bf16[2,1024,1536]{2,1,0:T(8,128)(2,1)S(1)} copy-done((bf16[2,1024,1536]{2,1,0:T(8,128)(2,1)S(1)}, bf16[2,1024,1536]{2,1,0:T(8,128)(2,1)}, u32[]{:S(2)}) %copy-start) | copy-done | bytes 6291480
  48.6 2.5 %shard_map.96 = (bf16[1024,512]{1,0:T(8,128)(2,1)S(1)}, bf16[768,512]{1,0:T(8,128)(2,1)S(1)}, bf16[512,768]{1,0:T(8,128)(2,1)S(1)}, bf16[512,768]{1,0:T(8,128)(2,1)S(1)}) custom-call(s32[10]{0:T(128)S(1)} %stack.52.scal, bf16[128,2048]{1,0:T(8,128)(2,1)S(1)} %get-tuple-element.42.refs_0_, bf16[128,2048]{1,0:T(8,128)(2,1)S(1)} %collective-permute-done.1.refs_1_, ...), custom_call_target="tpu_custom_call" | custom-call | flops 1610612736 | bytes 1610612 | tf_op jit(solution)/shard_map/pallas_call | solution.py:38
  51.2 0.0 copy-start.1
  51.2 2.5 %shard_map.97 = (bf16[1024,512]{1,0:T(8,128)(2,1)S(1)}, bf16[768,512]{1,0:T(8,128)(2,1)S(1)}, bf16[512,768]{1,0:T(8,128)(2,1)S(1)}, bf16[512,768]{1,0:T(8,128)(2,1)S(1)}) custom-call(s32[10]{0:T(128)S(1)} %stack.52.scal, bf16[128,1024]{1,0:T(8,128)(2,1)S(1)} %get-tuple-element.51.refs_0_, bf16[128,1024]{1,0:T(8,128)(2,1)S(1)} %collective-permute-done.7.refs_1_, ...), custom_call_target="tpu_custom_call" | custom-call | flops 1610612736 | bytes 1610612 | tf_op jit(solution)/shard_map/pallas_call | solution.py:38
  53.7 0.8 collective-permute-done.4.refs_5_
  54.5 4.9 %collective-permute-done.5.refs_6_ = bf16[128,1024]{1,0:T(8,128)(2,1)S(1)} collective-permute-done((bf16[128,1024]{1,0:T(8,128)(2,1)S(1)}, bf16[128,1024]{1,0:T(8,128)(2,1)S(1)}, u32[]{:S(2)}, u32[]{:S(2)}) %collective-permute-start.5) | collective-permute-done | bytes 262176 | tf_op jit(solution)/shard_map/ppermute | solution.py:227
  59.4 4.1 %shard_map.98 = (bf16[4,96,1024]{2,1,0:T(8,128)(2,1)S(1)}, bf16[4,96,1024]{2,1,0:T(8,128)(2,1)S(1)}, bf16[512,1536]{1,0:T(8,128)(2,1)S(1)}, bf16[512,1536]{1,0:T(8,128)(2,1)S(1)}) custom-call(s32[10]{0:T(128)S(1)} %stack.52.scal, bf16[128,2048]{1,0:T(8,128)(2,1)S(1)} %get-tuple-element.42.refs_0_, bf16[128,2048]{1,0:T(8,128)(2,1)S(1)} %collective-permute-done.1.refs_1_, ...), custom_call_target="tpu_custom_call" | custom-call | flops 3221225472 | bytes 3221225 | tf_op jit(solution)/shard_map/pallas_call | solution.py:38
  63.5 3.9 %shard_map.101 = (bf16[4,128,1536]{2,1,0:T(8,128)(2,1)S(1)}, bf16[4,128,1536]{2,1,0:T(8,128)(2,1)S(1)}) custom-call(s32[10]{0:T(128)S(1)} %stack.52.scal, bf16[1024,512]{1,0:T(8,128)(2,1)S(1)} %get-tuple-element.70.rows_a, bf16[1024,512]{1,0:T(8,128)(2,1)S(1)} %get-tuple-element.71.rows_b, bf16[512,1536]{1,0:T(8,128)(2,1)S(1)} %get-tuple-element.60.pair_a, ...), custom_call_target="tpu_custom_call" | custom-call | flops 3221225472 | bytes 3221225 | tf_op jit(solution)/shard_map/pallas_call | solution.py:38
  67.5 0.1 collective-permute-start.15
  67.6 0.5 collective-permute-start.14
  68.1 4.0 %shard_map.99 = (bf16[256,1024]{1,0:T(8,128)(2,1)S(1)}, bf16[256,1024]{1,0:T(8,128)(2,1)S(1)}, bf16[256,1024]{1,0:T(8,128)(2,1)S(1)}, bf16[256,1024]{1,0:T(8,128)(2,1)S(1)}) custom-call(s32[10]{0:T(128)S(1)} %stack.52.scal, bf16[512,1536]{1,0:T(8,128)(2,1)S(1)} %get-tuple-element.60.pair_a, bf16[512,1536]{1,0:T(8,128)(2,1)S(1)} %get-tuple-element.61.pair_b, ...), custom_call_target="tpu_custom_call" | custom-call | flops 3221225472 | bytes 3221225 | tf_op jit(solution)/shard_map/pallas_call | solution.py:38
  72.1 0.7 copy-done.2
  72.9 0.2 copy-done.3
  73.1 0.2 copy-done.4
  73.2 2.2 %shard_map.102 = bf16[4,288,1024]{2,1,0:T(8,128)(2,1)} custom-call(s32[10]{0:T(128)S(1)} %stack.52.scal, bf16[4,96,1024]{2,1,0:T(8,128)(2,1)S(1)} %get-tuple-element.68.keep_down, bf16[4,96,1024]{2,1,0:T(8,128)(2,1)S(1)} %collective-permute-done.14.other_down, bf16[4,128,1536]{2,1,0:T(8,128)(2,1)S(1)} %get-tuple-element.72.refs_0_, ...), custom_call_target="tpu_custom_call" | custom-call | flops 1 | tf_op jit(solution)/shard_map/pallas_call | solution.py:38
  75.4 4.9 %all-to-all-start = ((bf16[4,288,1024]{2,1,0:T(8,128)(2,1)}), bf16[4,288,1024]{2,1,0:T(8,128)(2,1)S(1)}, u32[]{:S(2)}, u32[]{:S(2)}) async-start(bf16[4,288,1024]{2,1,0:T(8,128)(2,1)} %shard_map.102), calls=%async_computation | async-start | bytes 4718592 | tf_op jit(solution)/shard_map/all_to_all | solution.py:308
  80.3 1.3 collective-permute-start.10
  81.6 0.8 collective-permute-start.11
  82.4 1.4 %collective-permute-start.12 = (bf16[256,1024]{1,0:T(8,128)(2,1)}, bf16[256,1024]{1,0:T(8,128)(2,1)S(1)}, u32[]{:S(2)}, u32[]{:S(2)}) collective-permute-start(bf16[256,1024]{1,0:T(8,128)(2,1)} %copy-done.2), channel_id=1, source_target_pairs={{0,3},{1,2},{2,1},{3,0},{4,7},{5,6},{6,5},{7,4},{8,11},{9,10},{10,... | collective-permute-start | bytes 1572872 | tf_op jit(solution)/shard_map/ppermute | solution.py:227
  83.8 11.5 %collective-permute-done.10.refs_1_ = bf16[256,1024]{1,0:T(8,128)(2,1)S(1)} collective-permute-done((bf16[256,1024]{1,0:T(8,128)(2,1)}, bf16[256,1024]{1,0:T(8,128)(2,1)S(1)}, u32[]{:S(2)}, u32[]{:S(2)}) %collective-permute-start.10) | collective-permute-done | bytes 524320 | tf_op jit(solution)/shard_map/ppermute | solution.py:227
  95.3 9.5 %collective-permute-done.11.refs_2_ = bf16[256,1024]{1,0:T(8,128)(2,1)S(1)} collective-permute-done((bf16[256,1024]{1,0:T(8,128)(2,1)}, bf16[256,1024]{1,0:T(8,128)(2,1)S(1)}, u32[]{:S(2)}, u32[]{:S(2)}) %collective-permute-start.11) | collective-permute-done | bytes 524320 | tf_op jit(solution)/shard_map/ppermute | solution.py:227
  104.8 1.6 %collective-permute-done.12.refs_3_ = bf16[256,1024]{1,0:T(8,128)(2,1)S(1)} collective-permute-done((bf16[256,1024]{1,0:T(8,128)(2,1)}, bf16[256,1024]{1,0:T(8,128)(2,1)S(1)}, u32[]{:S(2)}, u32[]{:S(2)}) %collective-permute-start.12) | collective-permute-done | bytes 524320 | tf_op jit(solution)/shard_map/ppermute | solution.py:227
  106.4 1.3 shard_map.100
  107.7 1.8 %collective-permute-start.13 = (bf16[256,1024]{1,0:T(8,128)(2,1)S(1)}, bf16[256,1024]{1,0:T(8,128)(2,1)S(1)}, u32[]{:S(2)}, u32[]{:S(2)}) collective-permute-start(bf16[256,1024]{1,0:T(8,128)(2,1)S(1)} %get-tuple-element.67), channel_id=1, source_target_pairs={{0,8},{4,12},{8,0},{12,4},{16,24},{20,28},{24,16},{28,20},{1,9},{5... | collective-permute-start | bytes 1572872 | tf_op jit(solution)/shard_map/ppermute | solution.py:226
  109.5 20.4 %collective-permute-done.13 = bf16[256,1024]{1,0:T(8,128)(2,1)S(1)} collective-permute-done((bf16[256,1024]{1,0:T(8,128)(2,1)S(1)}, bf16[256,1024]{1,0:T(8,128)(2,1)S(1)}, u32[]{:S(2)}, u32[]{:S(2)}) %collective-permute-start.13) | collective-permute-done | bytes 524320 | tf_op jit(solution)/shard_map/ppermute | solution.py:226
  129.9 1.0 add_convert_fusion
  130.9 3.5 %all-to-all-done.terms = bf16[4,288,1024]{2,1,0:T(8,128)(2,1)S(1)} async-done(((bf16[4,288,1024]{2,1,0:T(8,128)(2,1)}), bf16[4,288,1024]{2,1,0:T(8,128)(2,1)S(1)}, u32[]{:S(2)}, u32[]{:S(2)}) %all-to-all-start) | async-done | bytes 2359328 | tf_op jit(solution)/shard_map/all_to_all | solution.py:308
  134.4 2.1 %shard_map.103 = (f32[2,128,1536]{2,1,0:T(8,128)}, f32[2,96,1024]{2,1,0:T(8,128)}) custom-call(s32[10]{0:T(128)S(1)} %stack.52.scal, bf16[4,288,1024]{2,1,0:T(8,128)(2,1)S(1)} %all-to-all-done.terms), custom_call_target="tpu_custom_call" | custom-call | flops 1 | tf_op jit(solution)/shard_map/pallas_call | solution.py:38
  (24 shorter events, 0.1 us)
Async XLA Ops:
  2.9 48.3 %slice-start = ((s8[6291456]{0:T(1024)(128)(4,1)}), s8[2097152]{0:T(1024)(128)(4,1)S(1)}, s32[]{:S(2)}) async-start(s8[6291456]{0:T(1024)(128)(4,1)} %bitcast.11), calls=%async_computation.1 | async-start | bytes 4194304
  4.3 27.1 %collective-permute-start = (bf16[528,1024]{1,0:T(8,128)(2,1)S(1)}, bf16[528,1024]{1,0:T(8,128)(2,1)}, u32[]{:S(2)}, u32[]{:S(2)}) collective-permute-start(bf16[528,1024]{1,0:T(8,128)(2,1)S(1)} %pad_maximum_fusion.block), channel_id=1, source_target_pairs={{0,8},{4,12},{8,0},{12,4},{16,24},{20,28},{24,16},{28,20},{1,9},{5... | collective-permute-start | bytes 3244040 | tf_op jit(solution)/shard_map/ppermute | solution.py:226
  8.8 28.3 %collective-permute-start.1 = (bf16[128,2048]{1,0:T(8,128)(2,1)S(1)}, bf16[128,2048]{1,0:T(8,128)(2,1)S(1)}, u32[]{:S(2)}, u32[]{:S(2)}) collective-permute-start(bf16[128,2048]{1,0:T(8,128)(2,1)S(1)} %get-tuple-element.43), channel_id=1, source_target_pairs={{0,1},{1,0},{2,3},{3,2},{4,5},{5,4},{6,7},{7,6},{8,9},{9,8},{10,11... | collective-permute-start | bytes 1572872 | tf_op jit(solution)/shard_map/ppermute | solution.py:227
  10.4 27.1 %collective-permute-start.2 = (bf16[128,2048]{1,0:T(8,128)(2,1)S(1)}, bf16[128,2048]{1,0:T(8,128)(2,1)S(1)}, u32[]{:S(2)}, u32[]{:S(2)}) collective-permute-start(bf16[128,2048]{1,0:T(8,128)(2,1)S(1)} %get-tuple-element.44), channel_id=1, source_target_pairs={{0,2},{1,3},{2,0},{3,1},{4,6},{5,7},{6,4},{7,5},{8,10},{9,11},{10,... | collective-permute-start | bytes 1572872 | tf_op jit(solution)/shard_map/ppermute | solution.py:227
  11.9 27.3 %collective-permute-start.3 = (bf16[128,2048]{1,0:T(8,128)(2,1)S(1)}, bf16[128,2048]{1,0:T(8,128)(2,1)S(1)}, u32[]{:S(2)}, u32[]{:S(2)}) collective-permute-start(bf16[128,2048]{1,0:T(8,128)(2,1)S(1)} %get-tuple-element.45), channel_id=1, source_target_pairs={{0,3},{1,2},{2,1},{3,0},{4,7},{5,6},{6,5},{7,4},{8,11},{9,10},{10,... | collective-permute-start | bytes 1572872 | tf_op jit(solution)/shard_map/ppermute | solution.py:227
  33.9 9.3 %collective-permute-start.7 = (bf16[128,1024]{1,0:T(8,128)(2,1)S(1)}, bf16[128,1024]{1,0:T(8,128)(2,1)S(1)}, u32[]{:S(2)}, u32[]{:S(2)}) collective-permute-start(bf16[128,1024]{1,0:T(8,128)(2,1)S(1)} %get-tuple-element.52), channel_id=1, source_target_pairs={{0,1},{1,0},{2,3},{3,2},{4,5},{5,4},{6,7},{7,6},{8,9},{9,8},{10,11... | collective-permute-start | bytes 786440 | tf_op jit(solution)/shard_map/ppermute | solution.py:227
  35.6 15.5 %collective-permute-start.8 = (bf16[128,1024]{1,0:T(8,128)(2,1)S(1)}, bf16[128,1024]{1,0:T(8,128)(2,1)S(1)}, u32[]{:S(2)}, u32[]{:S(2)}) collective-permute-start(bf16[128,1024]{1,0:T(8,128)(2,1)S(1)} %get-tuple-element.53), channel_id=1, source_target_pairs={{0,2},{1,3},{2,0},{3,1},{4,6},{5,7},{6,4},{7,5},{8,10},{9,11},{10,... | collective-permute-start | bytes 786440 | tf_op jit(solution)/shard_map/ppermute | solution.py:227
  37.2 14.0 %collective-permute-start.9 = (bf16[128,1024]{1,0:T(8,128)(2,1)S(1)}, bf16[128,1024]{1,0:T(8,128)(2,1)S(1)}, u32[]{:S(2)}, u32[]{:S(2)}) collective-permute-start(bf16[128,1024]{1,0:T(8,128)(2,1)S(1)} %get-tuple-element.54), channel_id=1, source_target_pairs={{0,3},{1,2},{2,1},{3,0},{4,7},{5,6},{6,5},{7,4},{8,11},{9,10},{10,... | collective-permute-start | bytes 786440 | tf_op jit(solution)/shard_map/ppermute | solution.py:227
  37.5 17.0 %collective-permute-start.4 = (bf16[128,1024]{1,0:T(8,128)(2,1)S(1)}, bf16[128,1024]{1,0:T(8,128)(2,1)S(1)}, u32[]{:S(2)}, u32[]{:S(2)}) collective-permute-start(bf16[128,1024]{1,0:T(8,128)(2,1)S(1)} %get-tuple-element.47), channel_id=1, source_target_pairs={{0,1},{1,0},{2,3},{3,2},{4,5},{5,4},{6,7},{7,6},{8,9},{9,8},{10,11... | collective-permute-start | bytes 786440 | tf_op jit(solution)/shard_map/ppermute | solution.py:227
  39.1 20.3 %collective-permute-start.5 = (bf16[128,1024]{1,0:T(8,128)(2,1)S(1)}, bf16[128,1024]{1,0:T(8,128)(2,1)S(1)}, u32[]{:S(2)}, u32[]{:S(2)}) collective-permute-start(bf16[128,1024]{1,0:T(8,128)(2,1)S(1)} %get-tuple-element.48), channel_id=1, source_target_pairs={{0,2},{1,3},{2,0},{3,1},{4,6},{5,7},{6,4},{7,5},{8,10},{9,11},{10,... | collective-permute-start | bytes 786440 | tf_op jit(solution)/shard_map/ppermute | solution.py:227
  43.2 16.2 %collective-permute-start.6 = (bf16[128,1024]{1,0:T(8,128)(2,1)S(1)}, bf16[128,1024]{1,0:T(8,128)(2,1)S(1)}, u32[]{:S(2)}, u32[]{:S(2)}) collective-permute-start(bf16[128,1024]{1,0:T(8,128)(2,1)S(1)} %get-tuple-element.49), channel_id=1, source_target_pairs={{0,3},{1,2},{2,1},{3,0},{4,7},{5,6},{6,5},{7,4},{8,11},{9,10},{10,... | collective-permute-start | bytes 786440 | tf_op jit(solution)/shard_map/ppermute | solution.py:227
  45.8 2.8 %copy-start = (bf16[2,1024,1536]{2,1,0:T(8,128)(2,1)S(1)}, bf16[2,1024,1536]{2,1,0:T(8,128)(2,1)}, u32[]{:S(2)}) copy-start(bf16[2,1024,1536]{2,1,0:T(8,128)(2,1)} %w_in.1) | copy-start | bytes 18874372
  48.6 2.6 %slice-start.1 = ((s8[6291456]{0:T(1024)(128)(4,1)}), s8[4194304]{0:T(1024)(128)(4,1)S(1)}, s32[]{:S(2)}) async-start(s8[6291456]{0:T(1024)(128)(4,1)} %bitcast.11), calls=%async_computation.2 | async-start | bytes 8388608
  51.2 8.2 %copy-start.1 = (bf16[2,768,1024]{2,1,0:T(8,128)(2,1)S(1)}, bf16[2,768,1024]{2,1,0:T(8,128)(2,1)}, u32[]{:S(2)}) copy-start(bf16[2,768,1024]{2,1,0:T(8,128)(2,1)} %refs_8_.1) | copy-start | bytes 9437188
  67.5 4.6 %collective-permute-start.15 = (bf16[4,128,1536]{2,1,0:T(8,128)(2,1)S(1)}, bf16[4,128,1536]{2,1,0:T(8,128)(2,1)S(1)}, u32[]{:S(2)}, u32[]{:S(2)}) collective-permute-start(bf16[4,128,1536]{2,1,0:T(8,128)(2,1)S(1)} %get-tuple-element.73), channel_id=1, source_target_pairs={{0,4},{4,0},{8,12},{12,8},{16,20},{20,16},{24,28},{28,24},{1,5},{5... | collective-permute-start | bytes 4718600 | tf_op jit(solution)/shard_map/ppermute | solution.py:225
  67.6 4.6 %collective-permute-start.14 = (bf16[4,96,1024]{2,1,0:T(8,128)(2,1)S(1)}, bf16[4,96,1024]{2,1,0:T(8,128)(2,1)S(1)}, u32[]{:S(2)}, u32[]{:S(2)}) collective-permute-start(bf16[4,96,1024]{2,1,0:T(8,128)(2,1)S(1)} %get-tuple-element.69), channel_id=1, source_target_pairs={{0,4},{4,0},{8,12},{12,8},{16,20},{20,16},{24,28},{28,24},{1,5},{5... | collective-permute-start | bytes 2359304 | tf_op jit(solution)/shard_map/ppermute | solution.py:225
  72.1 0.8 copy-start.2
  72.1 1.0 copy-start.3
  72.1 1.1 copy-start.4
  75.4 58.9 %all-to-all-start = ((bf16[4,288,1024]{2,1,0:T(8,128)(2,1)}), bf16[4,288,1024]{2,1,0:T(8,128)(2,1)S(1)}, u32[]{:S(2)}, u32[]{:S(2)}) async-start(bf16[4,288,1024]{2,1,0:T(8,128)(2,1)} %shard_map.102), calls=%async_computation | async-start | bytes 4718592 | tf_op jit(solution)/shard_map/all_to_all | solution.py:308
  80.3 15.0 %collective-permute-start.10 = (bf16[256,1024]{1,0:T(8,128)(2,1)}, bf16[256,1024]{1,0:T(8,128)(2,1)S(1)}, u32[]{:S(2)}, u32[]{:S(2)}) collective-permute-start(bf16[256,1024]{1,0:T(8,128)(2,1)} %copy-done.4), channel_id=1, source_target_pairs={{0,1},{1,0},{2,3},{3,2},{4,5},{5,4},{6,7},{7,6},{8,9},{9,8},{10,11... | collective-permute-start | bytes 1572872 | tf_op jit(solution)/shard_map/ppermute | solution.py:227
  81.6 23.2 %collective-permute-start.11 = (bf16[256,1024]{1,0:T(8,128)(2,1)}, bf16[256,1024]{1,0:T(8,128)(2,1)S(1)}, u32[]{:S(2)}, u32[]{:S(2)}) collective-permute-start(bf16[256,1024]{1,0:T(8,128)(2,1)} %copy-done.3), channel_id=1, source_target_pairs={{0,2},{1,3},{2,0},{3,1},{4,6},{5,7},{6,4},{7,5},{8,10},{9,11},{10,... | collective-permute-start | bytes 1572872 | tf_op jit(solution)/shard_map/ppermute | solution.py:227
  82.4 24.0 %collective-permute-start.12 = (bf16[256,1024]{1,0:T(8,128)(2,1)}, bf16[256,1024]{1,0:T(8,128)(2,1)S(1)}, u32[]{:S(2)}, u32[]{:S(2)}) collective-permute-start(bf16[256,1024]{1,0:T(8,128)(2,1)} %copy-done.2), channel_id=1, source_target_pairs={{0,3},{1,2},{2,1},{3,0},{4,7},{5,6},{6,5},{7,4},{8,11},{9,10},{10,... | collective-permute-start | bytes 1572872 | tf_op jit(solution)/shard_map/ppermute | solution.py:227
  107.7 22.3 %collective-permute-start.13 = (bf16[256,1024]{1,0:T(8,128)(2,1)S(1)}, bf16[256,1024]{1,0:T(8,128)(2,1)S(1)}, u32[]{:S(2)}, u32[]{:S(2)}) collective-permute-start(bf16[256,1024]{1,0:T(8,128)(2,1)S(1)} %get-tuple-element.67), channel_id=1, source_target_pairs={{0,8},{4,12},{8,0},{12,4},{16,24},{20,28},{24,16},{28,20},{1,9},{5... | collective-permute-start | bytes 1572872 | tf_op jit(solution)/shard_map/ppermute | solution.py:226

commit v4 on v3

--- a/solution.py
+++ b/solution.py
@@ -53,6 +53,10 @@
     return jnp.concatenate([ref[:, pl.ds(column, columns)] for ref in refs], axis=0)
 
 
+def in_hbm(value):
+    return pltpu.with_memory_space_constraint(value, pltpu.HBM)
+
+
 def after(value, *others):
     return lax.optimization_barrier((value, *others))[0]
 
@@ -60,36 +64,19 @@
 ROUTE_ROWS = 16
 
 
-def route_rows(route_logits, expert_ids, slot_pos, width):
-    share = jax.nn.sigmoid(route_logits[:, 0] - route_logits[:, 1])
-    high = lax.reduce_precision(share, 8, 7)
-    middle = lax.reduce_precision(share - high, 8, 7)
-    low = share - high - middle
-    places = jnp.concatenate(
-        [x.astype(BF) for x in (expert_ids[:, 0], expert_ids[:, 1], slot_pos[:, 0], slot_pos[:, 1])]
-    )
-    shares = jnp.concatenate([x.astype(BF) for x in (high, middle, low)])
-    rows = [jnp.pad(x, (0, width - x.shape[0])) for x in (places, shares)]
-    return jnp.pad(jnp.stack(rows), ((0, ROUTE_ROWS - 2), (0, 0)))
-
-
-def slots_body(cap, n, scal, block, *refs):
-    outs, back = refs[:-1], refs[-1]
-    tokens = back.shape[0]
-    route = block[0:2, :].astype(F32)
-    row = lambda r, k: route[r : r + 1, k * tokens : (k + 1) * tokens]
-    slot = lax.broadcasted_iota(jnp.int32, (cap, tokens), 0)
+def fill_slots(cap, n, scal, route, tokens, cotangent, outs, back):
+    chosen, places, share = route
+    slot = lax.broadcasted_iota(jnp.int32, (cap, back.shape[0]), 0)
     slot = jnp.concatenate([slot + scal[2 + j] for j in range(n)], axis=0).astype(F32)
-    first = slot == row(0, 0) * cap + row(0, 2)
-    second = slot == row(0, 1) * cap + row(0, 3)
-    share = row(1, 0) + row(1, 1) + row(1, 2)
+    first = slot == chosen[0] * cap + places[0]
+    second = slot == chosen[1] * cap + places[1]
     hit = jnp.where(jnp.logical_or(first, second), 1.0, 0.0)
     factor = jnp.where(first, share, 0.0) + jnp.where(second, 1.0 - share, 0.0)
     factor = jnp.sum(factor, axis=1, keepdims=True)
     back[...] = jnp.transpose(hit).astype(BF)
     hit = hit.astype(BF)
-    rows = dot(hit, block[pl.ds(ROUTE_ROWS, tokens), :]).astype(BF)
-    scaled = (dot(hit, block[pl.ds(ROUTE_ROWS + tokens, tokens), :]) * factor).astype(BF)
+    rows = dot(hit, tokens).astype(BF)
+    scaled = (dot(hit, cotangent) * factor).astype(BF)
     rows = jnp.concatenate([rows, scaled], axis=1)
     column = 0
     for k in range(0, len(outs), n):
@@ -97,6 +84,39 @@
         for j in range(n):
             outs[k + j][...] = rows[j * cap : (j + 1) * cap, column : column + columns]
         column += columns
+
+
+def own_slots_body(cap, n, scal, logits, experts, places, tokens, cotangent, *refs):
+    outs, back, block = refs[:-2], refs[-2], refs[-1]
+    count, width = tokens.shape
+    share = jax.nn.sigmoid(logits[0:1, :] - logits[1:2, :])
+    high = share.astype(BF)
+    middle = (share - high.astype(F32)).astype(BF)
+    low = (share - high.astype(F32) - middle.astype(F32)).astype(BF)
+    chosen = experts[...].astype(F32)
+    slots = places[...].astype(F32)
+    rows = [x.astype(BF).astype(F32) for x in (chosen[0:1], chosen[1:2], slots[0:1], slots[1:2])]
+    shares = [x.astype(F32) for x in (high, middle, low)]
+    shares.append(jnp.zeros_like(share))
+    pad = [jnp.zeros((1, width - 4 * count), F32)] if width > 4 * count else []
+    head = [jnp.concatenate(x + pad, axis=1) for x in (rows, shares)]
+    head.append(jnp.zeros((ROUTE_ROWS - 2, width), F32))
+    block[pl.ds(0, ROUTE_ROWS), :] = jnp.concatenate(head, axis=0).astype(BF)
+    block[pl.ds(ROUTE_ROWS, count), :] = tokens[...]
+    block[pl.ds(ROUTE_ROWS + count, count), :] = cotangent[...]
+    route = ((chosen[0:1], chosen[1:2]), (slots[0:1], slots[1:2]), share)
+    fill_slots(cap, n, scal, route, tokens[...], cotangent[...], outs, back)
+
+
+def beside_slots_body(cap, n, scal, block, *refs):
+    outs, back = refs[:-1], refs[-1]
+    count = back.shape[0]
+    head = block[0:2, :].astype(F32)
+    row = lambda r, k: head[r : r + 1, k * count : (k + 1) * count]
+    share = row(1, 0) + row(1, 1) + row(1, 2)
+    route = ((row(0, 0), row(0, 1)), (row(0, 2), row(0, 3)), share)
+    tokens = block[pl.ds(ROUTE_ROWS, count), :]
+    fill_slots(cap, n, scal, route, tokens, block[pl.ds(ROUTE_ROWS + count, count), :], outs, back)
 
 
 def forward_body(tile, scal, *refs):
@@ -123,13 +143,16 @@
     return jnp.concatenate(taken, axis=0)
 
 
+def pair_body(column, scal, *refs):
+    *arrived, w_down, scale_gate, scale_up, pair = refs
+    grad_hidden = dot_nt(stack_rows(arrived, column, w_down.shape[2]), w_down[0])
+    ff = scale_gate.shape[1]
+    pair[:, pl.ds(0, ff)] = (grad_hidden * scale_gate[...].astype(F32)).astype(BF)
+    pair[:, pl.ds(ff, ff)] = (grad_hidden * scale_up[...].astype(F32)).astype(BF)
+
+
 def down_body(n, nz, scal, *refs):
-    arrived, (w_down, hidden_a, hidden_b, *scales), outs = (
-        refs[: 2 * n],
-        refs[2 * n : 2 * n + 7],
-        refs[2 * n + 7 :],
-    )
-    give, keep, *pairs = outs
+    arrived, (hidden_a, hidden_b, give, keep) = refs[: 2 * n], refs[2 * n :]
     part, width = give.shape[1:]
     slots = [stack_rows(arrived[:n], width, width), stack_rows(arrived[n:], 0, width)]
     left = shard_rows((hidden_a, hidden_b), scal, nz, part)
@@ -137,12 +160,6 @@
     for k in range(nz):
         give[k] = result[k * part : (k + 1) * part]
         keep[k] = result[(nz + k) * part : (nz + k + 1) * part]
-    for g in range(2):
-        grad_hidden = dot_nt(slots[g], w_down[0])
-        scale_gate, scale_up = scales[2 * g : 2 * g + 2]
-        ff = scale_gate.shape[1]
-        pairs[g][:, pl.ds(0, ff)] = (grad_hidden * scale_gate[...].astype(F32)).astype(BF)
-        pairs[g][:, pl.ds(ff, ff)] = (grad_hidden * scale_up[...].astype(F32)).astype(BF)
 
 
 def input_weight_body(first, nz, scal, rows_a, rows_b, pair_a, pair_b, give, keep):
@@ -192,18 +209,15 @@
             ]
 
 
-def returned_body(cap, scal, pair_a, pair_b, w_in, *outs):
-    for g, pair in enumerate((pair_a, pair_b)):
-        returned = dot_nt(pair[...], w_in[0]).astype(BF)
-        for j, out in enumerate(outs):
-            out[pl.ds(g * cap, cap), :] = returned[j * cap : (j + 1) * cap]
-
-
-def combine_body(cap, scal, back_a, back_b, *refs):
-    arrived, outs = refs[:-2], refs[-2:]
-    for g, (back, out) in enumerate(zip((back_a, back_b), outs)):
-        rows = jnp.concatenate([x[pl.ds(g * cap, cap), :] for x in arrived], axis=0)
-        out[...] = dot(back[...], rows).astype(BF)
+def returned_body(cap, scal, pair, w_in, *outs):
+    returned = dot_nt(pair[...], w_in[0]).astype(BF)
+    for j, out in enumerate(outs):
+        out[...] = returned[j * cap : (j + 1) * cap]
+
+
+def combine_body(scal, back, *refs):
+    *arrived, out = refs
+    out[...] = dot(back[...], stack_rows(arrived, 0, out.shape[1])).astype(BF)
 
 
 def per_device(tokens, cotangent, route_logits, expert_ids, slot_pos, w_in, w_down):
@@ -228,22 +242,26 @@
     same_core = [list(range(c, ndp, 2)) for c in range(2)]
     macs = 2 * slots * width * ff
 
-    block = jnp.concatenate(
-        [route_rows(route_logits, expert_ids, slot_pos, width), tokens, cotangent], axis=0
-    )
-    messages = ([2 * width], [width, width])
-    arrived, backs = [], []
-    for parts, block in zip(messages, (block, along_z(block, 1))):
-        *sent, back = call(
-            functools.partial(slots_body, cap, n),
-            [bf(cap, c) for c in parts for _ in range(n)] + [bf(token_count, slots)],
-            macs // 4,
-            LIMITS[0],
-            scal,
-            block,
-        )
-        arrived.append([across(x, k % n) for k, x in enumerate(sent)])
-        backs.append(back)
+    count = token_count
+    *sent, back, block = call(
+        functools.partial(own_slots_body, cap, n),
+        [bf(cap, 2 * width)] * n + [bf(count, slots), bf(ROUTE_ROWS + 2 * count, width)],
+        macs // 4,
+        LIMITS[0],
+        scal,
+        *[in_hbm(x) for x in (route_logits.T, expert_ids.T, slot_pos.T, tokens, cotangent)],
+    )
+    arrived = [[across(x, j) for j, x in enumerate(sent)]]
+    *sent, back_beside = call(
+        functools.partial(beside_slots_body, cap, n),
+        [bf(cap, width)] * (2 * n) + [bf(count, slots)],
+        macs // 4,
+        LIMITS[0],
+        scal,
+        along_z(block, 1),
+    )
+    arrived.append([across(x, k % n) for k, x in enumerate(sent)])
+    backs = [back, back_beside]
 
     forwards = []
     for g in range(2):
@@ -262,21 +280,22 @@
         )
     (rows_a, hidden_a, *scales_a), (rows_b, hidden_b, *scales_b) = forwards
 
-    args = arrived[0] + arrived[1][n:] + [w_down, hidden_a, hidden_b] + scales_a + scales_b
-    specs = [whole(x) for x in args]
-    specs[2 * n] = of_expert(w_down)
-    give, keep, *pairs = call(
-        functools.partial(down_body, n, nz),
-        [bf(nz, ff // ndp, width)] * 2 + [bf(slots, 2 * ff)] * 2,
-        4 * macs,
-        LIMITS[2],
-        scal,
-        *args,
-        specs=specs,
-    )
-    terms = [keep, swap_core(give)]
+    pairs = []
+    for g, (column, scales) in enumerate(((width, scales_a), (0, scales_b))):
+        pieces = arrived[g][-n:]
+        args = pieces + [w_down] + scales
+        pairs += call(
+            functools.partial(pair_body, column),
+            [bf(slots, 2 * ff)],
+            macs,
+            LIMITS[2],
+            scal,
+            *args,
+            specs=[whole(x) for x in pieces] + [of_expert(w_down)] + [whole(x) for x in scales],
+        )
 
     columns = 2 * ff // IN_PARTS
+    terms = []
     for k in range(IN_PARTS):
         give, keep = call(
             functools.partial(input_weight_body, k * columns, nz),
@@ -289,18 +308,31 @@
             *pairs,
         )
         terms += [keep, swap_core(give)]
-    sent = call(
-        functools.partial(returned_body, cap),
-        [bf(2 * cap, width)] * n,
-        4 * macs,
-        LIMITS[4],
+    give, keep = call(
+        functools.partial(down_body, n, nz),
+        [bf(nz, ff // ndp, width)] * 2,
+        2 * macs,
+        LIMITS[2],
         scal,
-        pairs[0],
-        pairs[1],
-        w_in,
-        specs=[whole(x) for x in pairs] + [of_expert(w_in)],
-    )
-    terms[-1] = after(terms[-1], *sent)
+        *arrived[0],
+        *arrived[1][n:],
+        hidden_a,
+        hidden_b,
+    )
+    terms = [keep, swap_core(give)] + terms
+    returned = [
+        call(
+            functools.partial(returned_body, cap),
+            [bf(cap, width)] * n,
+            2 * macs,
+            LIMITS[4],
+            scal,
+            pair,
+            w_in,
+            specs=[whole(pair), of_expert(w_in)],
+        )
+        for pair in pairs
+    ]
     rows = ff // ndp + width // ndp * 2 * ff // width
     (total,) = call(
         functools.partial(pack_body, nz), [bf(nz, rows, width)], 1, LIMITS[6], scal, *terms
@@ -318,15 +350,11 @@
         scal,
         total,
     )
-    mine_sum, beside_sum = call(
-        functools.partial(combine_body, cap),
-        [bf(token_count, width)] * 2,
-        macs // 4,
-        LIMITS[5],
-        scal,
-        *backs,
-        *[across(x, j) for j, x in enumerate(sent)],
-    )
+    sums = []
+    for sent, back in zip(returned, backs):
+        arrived = [across(x, j) for j, x in enumerate(sent)]
+        sums += call(combine_body, [bf(count, width)], macs // 8, LIMITS[5], scal, back, *arrived)
+    mine_sum, beside_sum = sums
     input_grad = (mine_sum.astype(F32) + along_z(beside_sum, 1).astype(F32)).astype(BF)
     return (input_grad, grad_in, grad_down)
 

time: 137 us -> 131 us (0.956)
  waiting for transfers between devices: 73.8 us -> 61.8 us
  other arithmetic: 4.6 us -> 0.99 us
  starting transfers between devices: 26.7 us -> 30.3 us
  local copies, waits for them, and re-layouts: 4.02 us -> 7.61 us
  Pallas kernels: 26.5 us -> 29.4 us
    ppermute x2, waiting for transfers between devices: 39.5 us -> 29.7 us  [per_device(): lax.ppermute(x, 'dp', [(i, i ^ 2 * k) for i in range(ndp)])]
    ppermute x12 -> x15, waiting for transfers between devices: 30.8 us -> 26.7 us  [per_device(): lax.ppermute(x, 'expert', [(i, i ^ j) for i in range(n)])]
    unnamed x14 -> x18, local copies, waits for them, and re-layouts: 3.9 us -> 7.52 us
    ppermute x12 -> x15, starting transfers between devices: 16.4 us -> 19.9 us  [per_device(): lax.ppermute(x, 'expert', [(i, i ^ j) for i in range(n)])]
    pallas_call x10 -> x14, Pallas kernels: 26.5 us -> 29.4 us  [call(): pl.pallas_call(body, out_shape=out_shape, grid_spec=pltpu.PrefetchScalarG...]
    ppermute x2, waiting for transfers between devices: 0.01 us -> 1.91 us  [per_device(): lax.ppermute(x, 'dp', [(i, i ^ 1) for i in range(ndp)])]
    concatenate x3 -> x0, other arithmetic: 1.45 us -> none  [the longest x1 1.43 us: per_device(): jnp.concatenate([route_rows(route_logits, expert_ids, slot_pos, width), t...]
    another operation x3 -> x0, other arithmetic: 1.39 us -> none
  transfers between devices with their start and end apart: 17 -> 20, of which waited for: 9 -> 11; matrix products, arithmetic and copies ran while one was open for 1% -> 1% of each run, Pallas kernels for 10% -> 13%
where the time goes in v4:
time: 131 us
  waiting for transfers between devices  61.8 us (47%)
  starting transfers between devices  30.3 us (23%)
  Pallas kernels  29.4 us (22%)
  local copies, waits for them, and re-layouts  7.61 us (6%)
    ppermute x2, waiting for transfers between devices, per_device(): lax.ppermute(x, 'dp', [(i, i ^ 2 * k) for i in range(ndp)])  29.7 us
    pallas_call x14, Pallas kernels, call(): pl.pallas_call(body, out_shape=out_shape, grid_spec=pltpu.PrefetchScalarG...  29.4 us
    ppermute x15, waiting for transfers between devices, per_device(): lax.ppermute(x, 'expert', [(i, i ^ j) for i in range(n)])  26.7 us
    ppermute x15, starting transfers between devices, per_device(): lax.ppermute(x, 'expert', [(i, i ^ j) for i in range(n)])  19.9 us
    unnamed x18, local copies, waits for them, and re-layouts  7.52 us
    ppermute x2, starting transfers between devices, per_device(): lax.ppermute(x, 'dp', [(i, i ^ 2 * k) for i in range(ndp)])  4.89 us
    all_to_all x1, starting transfers between devices, per_device(): lax.all_to_all(total, 'dp', 0, 0, tiled=True, axis_index_groups=same_core)  4.89 us
    all_to_all x1, waiting for transfers between devices, per_device(): lax.all_to_all(total, 'dp', 0, 0, tiled=True, axis_index_groups=same_core)  3.47 us
  transfers between devices with their start and end apart: 20, of which 11 were waited for; matrix products, arithmetic and copies ran while one was open for 1% of the time, Pallas kernels for 13%

profile of v4, /device:TPU:0, one launch (start us, length us, event | category | flops | bytes accessed | tf_op | source)
XLA Modules:
  0.0 131.0 jit_solution(6762992687397983640)
XLA Ops:
  0.7 2.6 %shard_map.94 = (bf16[128,2048]{1,0:T(8,128)(2,1)S(1)}, bf16[128,2048]{1,0:T(8,128)(2,1)S(1)}, bf16[128,2048]{1,0:T(8,128)(2,1)S(1)}, bf16[128,2048]{1,0:T(8,128...) custom-call(s32[10]{0:T(128)S(1)} %stack.43.scal, f32[2,256]{1,0:T(2,128)} %bitcast.15, ...), custom_call_target="tpu_custom_call" | custom-call | flops 201326592 | bytes 201326 | tf_op jit(solution)/shard_map/pallas_call | solution.py:38
  3.3 3.1 %collective-permute-start.6 = (bf16[528,1024]{1,0:T(8,128)(2,1)S(1)}, bf16[528,1024]{1,0:T(8,128)(2,1)S(1)}, u32[]{:S(2)}, u32[]{:S(2)}) collective-permute-start(bf16[528,1024]{1,0:T(8,128)(2,1)S(1)} %get-tuple-element.51), channel_id=1, source_target_pairs={{0,8},{4,12},{8,0},{12,4},{16,24},{20,28},{24,16},{28,20},{1,9},{5... | collective-permute-start | bytes 3244040 | tf_op jit(solution)/shard_map/ppermute | solution.py:240
  6.4 1.5 %collective-permute-start = (bf16[128,2048]{1,0:T(8,128)(2,1)S(1)}, bf16[128,2048]{1,0:T(8,128)(2,1)S(1)}, u32[]{:S(2)}, u32[]{:S(2)}) collective-permute-start(bf16[128,2048]{1,0:T(8,128)(2,1)S(1)} %get-tuple-element.42), channel_id=1, source_target_pairs={{0,1},{1,0},{2,3},{3,2},{4,5},{5,4},{6,7},{7,6},{8,9},{9,8},{10,11... | collective-permute-start | bytes 1572872 | tf_op jit(solution)/shard_map/ppermute | solution.py:241
  7.9 1.5 %collective-permute-start.1 = (bf16[128,2048]{1,0:T(8,128)(2,1)S(1)}, bf16[128,2048]{1,0:T(8,128)(2,1)S(1)}, u32[]{:S(2)}, u32[]{:S(2)}) collective-permute-start(bf16[128,2048]{1,0:T(8,128)(2,1)S(1)} %get-tuple-element.43), channel_id=1, source_target_pairs={{0,2},{1,3},{2,0},{3,1},{4,6},{5,7},{6,4},{7,5},{8,10},{9,11},{10,... | collective-permute-start | bytes 1572872 | tf_op jit(solution)/shard_map/ppermute | solution.py:241
  9.4 0.5 collective-permute-start.2
  9.9 20.4 %collective-permute-done.6.block = bf16[528,1024]{1,0:T(8,128)(2,1)S(1)} collective-permute-done((bf16[528,1024]{1,0:T(8,128)(2,1)S(1)}, bf16[528,1024]{1,0:T(8,128)(2,1)S(1)}, u32[]{:S(2)}, u32[]{:S(2)}) %collective-permute-start.6) | collective-permute-done | bytes 1081376 | tf_op jit(solution)/shard_map/ppermute | solution.py:240
  30.3 1.3 shard_map.99
  31.6 1.7 %collective-permute-start.10 = (bf16[128,1024]{1,0:T(8,128)(2,1)S(1)}, bf16[128,1024]{1,0:T(8,128)(2,1)S(1)}, u32[]{:S(2)}, u32[]{:S(2)}) collective-permute-start(bf16[128,1024]{1,0:T(8,128)(2,1)S(1)} %get-tuple-element.58), channel_id=1, source_target_pairs={{0,1},{1,0},{2,3},{3,2},{4,5},{5,4},{6,7},{7,6},{8,9},{9,8},{10,11... | collective-permute-start | bytes 786440 | tf_op jit(solution)/shard_map/ppermute | solution.py:241
  33.3 1.5 %collective-permute-start.11 = (bf16[128,1024]{1,0:T(8,128)(2,1)S(1)}, bf16[128,1024]{1,0:T(8,128)(2,1)S(1)}, u32[]{:S(2)}, u32[]{:S(2)}) collective-permute-start(bf16[128,1024]{1,0:T(8,128)(2,1)S(1)} %get-tuple-element.59), channel_id=1, source_target_pairs={{0,2},{1,3},{2,0},{3,1},{4,6},{5,7},{6,4},{7,5},{8,10},{9,11},{10,... | collective-permute-start | bytes 786440 | tf_op jit(solution)/shard_map/ppermute | solution.py:241
  35.1 1.7 %collective-permute-start.7 = (bf16[128,1024]{1,0:T(8,128)(2,1)S(1)}, bf16[128,1024]{1,0:T(8,128)(2,1)S(1)}, u32[]{:S(2)}, u32[]{:S(2)}) collective-permute-start(bf16[128,1024]{1,0:T(8,128)(2,1)S(1)} %get-tuple-element.54), channel_id=1, source_target_pairs={{0,1},{1,0},{2,3},{3,2},{4,5},{5,4},{6,7},{7,6},{8,9},{9,8},{10,11... | collective-permute-start | bytes 786440 | tf_op jit(solution)/shard_map/ppermute | solution.py:241
  36.8 1.5 %collective-permute-start.8 = (bf16[128,1024]{1,0:T(8,128)(2,1)S(1)}, bf16[128,1024]{1,0:T(8,128)(2,1)S(1)}, u32[]{:S(2)}, u32[]{:S(2)}) collective-permute-start(bf16[128,1024]{1,0:T(8,128)(2,1)S(1)} %get-tuple-element.55), channel_id=1, source_target_pairs={{0,2},{1,3},{2,0},{3,1},{4,6},{5,7},{6,4},{7,5},{8,10},{9,11},{10,... | collective-permute-start | bytes 786440 | tf_op jit(solution)/shard_map/ppermute | solution.py:241
  38.3 2.6 %collective-permute-done.10.refs_1_ = bf16[128,1024]{1,0:T(8,128)(2,1)S(1)} collective-permute-done((bf16[128,1024]{1,0:T(8,128)(2,1)S(1)}, bf16[128,1024]{1,0:T(8,128)(2,1)S(1)}, u32[]{:S(2)}, u32[]{:S(2)}) %collective-permute-start.10) | collective-permute-done | bytes 262176 | tf_op jit(solution)/shard_map/ppermute | solution.py:241
  40.9 2.6 %collective-permute-start.9 = (bf16[128,1024]{1,0:T(8,128)(2,1)S(1)}, bf16[128,1024]{1,0:T(8,128)(2,1)S(1)}, u32[]{:S(2)}, u32[]{:S(2)}) collective-permute-start(bf16[128,1024]{1,0:T(8,128)(2,1)S(1)} %get-tuple-element.56), channel_id=1, source_target_pairs={{0,3},{1,2},{2,1},{3,0},{4,7},{5,6},{6,5},{7,4},{8,11},{9,10},{10,... | collective-permute-start | bytes 786440 | tf_op jit(solution)/shard_map/ppermute | solution.py:241
  43.5 2.8 %copy-done = bf16[2,1024,1536]{2,1,0:T(8,128)(2,1)S(1)} copy-done((bf16[2,1024,1536]{2,1,0:T(8,128)(2,1)S(1)}, bf16[2,1024,1536]{2,1,0:T(8,128)(2,1)}, u32[]{:S(2)}) %copy-start) | copy-done | bytes 6291480
  46.3 2.5 %shard_map.95 = (bf16[1024,512]{1,0:T(8,128)(2,1)S(1)}, bf16[768,512]{1,0:T(8,128)(2,1)S(1)}, bf16[512,768]{1,0:T(8,128)(2,1)S(1)}, bf16[512,768]{1,0:T(8,128)(2,1)S(1)}) custom-call(s32[10]{0:T(128)S(1)} %stack.43.scal, bf16[128,2048]{1,0:T(8,128)(2,1)S(1)} %get-tuple-element.41.refs_0_, bf16[128,2048]{1,0:T(8,128)(2,1)S(1)} %collective-permute-done.refs_1_, ...), custom_call_target="tpu_custom_call" | custom-call | flops 1610612736 | bytes 1610612 | tf_op jit(solution)/shard_map/pallas_call | solution.py:38
  48.8 1.6 %shard_map.96.pair.pair_a = bf16[512,1536]{1,0:T(8,128)(2,1)S(1)} custom-call(s32[10]{0:T(128)S(1)} %stack.43.scal, bf16[128,2048]{1,0:T(8,128)(2,1)S(1)} %get-tuple-element.41.refs_0_, bf16[128,2048]{1,0:T(8,128)(2,1)S(1)} %collective-permute-done.refs_1_, bf16[128,2048]{1,0:T(8,128)(2,1)S(1)} %collective-permute-done.1.refs_2_, ...), custom_call_target="tpu_custom_call" | custom-call | flops 805306368 | bytes 805306 | tf_op jit(solution)/shard_map/pallas_call | solution.py:38
  50.5 0.5 slice-done.1
  51.0 2.5 %shard_map.100 = (bf16[1024,512]{1,0:T(8,128)(2,1)S(1)}, bf16[768,512]{1,0:T(8,128)(2,1)S(1)}, bf16[512,768]{1,0:T(8,128)(2,1)S(1)}, bf16[512,768]{1,0:T(8,128)(2,1)S(1)}) custom-call(s32[10]{0:T(128)S(1)} %stack.43.scal, bf16[128,1024]{1,0:T(8,128)(2,1)S(1)} %get-tuple-element.57.refs_0_, bf16[128,1024]{1,0:T(8,128)(2,1)S(1)} %collective-permute-done.10.refs_1_, ...), custom_call_target="tpu_custom_call" | custom-call | flops 1610612736 | bytes 1610612 | tf_op jit(solution)/shard_map/pallas_call | solution.py:38
  53.6 3.5 %collective-permute-done.8.refs_2_.refs_6_ = bf16[128,1024]{1,0:T(8,128)(2,1)S(1)} collective-permute-done((bf16[128,1024]{1,0:T(8,128)(2,1)S(1)}, bf16[128,1024]{1,0:T(8,128)(2,1)S(1)}, u32[]{:S(2)}, u32[]{:S(2)}) %collective-permute-start.8) | collective-permute-done | bytes 262176 | tf_op jit(solution)/shard_map/ppermute | solution.py:241
  57.0 1.6 %shard_map.101.pair.pair_b = bf16[512,1536]{1,0:T(8,128)(2,1)S(1)} custom-call(s32[10]{0:T(128)S(1)} %stack.43.scal, bf16[128,1024]{1,0:T(8,128)(2,1)S(1)} %get-tuple-element.53.refs_0_.refs_4_, bf16[128,1024]{1,0:T(8,128)(2,1)S(1)} %collective-permute-done.7.refs_1_.refs_5_, bf16[128,1024]{1,0:T(8,128)(2,1)S(1)} %collective-permute-done.8.refs_2_.refs_6_, ...), custom_call_target="tpu_custom_call" | custom-call | flops 805306368 | bytes 805306 | tf_op jit(solution)/shard_map/pallas_call | solution.py:38
  58.7 3.9 %shard_map.105 = (bf16[4,128,1536]{2,1,0:T(8,128)(2,1)S(1)}, bf16[4,128,1536]{2,1,0:T(8,128)(2,1)S(1)}) custom-call(s32[10]{0:T(128)S(1)} %stack.43.scal, bf16[1024,512]{1,0:T(8,128)(2,1)S(1)} %get-tuple-element.71.rows_a, bf16[1024,512]{1,0:T(8,128)(2,1)S(1)} %get-tuple-element.72.rows_b, bf16[512,1536]{1,0:T(8,128)(2,1)S(1)} %shard_map.96.pair.pair_a, ...), custom_call_target="tpu_custom_call" | custom-call | flops 3221225472 | bytes 3221225 | tf_op jit(solution)/shard_map/pallas_call | solution.py:38
  62.7 2.3 %shard_map.104 = (bf16[4,96,1024]{2,1,0:T(8,128)(2,1)S(1)}, bf16[4,96,1024]{2,1,0:T(8,128)(2,1)S(1)}) custom-call(s32[10]{0:T(128)S(1)} %stack.43.scal, bf16[128,2048]{1,0:T(8,128)(2,1)S(1)} %get-tuple-element.41.refs_0_, bf16[128,2048]{1,0:T(8,128)(2,1)S(1)} %collective-permute-done.refs_1_, bf16[128,2048]{1,0:T(8,128)(2,1)S(1)} %collective-permute-done.1.refs_2_, ...), custom_call_target="tpu_custom_call" | custom-call | flops 1610612736 | bytes 1610612 | tf_op jit(solution)/shard_map/pallas_call | solution.py:38
  65.1 0.5 collective-permute-start.17
  65.6 1.9 %collective-permute-done.17.other_down = bf16[4,96,1024]{2,1,0:T(8,128)(2,1)S(1)} collective-permute-done((bf16[4,96,1024]{2,1,0:T(8,128)(2,1)S(1)}, bf16[4,96,1024]{2,1,0:T(8,128)(2,1)S(1)}, u32[]{:S(2)}, u32[]{:S(2)}) %collective-permute-start.17) | collective-permute-done | bytes 786464 | tf_op jit(solution)/shard_map/ppermute | solution.py:239
  67.5 2.2 %shard_map.106 = bf16[4,288,1024]{2,1,0:T(8,128)(2,1)} custom-call(s32[10]{0:T(128)S(1)} %stack.43.scal, bf16[4,96,1024]{2,1,0:T(8,128)(2,1)S(1)} %get-tuple-element.69.keep_down, bf16[4,96,1024]{2,1,0:T(8,128)(2,1)S(1)} %collective-permute-done.17.other_down, bf16[4,128,1536]{2,1,0:T(8,128)(2,1)S(1)} %get-tuple-element.73.refs_0_, ...), custom_call_target="tpu_custom_call" | custom-call | flops 1 | tf_op jit(solution)/shard_map/pallas_call | solution.py:38
  69.7 4.9 %all-to-all-start = ((bf16[4,288,1024]{2,1,0:T(8,128)(2,1)}), bf16[4,288,1024]{2,1,0:T(8,128)(2,1)S(1)}, u32[]{:S(2)}, u32[]{:S(2)}) async-start(bf16[4,288,1024]{2,1,0:T(8,128)(2,1)} %shard_map.106), calls=%async_computation | async-start | bytes 4718592 | tf_op jit(solution)/shard_map/all_to_all | solution.py:340
  74.6 2.8 %copy-done.1 = bf16[2,1024,1536]{2,1,0:T(8,128)(2,1)S(1)} copy-done((bf16[2,1024,1536]{2,1,0:T(8,128)(2,1)S(1)}, bf16[2,1024,1536]{2,1,0:T(8,128)(2,1)}, u32[]{:S(2)}) %copy-start.1) | copy-done | bytes 6291480
  77.4 1.4 %copy-done.6 = bf16[512,1536]{1,0:T(8,128)(2,1)S(1)} copy-done((bf16[512,1536]{1,0:T(8,128)(2,1)S(1)}, bf16[512,1536]{1,0:T(8,128)(2,1)}, u32[]{:S(2)}) %copy-start.6) | copy-done | bytes 1572888
  78.8 2.4 %shard_map.102 = (bf16[128,1024]{1,0:T(8,128)(2,1)S(1)}, bf16[128,1024]{1,0:T(8,128)(2,1)S(1)}, bf16[128,1024]{1,0:T(8,128)(2,1)S(1)}, bf16[128,1024]{1,0:T(8,128)(2,1)S(1)}) custom-call(s32[10]{0:T(128)S(1)} %stack.43.scal, bf16[512,1536]{1,0:T(8,128)(2,1)S(1)} %copy-done.6, bf16[2,1024,1536]{2,1,0:T(8,128)(2,1)S(1)} %copy-done.1), custom_call_target="tpu_custom_call" | custom-call | flops 1610612736 | bytes 1610612 | tf_op jit(solution)/shard_map/pallas_call | solution.py:38
  81.2 1.3 %collective-permute-start.13 = (bf16[128,1024]{1,0:T(8,128)(2,1)S(1)}, bf16[128,1024]{1,0:T(8,128)(2,1)S(1)}, u32[]{:S(2)}, u32[]{:S(2)}) collective-permute-start(bf16[128,1024]{1,0:T(8,128)(2,1)S(1)} %get-tuple-element.64), channel_id=1, source_target_pairs={{0,1},{1,0},{2,3},{3,2},{4,5},{5,4},{6,7},{7,6},{8,9},{9,8},{10,11... | collective-permute-start | bytes 786440 | tf_op jit(solution)/shard_map/ppermute | solution.py:241
  82.5 0.8 collective-permute-start.14
  83.3 1.4 %collective-permute-start.15 = (bf16[128,1024]{1,0:T(8,128)(2,1)S(1)}, bf16[128,1024]{1,0:T(8,128)(2,1)S(1)}, u32[]{:S(2)}, u32[]{:S(2)}) collective-permute-start(bf16[128,1024]{1,0:T(8,128)(2,1)S(1)} %get-tuple-element.66), channel_id=1, source_target_pairs={{0,3},{1,2},{2,1},{3,0},{4,7},{5,6},{6,5},{7,4},{8,11},{9,10},{10,... | collective-permute-start | bytes 786440 | tf_op jit(solution)/shard_map/ppermute | solution.py:241
  84.7 5.7 %collective-permute-done.13.refs_1_ = bf16[128,1024]{1,0:T(8,128)(2,1)S(1)} collective-permute-done((bf16[128,1024]{1,0:T(8,128)(2,1)S(1)}, bf16[128,1024]{1,0:T(8,128)(2,1)S(1)}, u32[]{:S(2)}, u32[]{:S(2)}) %collective-permute-start.13) | collective-permute-done | bytes 262176 | tf_op jit(solution)/shard_map/ppermute | solution.py:241
  90.4 4.1 %collective-permute-done.14.refs_2_ = bf16[128,1024]{1,0:T(8,128)(2,1)S(1)} collective-permute-done((bf16[128,1024]{1,0:T(8,128)(2,1)S(1)}, bf16[128,1024]{1,0:T(8,128)(2,1)S(1)}, u32[]{:S(2)}, u32[]{:S(2)}) %collective-permute-start.14) | collective-permute-done | bytes 262176 | tf_op jit(solution)/shard_map/ppermute | solution.py:241
  94.5 1.7 %collective-permute-done.15.refs_3_ = bf16[128,1024]{1,0:T(8,128)(2,1)S(1)} collective-permute-done((bf16[128,1024]{1,0:T(8,128)(2,1)S(1)}, bf16[128,1024]{1,0:T(8,128)(2,1)S(1)}, u32[]{:S(2)}, u32[]{:S(2)}) %collective-permute-start.15) | collective-permute-done | bytes 262176 | tf_op jit(solution)/shard_map/ppermute | solution.py:241
  96.1 1.0 shard_map.103
  97.1 1.8 %collective-permute-start.16 = (bf16[256,1024]{1,0:T(8,128)(2,1)S(1)}, bf16[256,1024]{1,0:T(8,128)(2,1)S(1)}, u32[]{:S(2)}, u32[]{:S(2)}) collective-permute-start(bf16[256,1024]{1,0:T(8,128)(2,1)S(1)} %shard_map.103), channel_id=1, source_target_pairs={{0,8},{4,12},{8,0},{12,4},{16,24},{20,28},{24,16},{28,20},{1,9},{5... | collective-permute-start | bytes 1572872 | tf_op jit(solution)/shard_map/ppermute | solution.py:240
  98.9 2.4 %shard_map.97 = (bf16[128,1024]{1,0:T(8,128)(2,1)S(1)}, bf16[128,1024]{1,0:T(8,128)(2,1)S(1)}, bf16[128,1024]{1,0:T(8,128)(2,1)S(1)}, bf16[128,1024]{1,0:T(8,128)(2,1)S(1)}) custom-call(s32[10]{0:T(128)S(1)} %stack.43.scal, bf16[512,1536]{1,0:T(8,128)(2,1)S(1)} %copy-done.4, bf16[2,1024,1536]{2,1,0:T(8,128)(2,1)S(1)} %copy-done.1), custom_call_target="tpu_custom_call" | custom-call | flops 1610612736 | bytes 1610612 | tf_op jit(solution)/shard_map/pallas_call | solution.py:38
  101.3 0.8 collective-permute-start.3
  102.1 1.5 %collective-permute-start.4 = (bf16[128,1024]{1,0:T(8,128)(2,1)S(1)}, bf16[128,1024]{1,0:T(8,128)(2,1)S(1)}, u32[]{:S(2)}, u32[]{:S(2)}) collective-permute-start(bf16[128,1024]{1,0:T(8,128)(2,1)S(1)} %get-tuple-element.49), channel_id=1, source_target_pairs={{0,2},{1,3},{2,0},{3,1},{4,6},{5,7},{6,4},{7,5},{8,10},{9,11},{10,... | collective-permute-start | bytes 786440 | tf_op jit(solution)/shard_map/ppermute | solution.py:241
  103.6 1.2 collective-permute-start.5
  104.9 5.8 %collective-permute-done.3.refs_1_ = bf16[128,1024]{1,0:T(8,128)(2,1)S(1)} collective-permute-done((bf16[128,1024]{1,0:T(8,128)(2,1)S(1)}, bf16[128,1024]{1,0:T(8,128)(2,1)S(1)}, u32[]{:S(2)}, u32[]{:S(2)}) %collective-permute-start.3) | collective-permute-done | bytes 262176 | tf_op jit(solution)/shard_map/ppermute | solution.py:241
  110.6 3.5 %collective-permute-done.4.refs_2_ = bf16[128,1024]{1,0:T(8,128)(2,1)S(1)} collective-permute-done((bf16[128,1024]{1,0:T(8,128)(2,1)S(1)}, bf16[128,1024]{1,0:T(8,128)(2,1)S(1)}, u32[]{:S(2)}, u32[]{:S(2)}) %collective-permute-start.4) | collective-permute-done | bytes 262176 | tf_op jit(solution)/shard_map/ppermute | solution.py:241
  114.1 1.0 shard_map.98
  115.1 9.4 %collective-permute-done.16 = bf16[256,1024]{1,0:T(8,128)(2,1)S(1)} collective-permute-done((bf16[256,1024]{1,0:T(8,128)(2,1)S(1)}, bf16[256,1024]{1,0:T(8,128)(2,1)S(1)}, u32[]{:S(2)}, u32[]{:S(2)}) %collective-permute-start.16) | collective-permute-done | bytes 524320 | tf_op jit(solution)/shard_map/ppermute | solution.py:240
  124.5 1.0 add_convert_fusion
  125.5 3.5 %all-to-all-done.terms = bf16[4,288,1024]{2,1,0:T(8,128)(2,1)S(1)} async-done(((bf16[4,288,1024]{2,1,0:T(8,128)(2,1)}), bf16[4,288,1024]{2,1,0:T(8,128)(2,1)S(1)}, u32[]{:S(2)}, u32[]{:S(2)}) %all-to-all-start) | async-done | bytes 2359328 | tf_op jit(solution)/shard_map/all_to_all | solution.py:340
  128.9 2.1 %shard_map.107 = (f32[2,128,1536]{2,1,0:T(8,128)}, f32[2,96,1024]{2,1,0:T(8,128)}) custom-call(s32[10]{0:T(128)S(1)} %stack.43.scal, bf16[4,288,1024]{2,1,0:T(8,128)(2,1)S(1)} %all-to-all-done.terms), custom_call_target="tpu_custom_call" | custom-call | flops 1 | tf_op jit(solution)/shard_map/pallas_call | solution.py:38
  (27 shorter events, 0.5 us)
Async XLA Ops:
  3.3 26.9 %collective-permute-start.6 = (bf16[528,1024]{1,0:T(8,128)(2,1)S(1)}, bf16[528,1024]{1,0:T(8,128)(2,1)S(1)}, u32[]{:S(2)}, u32[]{:S(2)}) collective-permute-start(bf16[528,1024]{1,0:T(8,128)(2,1)S(1)} %get-tuple-element.51), channel_id=1, source_target_pairs={{0,8},{4,12},{8,0},{12,4},{16,24},{20,28},{24,16},{28,20},{1,9},{5... | collective-permute-start | bytes 3244040 | tf_op jit(solution)/shard_map/ppermute | solution.py:240
  6.4 28.4 %collective-permute-start = (bf16[128,2048]{1,0:T(8,128)(2,1)S(1)}, bf16[128,2048]{1,0:T(8,128)(2,1)S(1)}, u32[]{:S(2)}, u32[]{:S(2)}) collective-permute-start(bf16[128,2048]{1,0:T(8,128)(2,1)S(1)} %get-tuple-element.42), channel_id=1, source_target_pairs={{0,1},{1,0},{2,3},{3,2},{4,5},{5,4},{6,7},{7,6},{8,9},{9,8},{10,11... | collective-permute-start | bytes 1572872 | tf_op jit(solution)/shard_map/ppermute | solution.py:241
  7.9 27.2 %collective-permute-start.1 = (bf16[128,2048]{1,0:T(8,128)(2,1)S(1)}, bf16[128,2048]{1,0:T(8,128)(2,1)S(1)}, u32[]{:S(2)}, u32[]{:S(2)}) collective-permute-start(bf16[128,2048]{1,0:T(8,128)(2,1)S(1)} %get-tuple-element.43), channel_id=1, source_target_pairs={{0,2},{1,3},{2,0},{3,1},{4,6},{5,7},{6,4},{7,5},{8,10},{9,11},{10,... | collective-permute-start | bytes 1572872 | tf_op jit(solution)/shard_map/ppermute | solution.py:241
  9.4 27.4 %collective-permute-start.2 = (bf16[128,2048]{1,0:T(8,128)(2,1)S(1)}, bf16[128,2048]{1,0:T(8,128)(2,1)S(1)}, u32[]{:S(2)}, u32[]{:S(2)}) collective-permute-start(bf16[128,2048]{1,0:T(8,128)(2,1)S(1)} %get-tuple-element.44), channel_id=1, source_target_pairs={{0,3},{1,2},{2,1},{3,0},{4,7},{5,6},{6,5},{7,4},{8,11},{9,10},{10,... | collective-permute-start | bytes 1572872 | tf_op jit(solution)/shard_map/ppermute | solution.py:241
  31.6 9.3 %collective-permute-start.10 = (bf16[128,1024]{1,0:T(8,128)(2,1)S(1)}, bf16[128,1024]{1,0:T(8,128)(2,1)S(1)}, u32[]{:S(2)}, u32[]{:S(2)}) collective-permute-start(bf16[128,1024]{1,0:T(8,128)(2,1)S(1)} %get-tuple-element.58), channel_id=1, source_target_pairs={{0,1},{1,0},{2,3},{3,2},{4,5},{5,4},{6,7},{7,6},{8,9},{9,8},{10,11... | collective-permute-start | bytes 786440 | tf_op jit(solution)/shard_map/ppermute | solution.py:241
  33.3 17.2 %collective-permute-start.11 = (bf16[128,1024]{1,0:T(8,128)(2,1)S(1)}, bf16[128,1024]{1,0:T(8,128)(2,1)S(1)}, u32[]{:S(2)}, u32[]{:S(2)}) collective-permute-start(bf16[128,1024]{1,0:T(8,128)(2,1)S(1)} %get-tuple-element.59), channel_id=1, source_target_pairs={{0,2},{1,3},{2,0},{3,1},{4,6},{5,7},{6,4},{7,5},{8,10},{9,11},{10,... | collective-permute-start | bytes 786440 | tf_op jit(solution)/shard_map/ppermute | solution.py:241
  34.8 15.7 %collective-permute-start.12 = (bf16[128,1024]{1,0:T(8,128)(2,1)S(1)}, bf16[128,1024]{1,0:T(8,128)(2,1)S(1)}, u32[]{:S(2)}, u32[]{:S(2)}) collective-permute-start(bf16[128,1024]{1,0:T(8,128)(2,1)S(1)} %get-tuple-element.60), channel_id=1, source_target_pairs={{0,3},{1,2},{2,1},{3,0},{4,7},{5,6},{6,5},{7,4},{8,11},{9,10},{10,... | collective-permute-start | bytes 786440 | tf_op jit(solution)/shard_map/ppermute | solution.py:241
  35.1 18.4 %collective-permute-start.7 = (bf16[128,1024]{1,0:T(8,128)(2,1)S(1)}, bf16[128,1024]{1,0:T(8,128)(2,1)S(1)}, u32[]{:S(2)}, u32[]{:S(2)}) collective-permute-start(bf16[128,1024]{1,0:T(8,128)(2,1)S(1)} %get-tuple-element.54), channel_id=1, source_target_pairs={{0,1},{1,0},{2,3},{3,2},{4,5},{5,4},{6,7},{7,6},{8,9},{9,8},{10,11... | collective-permute-start | bytes 786440 | tf_op jit(solution)/shard_map/ppermute | solution.py:241
  36.8 20.2 %collective-permute-start.8 = (bf16[128,1024]{1,0:T(8,128)(2,1)S(1)}, bf16[128,1024]{1,0:T(8,128)(2,1)S(1)}, u32[]{:S(2)}, u32[]{:S(2)}) collective-permute-start(bf16[128,1024]{1,0:T(8,128)(2,1)S(1)} %get-tuple-element.55), channel_id=1, source_target_pairs={{0,2},{1,3},{2,0},{3,1},{4,6},{5,7},{6,4},{7,5},{8,10},{9,11},{10,... | collective-permute-start | bytes 786440 | tf_op jit(solution)/shard_map/ppermute | solution.py:241
  40.9 16.2 %collective-permute-start.9 = (bf16[128,1024]{1,0:T(8,128)(2,1)S(1)}, bf16[128,1024]{1,0:T(8,128)(2,1)S(1)}, u32[]{:S(2)}, u32[]{:S(2)}) collective-permute-start(bf16[128,1024]{1,0:T(8,128)(2,1)S(1)} %get-tuple-element.56), channel_id=1, source_target_pairs={{0,3},{1,2},{2,1},{3,0},{4,7},{5,6},{6,5},{7,4},{8,11},{9,10},{10,... | collective-permute-start | bytes 786440 | tf_op jit(solution)/shard_map/ppermute | solution.py:241
  43.5 2.8 %copy-start = (bf16[2,1024,1536]{2,1,0:T(8,128)(2,1)S(1)}, bf16[2,1024,1536]{2,1,0:T(8,128)(2,1)}, u32[]{:S(2)}) copy-start(bf16[2,1024,1536]{2,1,0:T(8,128)(2,1)} %w_in.3) | copy-start | bytes 18874372
  46.3 2.6 %copy-start.2 = (bf16[2,768,1024]{2,1,0:T(8,128)(2,1)S(1)}, bf16[2,768,1024]{2,1,0:T(8,128)(2,1)}, u32[]{:S(2)}) copy-start(bf16[2,768,1024]{2,1,0:T(8,128)(2,1)} %refs_4_.7) | copy-start | bytes 9437188
  46.3 4.2 %slice-start = ((s8[6291456]{0:T(1024)(128)(4,1)}), s8[2097152]{0:T(1024)(128)(4,1)S(1)}, s32[]{:S(2)}) async-start(s8[6291456]{0:T(1024)(128)(4,1)} %bitcast.13), calls=%async_computation.1 | async-start | bytes 4194304
  48.8 2.2 %slice-start.1 = ((s8[6291456]{0:T(1024)(128)(4,1)}), s8[4194304]{0:T(1024)(128)(4,1)S(1)}, s32[]{:S(2)}) async-start(s8[6291456]{0:T(1024)(128)(4,1)} %bitcast.13), calls=%async_computation.2 | async-start | bytes 8388608
  50.5 8.2 %copy-start.3 = (bf16[512,1536]{1,0:T(8,128)(2,1)}, bf16[512,1536]{1,0:T(8,128)(2,1)S(1)}, u32[]{:S(2)}) copy-start(bf16[512,1536]{1,0:T(8,128)(2,1)S(1)} %shard_map.96.pair.pair_a) | copy-start | bytes 4718596
  58.6 4.0 %copy-start.5 = (bf16[512,1536]{1,0:T(8,128)(2,1)}, bf16[512,1536]{1,0:T(8,128)(2,1)S(1)}, u32[]{:S(2)}) copy-start(bf16[512,1536]{1,0:T(8,128)(2,1)S(1)} %shard_map.101.pair.pair_b) | copy-start | bytes 4718596
  62.6 4.9 %collective-permute-start.18 = (bf16[4,128,1536]{2,1,0:T(8,128)(2,1)S(1)}, bf16[4,128,1536]{2,1,0:T(8,128)(2,1)S(1)}, u32[]{:S(2)}, u32[]{:S(2)}) collective-permute-start(bf16[4,128,1536]{2,1,0:T(8,128)(2,1)S(1)} %get-tuple-element.74), channel_id=1, source_target_pairs={{0,4},{4,0},{8,12},{12,8},{16,20},{20,16},{24,28},{28,24},{1,5},{5... | collective-permute-start | bytes 4718600 | tf_op jit(solution)/shard_map/ppermute | solution.py:239
  65.1 2.5 %collective-permute-start.17 = (bf16[4,96,1024]{2,1,0:T(8,128)(2,1)S(1)}, bf16[4,96,1024]{2,1,0:T(8,128)(2,1)S(1)}, u32[]{:S(2)}, u32[]{:S(2)}) collective-permute-start(bf16[4,96,1024]{2,1,0:T(8,128)(2,1)S(1)} %get-tuple-element.70), channel_id=1, source_target_pairs={{0,4},{4,0},{8,12},{12,8},{16,20},{20,16},{24,28},{28,24},{1,5},{5... | collective-permute-start | bytes 2359304 | tf_op jit(solution)/shard_map/ppermute | solution.py:239
  69.7 59.2 %all-to-all-start = ((bf16[4,288,1024]{2,1,0:T(8,128)(2,1)}), bf16[4,288,1024]{2,1,0:T(8,128)(2,1)S(1)}, u32[]{:S(2)}, u32[]{:S(2)}) async-start(bf16[4,288,1024]{2,1,0:T(8,128)(2,1)} %shard_map.106), calls=%async_computation | async-start | bytes 4718592 | tf_op jit(solution)/shard_map/all_to_all | solution.py:340
  74.6 2.8 %copy-start.1 = (bf16[2,1024,1536]{2,1,0:T(8,128)(2,1)S(1)}, bf16[2,1024,1536]{2,1,0:T(8,128)(2,1)}, u32[]{:S(2)}) copy-start(bf16[2,1024,1536]{2,1,0:T(8,128)(2,1)} %w_in.3) | copy-start | bytes 18874372
  77.4 1.4 %copy-start.6 = (bf16[512,1536]{1,0:T(8,128)(2,1)S(1)}, bf16[512,1536]{1,0:T(8,128)(2,1)}, u32[]{:S(2)}) copy-start(bf16[512,1536]{1,0:T(8,128)(2,1)} %copy-done.5) | copy-start | bytes 4718596
  81.2 17.8 %copy-start.4 = (bf16[512,1536]{1,0:T(8,128)(2,1)S(1)}, bf16[512,1536]{1,0:T(8,128)(2,1)}, u32[]{:S(2)}) copy-start(bf16[512,1536]{1,0:T(8,128)(2,1)} %copy-done.3) | copy-start | bytes 4718596
  81.2 9.2 %collective-permute-start.13 = (bf16[128,1024]{1,0:T(8,128)(2,1)S(1)}, bf16[128,1024]{1,0:T(8,128)(2,1)S(1)}, u32[]{:S(2)}, u32[]{:S(2)}) collective-permute-start(bf16[128,1024]{1,0:T(8,128)(2,1)S(1)} %get-tuple-element.64), channel_id=1, source_target_pairs={{0,1},{1,0},{2,3},{3,2},{4,5},{5,4},{6,7},{7,6},{8,9},{9,8},{10,11... | collective-permute-start | bytes 786440 | tf_op jit(solution)/shard_map/ppermute | solution.py:241
  82.5 12.0 %collective-permute-start.14 = (bf16[128,1024]{1,0:T(8,128)(2,1)S(1)}, bf16[128,1024]{1,0:T(8,128)(2,1)S(1)}, u32[]{:S(2)}, u32[]{:S(2)}) collective-permute-start(bf16[128,1024]{1,0:T(8,128)(2,1)S(1)} %get-tuple-element.65), channel_id=1, source_target_pairs={{0,2},{1,3},{2,0},{3,1},{4,6},{5,7},{6,4},{7,5},{8,10},{9,11},{10,... | collective-permute-start | bytes 786440 | tf_op jit(solution)/shard_map/ppermute | solution.py:241
  83.3 12.8 %collective-permute-start.15 = (bf16[128,1024]{1,0:T(8,128)(2,1)S(1)}, bf16[128,1024]{1,0:T(8,128)(2,1)S(1)}, u32[]{:S(2)}, u32[]{:S(2)}) collective-permute-start(bf16[128,1024]{1,0:T(8,128)(2,1)S(1)} %get-tuple-element.66), channel_id=1, source_target_pairs={{0,3},{1,2},{2,1},{3,0},{4,7},{5,6},{6,5},{7,4},{8,11},{9,10},{10,... | collective-permute-start | bytes 786440 | tf_op jit(solution)/shard_map/ppermute | solution.py:241
  97.1 27.4 %collective-permute-start.16 = (bf16[256,1024]{1,0:T(8,128)(2,1)S(1)}, bf16[256,1024]{1,0:T(8,128)(2,1)S(1)}, u32[]{:S(2)}, u32[]{:S(2)}) collective-permute-start(bf16[256,1024]{1,0:T(8,128)(2,1)S(1)} %shard_map.103), channel_id=1, source_target_pairs={{0,8},{4,12},{8,0},{12,4},{16,24},{20,28},{24,16},{28,20},{1,9},{5... | collective-permute-start | bytes 1572872 | tf_op jit(solution)/shard_map/ppermute | solution.py:240
  101.3 9.3 %collective-permute-start.3 = (bf16[128,1024]{1,0:T(8,128)(2,1)S(1)}, bf16[128,1024]{1,0:T(8,128)(2,1)S(1)}, u32[]{:S(2)}, u32[]{:S(2)}) collective-permute-start(bf16[128,1024]{1,0:T(8,128)(2,1)S(1)} %get-tuple-element.48), channel_id=1, source_target_pairs={{0,1},{1,0},{2,3},{3,2},{4,5},{5,4},{6,7},{7,6},{8,9},{9,8},{10,11... | collective-permute-start | bytes 786440 | tf_op jit(solution)/shard_map/ppermute | solution.py:241
  102.1 12.0 %collective-permute-start.4 = (bf16[128,1024]{1,0:T(8,128)(2,1)S(1)}, bf16[128,1024]{1,0:T(8,128)(2,1)S(1)}, u32[]{:S(2)}, u32[]{:S(2)}) collective-permute-start(bf16[128,1024]{1,0:T(8,128)(2,1)S(1)} %get-tuple-element.49), channel_id=1, source_target_pairs={{0,2},{1,3},{2,0},{3,1},{4,6},{5,7},{6,4},{7,5},{8,10},{9,11},{10,... | collective-permute-start | bytes 786440 | tf_op jit(solution)/shard_map/ppermute | solution.py:241
  103.6 10.5 %collective-permute-start.5 = (bf16[128,1024]{1,0:T(8,128)(2,1)S(1)}, bf16[128,1024]{1,0:T(8,128)(2,1)S(1)}, u32[]{:S(2)}, u32[]{:S(2)}) collective-permute-start(bf16[128,1024]{1,0:T(8,128)(2,1)S(1)} %get-tuple-element.50), channel_id=1, source_target_pairs={{0,3},{1,2},{2,1},{3,0},{4,7},{5,6},{6,5},{7,4},{8,11},{9,10},{10,... | collective-permute-start | bytes 786440 | tf_op jit(solution)/shard_map/ppermute | solution.py:241

commit v5 on v4

--- a/solution.py
+++ b/solution.py
@@ -10,7 +10,6 @@
 TOP = 2
 BF = jnp.bfloat16
 F32 = jnp.float32
-IN_PARTS = 1
 
 
 def dot(a, b):
@@ -34,19 +33,26 @@
     return pl.BlockSpec(shape, lambda step, scal: (scal[0], 0, index))
 
 
-def call(body, out_shape, flops, limit, scal, *args, specs=None):
-    return pl.pallas_call(
-        body,
+def call(body, out_shape, flops, limit, scal, *args, specs=None, out_specs=None, steps=1):
+    params = dict(
         out_shape=out_shape,
-        grid_spec=pltpu.PrefetchScalarGridSpec(
-            num_scalar_prefetch=1,
-            grid=(1,),
-            in_specs=specs or [whole(x) for x in args],
-            out_specs=[whole(x) for x in out_shape],
-        ),
         compiler_params=pltpu.CompilerParams(vmem_limit_bytes=limit << 20),
         cost_estimate=pl.CostEstimate(flops=flops, bytes_accessed=flops // 1000, transcendentals=0),
-    )(scal, *args)
+    )
+    if specs is None:
+        vmem = pl.BlockSpec(memory_space=pltpu.VMEM)
+        params.update(
+            in_specs=[pl.BlockSpec(memory_space=pltpu.SMEM)] + [vmem] * len(args),
+            out_specs=[vmem] * len(out_shape),
+        )
+    else:
+        params["grid_spec"] = pltpu.PrefetchScalarGridSpec(
+            num_scalar_prefetch=1,
+            grid=(steps,),
+            in_specs=specs,
+            out_specs=out_specs or [whole(x) for x in out_shape],
+        )
+    return pl.pallas_call(body, **params)(scal, *args)
 
 
 def stack_rows(refs, column, columns):
@@ -64,26 +70,23 @@
 ROUTE_ROWS = 16
 
 
-def fill_slots(cap, n, scal, route, tokens, cotangent, outs, back):
-    chosen, places, share = route
-    slot = lax.broadcasted_iota(jnp.int32, (cap, back.shape[0]), 0)
+def slot_hits(cap, n, scal, route, count):
+    chosen, places, _ = route
+    slot = lax.broadcasted_iota(jnp.int32, (cap, count), 0)
     slot = jnp.concatenate([slot + scal[2 + j] for j in range(n)], axis=0).astype(F32)
-    first = slot == chosen[0] * cap + places[0]
-    second = slot == chosen[1] * cap + places[1]
-    hit = jnp.where(jnp.logical_or(first, second), 1.0, 0.0)
-    factor = jnp.where(first, share, 0.0) + jnp.where(second, 1.0 - share, 0.0)
-    factor = jnp.sum(factor, axis=1, keepdims=True)
+    return slot == chosen[0] * cap + places[0], slot == chosen[1] * cap + places[1]
+
+
+def token_rows(hits, tokens, back):
+    hit = jnp.where(jnp.logical_or(*hits), 1.0, 0.0)
     back[...] = jnp.transpose(hit).astype(BF)
-    hit = hit.astype(BF)
-    rows = dot(hit, tokens).astype(BF)
-    scaled = (dot(hit, cotangent) * factor).astype(BF)
-    rows = jnp.concatenate([rows, scaled], axis=1)
-    column = 0
-    for k in range(0, len(outs), n):
-        columns = outs[k].shape[1]
-        for j in range(n):
-            outs[k + j][...] = rows[j * cap : (j + 1) * cap, column : column + columns]
-        column += columns
+    return dot(hit.astype(BF), tokens).astype(BF)
+
+
+def cotangent_rows(hits, share, cotangent):
+    hit = jnp.where(jnp.logical_or(*hits), 1.0, 0.0).astype(BF)
+    factor = jnp.where(hits[0], share, 0.0) + jnp.where(hits[1], 1.0 - share, 0.0)
+    return (dot(hit, cotangent) * jnp.sum(factor, axis=1, keepdims=True)).astype(BF)
 
 
 def own_slots_body(cap, n, scal, logits, experts, places, tokens, cotangent, *refs):
@@ -95,7 +98,7 @@
     low = (share - high.astype(F32) - middle.astype(F32)).astype(BF)
     chosen = experts[...].astype(F32)
     slots = places[...].astype(F32)
-    rows = [x.astype(BF).astype(F32) for x in (chosen[0:1], chosen[1:2], slots[0:1], slots[1:2])]
+    rows = [chosen[0:1], chosen[1:2], slots[0:1], slots[1:2]]
     shares = [x.astype(F32) for x in (high, middle, low)]
     shares.append(jnp.zeros_like(share))
     pad = [jnp.zeros((1, width - 4 * count), F32)] if width > 4 * count else []
@@ -103,20 +106,37 @@
     head.append(jnp.zeros((ROUTE_ROWS - 2, width), F32))
     block[pl.ds(0, ROUTE_ROWS), :] = jnp.concatenate(head, axis=0).astype(BF)
     block[pl.ds(ROUTE_ROWS, count), :] = tokens[...]
-    block[pl.ds(ROUTE_ROWS + count, count), :] = cotangent[...]
     route = ((chosen[0:1], chosen[1:2]), (slots[0:1], slots[1:2]), share)
-    fill_slots(cap, n, scal, route, tokens[...], cotangent[...], outs, back)
-
-
-def beside_slots_body(cap, n, scal, block, *refs):
-    outs, back = refs[:-1], refs[-1]
-    count = back.shape[0]
+    hits = slot_hits(cap, n, scal, route, count)
+    rows = token_rows(hits, tokens[...], back)
+    scaled = cotangent_rows(hits, share, cotangent[...])
+    for j, out in enumerate(outs):
+        out[:, pl.ds(0, width)] = rows[j * cap : (j + 1) * cap]
+        out[:, pl.ds(width, width)] = scaled[j * cap : (j + 1) * cap]
+
+
+def read_route(block, count):
     head = block[0:2, :].astype(F32)
     row = lambda r, k: head[r : r + 1, k * count : (k + 1) * count]
     share = row(1, 0) + row(1, 1) + row(1, 2)
-    route = ((row(0, 0), row(0, 1)), (row(0, 2), row(0, 3)), share)
-    tokens = block[pl.ds(ROUTE_ROWS, count), :]
-    fill_slots(cap, n, scal, route, tokens, block[pl.ds(ROUTE_ROWS + count, count), :], outs, back)
+    return (row(0, 0), row(0, 1)), (row(0, 2), row(0, 3)), share
+
+
+def beside_tokens_body(cap, n, scal, block, *refs):
+    outs, back = refs[:-1], refs[-1]
+    count = back.shape[0]
+    hits = slot_hits(cap, n, scal, read_route(block, count), count)
+    rows = token_rows(hits, block[pl.ds(ROUTE_ROWS, count), :], back)
+    for j, out in enumerate(outs):
+        out[...] = rows[j * cap : (j + 1) * cap]
+
+
+def beside_cotangents_body(cap, n, scal, block, cotangent, *outs):
+    count = cotangent.shape[0]
+    route = read_route(block, count)
+    rows = cotangent_rows(slot_hits(cap, n, scal, route, count), route[2], cotangent[...])
+    for j, out in enumerate(outs):
+        out[...] = rows[j * cap : (j + 1) * cap]
 
 
 def forward_body(tile, scal, *refs):
@@ -151,26 +171,27 @@
     pair[:, pl.ds(ff, ff)] = (grad_hidden * scale_up[...].astype(F32)).astype(BF)
 
 
-def down_body(n, nz, scal, *refs):
-    arrived, (hidden_a, hidden_b, give, keep) = refs[: 2 * n], refs[2 * n :]
+def put_shards(result, nz, part, before, give, keep):
+    for k in range(nz):
+        for out, earlier, first in ((give, before[:1], k), (keep, before[1:], nz + k)):
+            total = result[first * part : (first + 1) * part]
+            for x in earlier:
+                total = total + x[k].astype(F32)
+            out[k] = total.astype(BF)
+
+
+def down_body(n, nz, column, scal, *refs):
+    arrived, hidden, before, (give, keep) = refs[:n], refs[n], refs[n + 1 : -2], refs[-2:]
     part, width = give.shape[1:]
-    slots = [stack_rows(arrived[:n], width, width), stack_rows(arrived[n:], 0, width)]
-    left = shard_rows((hidden_a, hidden_b), scal, nz, part)
-    result = dot(left, jnp.concatenate(slots, axis=0)).astype(BF)
-    for k in range(nz):
-        give[k] = result[k * part : (k + 1) * part]
-        keep[k] = result[(nz + k) * part : (nz + k + 1) * part]
-
-
-def input_weight_body(first, nz, scal, rows_a, rows_b, pair_a, pair_b, give, keep):
-    part, columns = give.shape[1:]
-    pair = jnp.concatenate(
-        [pair_a[:, pl.ds(first, columns)], pair_b[:, pl.ds(first, columns)]], axis=0
-    )
-    result = dot(shard_rows((rows_a, rows_b), scal, nz, part), pair).astype(BF)
-    for k in range(nz):
-        give[k] = result[k * part : (k + 1) * part]
-        keep[k] = result[(nz + k) * part : (nz + k + 1) * part]
+    left = shard_rows((hidden,), scal, nz, part)
+    put_shards(dot(left, stack_rows(arrived, column, width)), nz, part, before, give, keep)
+
+
+def input_weight_body(nz, scal, rows, pair, *refs):
+    before, (give, keep) = refs[:-2], refs[-2:]
+    part = give.shape[1]
+    left = shard_rows((rows,), scal, nz, part)
+    put_shards(dot(left, pair[...]), nz, part, before, give, keep)
 
 
 def in_blocks(rows, width, columns):
@@ -183,30 +204,29 @@
     return blocks
 
 
-def pack_body(nz, scal, keep_down, other_down, *refs):
+def pack_body(scal, keep_down, other_down, *refs):
     ins, out = refs[:-1], refs[-1]
     width = keep_down.shape[2]
     top = keep_down.shape[1]
     rows = ins[0].shape[1]
-    for k in range(nz):
-        out[k, pl.ds(0, top), :] = keep_down[k] + other_down[k]
-        total = jnp.concatenate([x[k] + y[k] for x, y in zip(ins[::2], ins[1::2])], axis=1)
-        for c, columns, r, count, place, column in in_blocks(rows, width, total.shape[1]):
-            out[k, pl.ds(top + place, count), pl.ds(column, columns)] = total[
-                r : r + count, c : c + columns
-            ]
-
-
-def unpack_body(sets, scal, terms, grad_in, grad_down):
+    out[0, pl.ds(0, top), :] = keep_down[0] + other_down[0]
+    total = jnp.concatenate([x[0] + y[0] for x, y in zip(ins[::2], ins[1::2])], axis=1)
+    for c, columns, r, count, place, column in in_blocks(rows, width, total.shape[1]):
+        out[0, pl.ds(top + place, count), pl.ds(column, columns)] = total[
+            r : r + count, c : c + columns
+        ]
+
+
+def unpack_body(scal, *refs):
+    terms, (grad_in, grad_down) = refs[:-2], refs[-2:]
     top, width = grad_down.shape[1:]
     rows, columns = grad_in.shape[1:]
-    for e, members in enumerate(sets):
-        total = functools.reduce(jnp.add, [terms[k].astype(F32) for k in members])
-        grad_down[e] = total[:top]
-        for c, some, r, count, place, column in in_blocks(rows, width, columns):
-            grad_in[e, pl.ds(r, count), pl.ds(c, some)] = total[
-                top + place : top + place + count, column : column + some
-            ]
+    total = functools.reduce(jnp.add, [x[0].astype(F32) for x in terms])
+    grad_down[0] = total[:top]
+    for c, some, r, count, place, column in in_blocks(rows, width, columns):
+        grad_in[0, pl.ds(r, count), pl.ds(c, some)] = total[
+            top + place : top + place + count, column : column + some
+        ]
 
 
 def returned_body(cap, scal, pair, w_in, *outs):
@@ -243,24 +263,37 @@
     macs = 2 * slots * width * ff
 
     count = token_count
+    held = [in_hbm(x) for x in (route_logits.T, expert_ids.T, slot_pos.T, tokens, cotangent)]
     *sent, back, block = call(
         functools.partial(own_slots_body, cap, n),
-        [bf(cap, 2 * width)] * n + [bf(count, slots), bf(ROUTE_ROWS + 2 * count, width)],
+        [bf(cap, 2 * width)] * n + [bf(count, slots), bf(ROUTE_ROWS + count, width)],
         macs // 4,
         LIMITS[0],
         scal,
-        *[in_hbm(x) for x in (route_logits.T, expert_ids.T, slot_pos.T, tokens, cotangent)],
+        *held,
+        specs=[whole(x) for x in held],
     )
     arrived = [[across(x, j) for j, x in enumerate(sent)]]
+    block = along_z(block, 1)
+    cotangent = along_z(cotangent, 1)
     *sent, back_beside = call(
-        functools.partial(beside_slots_body, cap, n),
-        [bf(cap, width)] * (2 * n) + [bf(count, slots)],
-        macs // 4,
+        functools.partial(beside_tokens_body, cap, n),
+        [bf(cap, width)] * n + [bf(count, slots)],
+        macs // 8,
         LIMITS[0],
         scal,
-        along_z(block, 1),
-    )
-    arrived.append([across(x, k % n) for k, x in enumerate(sent)])
+        block,
+    )
+    scaled = call(
+        functools.partial(beside_cotangents_body, cap, n),
+        [bf(cap, width)] * n,
+        macs // 8,
+        LIMITS[0],
+        scal,
+        block,
+        cotangent,
+    )
+    arrived.append([across(x, j) for x_all in (sent, scaled) for j, x in enumerate(x_all)])
     backs = [back, back_beside]
 
     forwards = []
@@ -294,32 +327,30 @@
             specs=[whole(x) for x in pieces] + [of_expert(w_down)] + [whole(x) for x in scales],
         )
 
-    columns = 2 * ff // IN_PARTS
-    terms = []
-    for k in range(IN_PARTS):
-        give, keep = call(
-            functools.partial(input_weight_body, k * columns, nz),
-            [bf(nz, width // ndp, columns)] * 2,
-            4 * macs // IN_PARTS,
+    ins, downs = [], []
+    for rows, pair in zip((rows_a, rows_b), pairs):
+        ins = call(
+            functools.partial(input_weight_body, nz),
+            [bf(nz, width // ndp, 2 * ff)] * 2,
+            2 * macs,
             LIMITS[3],
             scal,
-            rows_a,
-            rows_b,
-            *pairs,
-        )
-        terms += [keep, swap_core(give)]
-    give, keep = call(
-        functools.partial(down_body, n, nz),
-        [bf(nz, ff // ndp, width)] * 2,
-        2 * macs,
-        LIMITS[2],
-        scal,
-        *arrived[0],
-        *arrived[1][n:],
-        hidden_a,
-        hidden_b,
-    )
-    terms = [keep, swap_core(give)] + terms
+            rows,
+            pair,
+            *ins,
+        )
+    for g, (column, hidden) in enumerate(((width, hidden_a), (0, hidden_b))):
+        downs = call(
+            functools.partial(down_body, n, nz, column),
+            [bf(nz, ff // ndp, width)] * 2,
+            macs,
+            LIMITS[2],
+            scal,
+            *arrived[g][-n:],
+            hidden,
+            *downs,
+        )
+    terms = [downs[1], swap_core(downs[0]), ins[1], swap_core(ins[0])]
     returned = [
         call(
             functools.partial(returned_body, cap),
@@ -334,21 +365,40 @@
         for pair in pairs
     ]
     rows = ff // ndp + width // ndp * 2 * ff // width
+    by_z = lambda x: pl.BlockSpec((1,) + x.shape[1:], lambda k, scal: (k, 0, 0))
+    packed = bf(nz, rows, width)
     (total,) = call(
-        functools.partial(pack_body, nz), [bf(nz, rows, width)], 1, LIMITS[6], scal, *terms
+        pack_body,
+        [packed],
+        1,
+        LIMITS[6],
+        scal,
+        *terms,
+        specs=[by_z(x) for x in terms],
+        out_specs=[by_z(packed)],
+        steps=nz,
     )
     total = lax.all_to_all(total, "dp", 0, 0, tiled=True, axis_index_groups=same_core)
     sets = [[k for k in range(nz) if expert_of(k) == e] for e in range(experts)]
+    members = jnp.array(sets, jnp.int32).reshape(-1)
+    many = len(sets[0])
+    by_expert = lambda *shape: pl.BlockSpec((1,) + shape, lambda e, scal: (e, 0, 0))
     grad_in, grad_down = call(
-        functools.partial(unpack_body, sets),
+        unpack_body,
         [
             jax.ShapeDtypeStruct((experts, width // ndp, 2 * ff), F32),
             jax.ShapeDtypeStruct((experts, ff // ndp, width), F32),
         ],
         1,
         LIMITS[6],
-        scal,
-        total,
+        members,
+        *[total] * many,
+        specs=[
+            pl.BlockSpec((1,) + total.shape[1:], lambda e, scal, m=m: (scal[e * many + m], 0, 0))
+            for m in range(many)
+        ],
+        out_specs=[by_expert(width // ndp, 2 * ff), by_expert(ff // ndp, width)],
+        steps=experts,
     )
     sums = []
     for sent, back in zip(returned, backs):

time: 131 us -> 128 us (0.977)
  waiting for transfers between devices: 61.8 us -> 59.1 us
  starting transfers between devices: 30.3 us -> 28.3 us
    ppermute x2 -> x3, waiting for transfers between devices: 29.7 us -> 19.5 us  [per_device(): lax.ppermute(x, 'dp', [(i, i ^ 2 * k) for i in range(ndp)])]
    ppermute x15, waiting for transfers between devices: 26.7 us -> 34.3 us  [per_device(): lax.ppermute(x, 'expert', [(i, i ^ j) for i in range(n)])]
    unnamed x18 -> x22, local copies, waits for them, and re-layouts: 7.52 us -> 8.44 us
    pallas_call x14 -> x17, Pallas kernels: 29.4 us -> 30 us  [call(): return pl.pallas_call(body, **params)(scal, *args)]
    ppermute x2 -> x3, starting transfers between devices: 4.89 us -> 4.75 us  [per_device(): lax.ppermute(x, 'dp', [(i, i ^ 2 * k) for i in range(ndp)])]
  transfers between devices with their start and end apart: 20 -> 21, of which waited for: 11 -> 11; matrix products, arithmetic and copies ran while one was open for 1% -> 1% of each run, Pallas kernels for 13% -> 16%
where the time goes in v5:
time: 128 us
  waiting for transfers between devices  59.1 us (46%)
  Pallas kernels  30 us (23%)
  starting transfers between devices  28.3 us (22%)
  local copies, waits for them, and re-layouts  8.52 us (7%)
    ppermute x15, waiting for transfers between devices, per_device(): lax.ppermute(x, 'expert', [(i, i ^ j) for i in range(n)])  34.3 us
    pallas_call x17, Pallas kernels, call(): return pl.pallas_call(body, **params)(scal, *args)  30 us
    ppermute x3, waiting for transfers between devices, per_device(): lax.ppermute(x, 'dp', [(i, i ^ 2 * k) for i in range(ndp)])  19.5 us
    ppermute x15, starting transfers between devices, per_device(): lax.ppermute(x, 'expert', [(i, i ^ j) for i in range(n)])  19 us
    unnamed x22, local copies, waits for them, and re-layouts  8.44 us
    ppermute x3, starting transfers between devices, per_device(): lax.ppermute(x, 'dp', [(i, i ^ 2 * k) for i in range(ndp)])  4.75 us
    all_to_all x1, starting transfers between devices, per_device(): lax.all_to_all(total, 'dp', 0, 0, tiled=True, axis_index_groups=same_core)  3.87 us
    all_to_all x1, waiting for transfers between devices, per_device(): lax.all_to_all(total, 'dp', 0, 0, tiled=True, axis_index_groups=same_core)  3.41 us
  transfers between devices with their start and end apart: 21, of which 11 were waited for; matrix products, arithmetic and copies ran while one was open for 1% of the time, Pallas kernels for 16%

profile of v5, /device:TPU:0, one launch (start us, length us, event | category | flops | bytes accessed | tf_op | source)
XLA Modules:
  0.0 127.8 jit_solution(9447141843384186576)
XLA Ops:
  0.7 2.5 %shard_map.103 = (bf16[128,2048]{1,0:T(8,128)(2,1)S(1)}, bf16[128,2048]{1,0:T(8,128)(2,1)S(1)}, bf16[128,2048]{1,0:T(8,128)(2,1)S(1)}, bf16[128,2048]{1,0:T(8,12...) custom-call(s32[10]{0:T(128)S(1)} %stack.43.scal, f32[2,256]{1,0:T(2,128)} %bitcast.15, ...), custom_call_target="tpu_custom_call" | custom-call | flops 201326592 | bytes 201326 | tf_op jit(solution)/shard_map/pallas_call | solution.py:55
  3.3 3.1 %collective-permute-start.6 = (bf16[272,1024]{1,0:T(8,128)(2,1)S(1)}, bf16[272,1024]{1,0:T(8,128)(2,1)S(1)}, u32[]{:S(2)}, u32[]{:S(2)}) collective-permute-start(bf16[272,1024]{1,0:T(8,128)(2,1)S(1)} %get-tuple-element.55), channel_id=1, source_target_pairs={{0,8},{4,12},{8,0},{12,4},{16,24},{20,28},{24,16},{28,20},{1,9},{5... | collective-permute-start | bytes 1671176 | tf_op jit(solution)/shard_map/ppermute | solution.py:260
  6.4 1.5 %collective-permute-start = (bf16[128,2048]{1,0:T(8,128)(2,1)S(1)}, bf16[128,2048]{1,0:T(8,128)(2,1)S(1)}, u32[]{:S(2)}, u32[]{:S(2)}) collective-permute-start(bf16[128,2048]{1,0:T(8,128)(2,1)S(1)} %get-tuple-element.46), channel_id=1, source_target_pairs={{0,1},{1,0},{2,3},{3,2},{4,5},{5,4},{6,7},{7,6},{8,9},{9,8},{10,11... | collective-permute-start | bytes 1572872 | tf_op jit(solution)/shard_map/ppermute | solution.py:261
  7.9 1.5 %collective-permute-start.1 = (bf16[128,2048]{1,0:T(8,128)(2,1)S(1)}, bf16[128,2048]{1,0:T(8,128)(2,1)S(1)}, u32[]{:S(2)}, u32[]{:S(2)}) collective-permute-start(bf16[128,2048]{1,0:T(8,128)(2,1)S(1)} %get-tuple-element.47), channel_id=1, source_target_pairs={{0,2},{1,3},{2,0},{3,1},{4,6},{5,7},{6,4},{7,5},{8,10},{9,11},{10,... | collective-permute-start | bytes 1572872 | tf_op jit(solution)/shard_map/ppermute | solution.py:261
  10.0 9.9 %collective-permute-done.6.block = bf16[272,1024]{1,0:T(8,128)(2,1)S(1)} collective-permute-done((bf16[272,1024]{1,0:T(8,128)(2,1)S(1)}, bf16[272,1024]{1,0:T(8,128)(2,1)S(1)}, u32[]{:S(2)}, u32[]{:S(2)}) %collective-permute-start.6) | collective-permute-done | bytes 557088 | tf_op jit(solution)/shard_map/ppermute | solution.py:260
  19.8 1.0 shard_map.108
  20.8 2.0 %collective-permute-start.11 = (bf16[128,1024]{1,0:T(8,128)(2,1)S(1)}, bf16[128,1024]{1,0:T(8,128)(2,1)S(1)}, u32[]{:S(2)}, u32[]{:S(2)}) collective-permute-start(bf16[128,1024]{1,0:T(8,128)(2,1)S(1)} %get-tuple-element.62), channel_id=1, source_target_pairs={{0,1},{1,0},{2,3},{3,2},{4,5},{5,4},{6,7},{7,6},{8,9},{9,8},{10,11... | collective-permute-start | bytes 786440 | tf_op jit(solution)/shard_map/ppermute | solution.py:261
  22.9 1.5 %collective-permute-start.12 = (bf16[128,1024]{1,0:T(8,128)(2,1)S(1)}, bf16[128,1024]{1,0:T(8,128)(2,1)S(1)}, u32[]{:S(2)}, u32[]{:S(2)}) collective-permute-start(bf16[128,1024]{1,0:T(8,128)(2,1)S(1)} %get-tuple-element.63), channel_id=1, source_target_pairs={{0,2},{1,3},{2,0},{3,1},{4,6},{5,7},{6,4},{7,5},{8,10},{9,11},{10,... | collective-permute-start | bytes 786440 | tf_op jit(solution)/shard_map/ppermute | solution.py:261
  24.4 8.0 %collective-permute-done.1.refs_2_ = bf16[128,2048]{1,0:T(8,128)(2,1)S(1)} collective-permute-done((bf16[128,2048]{1,0:T(8,128)(2,1)S(1)}, bf16[128,2048]{1,0:T(8,128)(2,1)S(1)}, u32[]{:S(2)}, u32[]{:S(2)}) %collective-permute-start.1) | collective-permute-done | bytes 524320 | tf_op jit(solution)/shard_map/ppermute | solution.py:261
  32.8 0.7 collective-permute-done.2.refs_3_
  33.5 2.8 %copy-done = bf16[2,1024,1536]{2,1,0:T(8,128)(2,1)S(1)} copy-done((bf16[2,1024,1536]{2,1,0:T(8,128)(2,1)S(1)}, bf16[2,1024,1536]{2,1,0:T(8,128)(2,1)}, u32[]{:S(2)}) %copy-start) | copy-done | bytes 6291480
  36.3 2.5 %shard_map.104 = (bf16[1024,512]{1,0:T(8,128)(2,1)S(1)}, bf16[768,512]{1,0:T(8,128)(2,1)S(1)}, bf16[512,768]{1,0:T(8,128)(2,1)S(1)}, bf16[512,768]{1,0:T(8,128)(2,1)S(1)}) custom-call(s32[10]{0:T(128)S(1)} %stack.43.scal, bf16[128,2048]{1,0:T(8,128)(2,1)S(1)} %get-tuple-element.45.refs_0_, bf16[128,2048]{1,0:T(8,128)(2,1)S(1)} %collective-permute-done.refs_1_, ...), custom_call_target="tpu_custom_call" | custom-call | flops 1610612736 | bytes 1610612 | tf_op jit(solution)/shard_map/pallas_call | solution.py:55
  38.8 1.6 %shard_map.105.pair = bf16[512,1536]{1,0:T(8,128)(2,1)S(1)} custom-call(s32[10]{0:T(128)S(1)} %stack.43.scal, bf16[128,2048]{1,0:T(8,128)(2,1)S(1)} %get-tuple-element.45.refs_0_, bf16[128,2048]{1,0:T(8,128)(2,1)S(1)} %collective-permute-done.refs_1_, bf16[128,2048]{1,0:T(8,128)(2,1)S(1)} %collective-permute-done.1.refs_2_, ...), custom_call_target="tpu_custom_call" | custom-call | flops 805306368 | bytes 805306 | tf_op jit(solution)/shard_map/pallas_call | solution.py:55
  40.4 1.0 shard_map.109
  41.4 2.9 %collective-permute-start.8 = (bf16[128,1024]{1,0:T(8,128)(2,1)S(1)}, bf16[128,1024]{1,0:T(8,128)(2,1)S(1)}, u32[]{:S(2)}, u32[]{:S(2)}) collective-permute-start(bf16[128,1024]{1,0:T(8,128)(2,1)S(1)} %get-tuple-element.58), channel_id=1, source_target_pairs={{0,1},{1,0},{2,3},{3,2},{4,5},{5,4},{6,7},{7,6},{8,9},{9,8},{10,11... | collective-permute-start | bytes 786440 | tf_op jit(solution)/shard_map/ppermute | solution.py:261
  44.4 1.5 %collective-permute-start.10 = (bf16[128,1024]{1,0:T(8,128)(2,1)S(1)}, bf16[128,1024]{1,0:T(8,128)(2,1)S(1)}, u32[]{:S(2)}, u32[]{:S(2)}) collective-permute-start(bf16[128,1024]{1,0:T(8,128)(2,1)S(1)} %get-tuple-element.60), channel_id=1, source_target_pairs={{0,3},{1,2},{2,1},{3,0},{4,7},{5,6},{6,5},{7,4},{8,11},{9,10},{10,... | collective-permute-start | bytes 786440 | tf_op jit(solution)/shard_map/ppermute | solution.py:261
  45.9 2.3 %shard_map.116 = (bf16[4,128,1536]{2,1,0:T(8,128)(2,1)S(1)}, bf16[4,128,1536]{2,1,0:T(8,128)(2,1)S(1)}) custom-call(s32[10]{0:T(128)S(1)} %stack.43.scal, bf16[1024,512]{1,0:T(8,128)(2,1)S(1)} %get-tuple-element.78.rows, bf16[512,1536]{1,0:T(8,128)(2,1)S(1)} %shard_map.105.pair), custom_call_target="tpu_custom_call" | custom-call | flops 1610612736 | bytes 1610612 | tf_op jit(solution)/shard_map/pallas_call | solution.py:55
  48.3 2.5 %shard_map.110 = (bf16[1024,512]{1,0:T(8,128)(2,1)S(1)}, bf16[768,512]{1,0:T(8,128)(2,1)S(1)}, bf16[512,768]{1,0:T(8,128)(2,1)S(1)}, bf16[512,768]{1,0:T(8,128)(2,1)S(1)}) custom-call(s32[10]{0:T(128)S(1)} %stack.43.scal, bf16[128,1024]{1,0:T(8,128)(2,1)S(1)} %get-tuple-element.61.refs_0_, bf16[128,1024]{1,0:T(8,128)(2,1)S(1)} %collective-permute-done.11.refs_1_, ...), custom_call_target="tpu_custom_call" | custom-call | flops 1610612736 | bytes 1610612 | tf_op jit(solution)/shard_map/pallas_call | solution.py:55
  50.8 4.7 %collective-permute-done.9.refs_2_ = bf16[128,1024]{1,0:T(8,128)(2,1)S(1)} collective-permute-done((bf16[128,1024]{1,0:T(8,128)(2,1)S(1)}, bf16[128,1024]{1,0:T(8,128)(2,1)S(1)}, u32[]{:S(2)}, u32[]{:S(2)}) %collective-permute-start.9) | collective-permute-done | bytes 262176 | tf_op jit(solution)/shard_map/ppermute | solution.py:261
  55.5 1.6 %shard_map.111.pair = bf16[512,1536]{1,0:T(8,128)(2,1)S(1)} custom-call(s32[10]{0:T(128)S(1)} %stack.43.scal, bf16[128,1024]{1,0:T(8,128)(2,1)S(1)} %get-tuple-element.57.refs_0_, bf16[128,1024]{1,0:T(8,128)(2,1)S(1)} %collective-permute-done.8.refs_1_, bf16[128,1024]{1,0:T(8,128)(2,1)S(1)} %collective-permute-done.9.refs_2_, ...), custom_call_target="tpu_custom_call" | custom-call | flops 805306368 | bytes 805306 | tf_op jit(solution)/shard_map/pallas_call | solution.py:55
  57.1 2.3 %shard_map.117 = (bf16[4,128,1536]{2,1,0:T(8,128)(2,1)S(1)}, bf16[4,128,1536]{2,1,0:T(8,128)(2,1)S(1)}) custom-call(s32[10]{0:T(128)S(1)} %stack.43.scal, bf16[1024,512]{1,0:T(8,128)(2,1)S(1)} %get-tuple-element.77.rows, bf16[512,1536]{1,0:T(8,128)(2,1)S(1)} %shard_map.111.pair, bf16[4,128,1536]{2,1,0:T(8,128)(2,1)S(1)} %get-tuple-element.79.refs_0_, ...), custom_call_target="tpu_custom_call" | custom-call | flops 1610612736 | bytes 1610612 | tf_op jit(solution)/shard_map/pallas_call | solution.py:55
  59.6 1.5 %shard_map.114 = (bf16[4,96,1024]{2,1,0:T(8,128)(2,1)S(1)}, bf16[4,96,1024]{2,1,0:T(8,128)(2,1)S(1)}) custom-call(s32[10]{0:T(128)S(1)} %stack.43.scal, bf16[128,2048]{1,0:T(8,128)(2,1)S(1)} %get-tuple-element.45.refs_0_, bf16[128,2048]{1,0:T(8,128)(2,1)S(1)} %collective-permute-done.refs_1_, bf16[128,2048]{1,0:T(8,128)(2,1)S(1)} %collective-permute-done.1.refs_2_, ...), custom_call_target="tpu_custom_call" | custom-call | flops 805306368 | bytes 805306 | tf_op jit(solution)/shard_map/pallas_call | solution.py:55
  61.1 1.5 %shard_map.115 = (bf16[4,96,1024]{2,1,0:T(8,128)(2,1)S(1)}, bf16[4,96,1024]{2,1,0:T(8,128)(2,1)S(1)}) custom-call(s32[10]{0:T(128)S(1)} %stack.43.scal, bf16[128,1024]{1,0:T(8,128)(2,1)S(1)} %get-tuple-element.57.refs_0_, bf16[128,1024]{1,0:T(8,128)(2,1)S(1)} %collective-permute-done.8.refs_1_, bf16[128,1024]{1,0:T(8,128)(2,1)S(1)} %collective-permute-done.9.refs_2_, ...), custom_call_target="tpu_custom_call" | custom-call | flops 805306368 | bytes 805306 | tf_op jit(solution)/shard_map/pallas_call | solution.py:55
  62.6 0.6 collective-permute-start.18
  63.2 1.9 %collective-permute-done.18.other_down = bf16[4,96,1024]{2,1,0:T(8,128)(2,1)S(1)} collective-permute-done((bf16[4,96,1024]{2,1,0:T(8,128)(2,1)S(1)}, bf16[4,96,1024]{2,1,0:T(8,128)(2,1)S(1)}, u32[]{:S(2)}, u32[]{:S(2)}) %collective-permute-start.18) | collective-permute-done | bytes 786464 | tf_op jit(solution)/shard_map/ppermute | solution.py:259
  65.1 0.8 shard_map.118
  66.0 1.4 %copy-done.3 = bf16[4,288,1024]{2,1,0:T(8,128)(2,1)} copy-done((bf16[4,288,1024]{2,1,0:T(8,128)(2,1)}, bf16[4,288,1024]{2,1,0:T(8,128)(2,1)S(1)}, u32[]{:S(2)}) %copy-start.3) | copy-done | bytes 2359320
  67.4 3.9 %all-to-all-start = ((bf16[4,288,1024]{2,1,0:T(8,128)(2,1)}), bf16[4,288,1024]{2,1,0:T(8,128)(2,1)S(1)}, u32[]{:S(2)}, u32[]{:S(2)}) async-start(bf16[4,288,1024]{2,1,0:T(8,128)(2,1)} %copy-done.3), calls=%async_computation | async-start | bytes 4718592 | tf_op jit(solution)/shard_map/all_to_all | solution.py:381
  71.3 2.8 %copy-done.1 = bf16[2,1024,1536]{2,1,0:T(8,128)(2,1)S(1)} copy-done((bf16[2,1024,1536]{2,1,0:T(8,128)(2,1)S(1)}, bf16[2,1024,1536]{2,1,0:T(8,128)(2,1)}, u32[]{:S(2)}) %copy-start.1) | copy-done | bytes 6291480
  74.1 1.4 %copy-done.7 = bf16[512,1536]{1,0:T(8,128)(2,1)S(1)} copy-done((bf16[512,1536]{1,0:T(8,128)(2,1)S(1)}, bf16[512,1536]{1,0:T(8,128)(2,1)}, u32[]{:S(2)}) %copy-start.7) | copy-done | bytes 1572888
  75.5 2.4 %shard_map.112 = (bf16[128,1024]{1,0:T(8,128)(2,1)S(1)}, bf16[128,1024]{1,0:T(8,128)(2,1)S(1)}, bf16[128,1024]{1,0:T(8,128)(2,1)S(1)}, bf16[128,1024]{1,0:T(8,128)(2,1)S(1)}) custom-call(s32[10]{0:T(128)S(1)} %stack.43.scal, bf16[512,1536]{1,0:T(8,128)(2,1)S(1)} %copy-done.7, bf16[2,1024,1536]{2,1,0:T(8,128)(2,1)S(1)} %copy-done.1), custom_call_target="tpu_custom_call" | custom-call | flops 1610612736 | bytes 1610612 | tf_op jit(solution)/shard_map/pallas_call | solution.py:55
  77.9 1.0 collective-permute-start.14
  79.2 2.2 %collective-permute-start.16 = (bf16[128,1024]{1,0:T(8,128)(2,1)S(1)}, bf16[128,1024]{1,0:T(8,128)(2,1)S(1)}, u32[]{:S(2)}, u32[]{:S(2)}) collective-permute-start(bf16[128,1024]{1,0:T(8,128)(2,1)S(1)} %get-tuple-element.70), channel_id=1, source_target_pairs={{0,3},{1,2},{2,1},{3,0},{4,7},{5,6},{6,5},{7,4},{8,11},{9,10},{10,... | collective-permute-start | bytes 786440 | tf_op jit(solution)/shard_map/ppermute | solution.py:261
  81.4 5.6 %collective-permute-done.14.refs_1_ = bf16[128,1024]{1,0:T(8,128)(2,1)S(1)} collective-permute-done((bf16[128,1024]{1,0:T(8,128)(2,1)S(1)}, bf16[128,1024]{1,0:T(8,128)(2,1)S(1)}, u32[]{:S(2)}, u32[]{:S(2)}) %collective-permute-start.14) | collective-permute-done | bytes 262176 | tf_op jit(solution)/shard_map/ppermute | solution.py:261
  87.1 5.7 %collective-permute-done.15.refs_2_ = bf16[128,1024]{1,0:T(8,128)(2,1)S(1)} collective-permute-done((bf16[128,1024]{1,0:T(8,128)(2,1)S(1)}, bf16[128,1024]{1,0:T(8,128)(2,1)S(1)}, u32[]{:S(2)}, u32[]{:S(2)}) %collective-permute-start.15) | collective-permute-done | bytes 262176 | tf_op jit(solution)/shard_map/ppermute | solution.py:261
  92.7 1.0 shard_map.113
  93.7 1.6 %collective-permute-start.17 = (bf16[256,1024]{1,0:T(8,128)(2,1)S(1)}, bf16[256,1024]{1,0:T(8,128)(2,1)S(1)}, u32[]{:S(2)}, u32[]{:S(2)}) collective-permute-start(bf16[256,1024]{1,0:T(8,128)(2,1)S(1)} %shard_map.113), channel_id=1, source_target_pairs={{0,8},{4,12},{8,0},{12,4},{16,24},{20,28},{24,16},{28,20},{1,9},{5... | collective-permute-start | bytes 1572872 | tf_op jit(solution)/shard_map/ppermute | solution.py:260
  95.3 2.4 %shard_map.106 = (bf16[128,1024]{1,0:T(8,128)(2,1)S(1)}, bf16[128,1024]{1,0:T(8,128)(2,1)S(1)}, bf16[128,1024]{1,0:T(8,128)(2,1)S(1)}, bf16[128,1024]{1,0:T(8,128)(2,1)S(1)}) custom-call(s32[10]{0:T(128)S(1)} %stack.43.scal, bf16[512,1536]{1,0:T(8,128)(2,1)S(1)} %copy-done.5, bf16[2,1024,1536]{2,1,0:T(8,128)(2,1)S(1)} %copy-done.1), custom_call_target="tpu_custom_call" | custom-call | flops 1610612736 | bytes 1610612 | tf_op jit(solution)/shard_map/pallas_call | solution.py:55
  97.7 1.2 collective-permute-start.3
  98.8 0.7 collective-permute-start.4
  99.5 1.7 %collective-permute-start.5 = (bf16[128,1024]{1,0:T(8,128)(2,1)S(1)}, bf16[128,1024]{1,0:T(8,128)(2,1)S(1)}, u32[]{:S(2)}, u32[]{:S(2)}) collective-permute-start(bf16[128,1024]{1,0:T(8,128)(2,1)S(1)} %get-tuple-element.54), channel_id=1, source_target_pairs={{0,3},{1,2},{2,1},{3,0},{4,7},{5,6},{6,5},{7,4},{8,11},{9,10},{10,... | collective-permute-start | bytes 786440 | tf_op jit(solution)/shard_map/ppermute | solution.py:261
  101.2 5.8 %collective-permute-done.3.refs_1_ = bf16[128,1024]{1,0:T(8,128)(2,1)S(1)} collective-permute-done((bf16[128,1024]{1,0:T(8,128)(2,1)S(1)}, bf16[128,1024]{1,0:T(8,128)(2,1)S(1)}, u32[]{:S(2)}, u32[]{:S(2)}) %collective-permute-start.3) | collective-permute-done | bytes 262176 | tf_op jit(solution)/shard_map/ppermute | solution.py:261
  107.0 3.9 %collective-permute-done.4.refs_2_ = bf16[128,1024]{1,0:T(8,128)(2,1)S(1)} collective-permute-done((bf16[128,1024]{1,0:T(8,128)(2,1)S(1)}, bf16[128,1024]{1,0:T(8,128)(2,1)S(1)}, u32[]{:S(2)}, u32[]{:S(2)}) %collective-permute-start.4) | collective-permute-done | bytes 262176 | tf_op jit(solution)/shard_map/ppermute | solution.py:261
  110.8 1.0 shard_map.107
  111.8 9.6 %collective-permute-done.17 = bf16[256,1024]{1,0:T(8,128)(2,1)S(1)} collective-permute-done((bf16[256,1024]{1,0:T(8,128)(2,1)S(1)}, bf16[256,1024]{1,0:T(8,128)(2,1)S(1)}, u32[]{:S(2)}, u32[]{:S(2)}) %collective-permute-start.17) | collective-permute-done | bytes 524320 | tf_op jit(solution)/shard_map/ppermute | solution.py:260
  121.4 1.0 add_convert_fusion
  122.4 3.4 %all-to-all-done.refs_0_.refs_1_ = bf16[4,288,1024]{2,1,0:T(8,128)(2,1)S(1)} async-done(((bf16[4,288,1024]{2,1,0:T(8,128)(2,1)}), bf16[4,288,1024]{2,1,0:T(8,128)(2,1)S(1)}, u32[]{:S(2)}, u32[]{:S(2)}) %all-to-all-start) | async-done | bytes 2359328 | tf_op jit(solution)/shard_map/all_to_all | solution.py:381
  125.8 2.0 %shard_map.119 = (f32[2,128,1536]{2,1,0:T(8,128)}, f32[2,96,1024]{2,1,0:T(8,128)}) custom-call(s32[4]{0:T(128)S(1)} %copy-done.8, bf16[4,288,1024]{2,1,0:T(8,128)(2,1)S(1)} %all-to-all-done.refs_0_.refs_1_, bf16[4,288,1024]{2,1,0:T(8,128)(2,1)S(1)} %all-to-all-done.refs_0_.refs_1_), custom_call_target="tpu_custom_call" | custom-call | flops 1 | tf_op jit(solution)/shard_map/pallas_call | solution.py:55
  (36 shorter events, 1.6 us)
Async XLA Ops:
  3.3 16.5 %collective-permute-start.6 = (bf16[272,1024]{1,0:T(8,128)(2,1)S(1)}, bf16[272,1024]{1,0:T(8,128)(2,1)S(1)}, u32[]{:S(2)}, u32[]{:S(2)}) collective-permute-start(bf16[272,1024]{1,0:T(8,128)(2,1)S(1)} %get-tuple-element.55), channel_id=1, source_target_pairs={{0,8},{4,12},{8,0},{12,4},{16,24},{20,28},{24,16},{28,20},{1,9},{5... | collective-permute-start | bytes 1671176 | tf_op jit(solution)/shard_map/ppermute | solution.py:260
  6.4 16.5 %collective-permute-start = (bf16[128,2048]{1,0:T(8,128)(2,1)S(1)}, bf16[128,2048]{1,0:T(8,128)(2,1)S(1)}, u32[]{:S(2)}, u32[]{:S(2)}) collective-permute-start(bf16[128,2048]{1,0:T(8,128)(2,1)S(1)} %get-tuple-element.46), channel_id=1, source_target_pairs={{0,1},{1,0},{2,3},{3,2},{4,5},{5,4},{6,7},{7,6},{8,9},{9,8},{10,11... | collective-permute-start | bytes 1572872 | tf_op jit(solution)/shard_map/ppermute | solution.py:261
  7.9 24.5 %collective-permute-start.1 = (bf16[128,2048]{1,0:T(8,128)(2,1)S(1)}, bf16[128,2048]{1,0:T(8,128)(2,1)S(1)}, u32[]{:S(2)}, u32[]{:S(2)}) collective-permute-start(bf16[128,2048]{1,0:T(8,128)(2,1)S(1)} %get-tuple-element.47), channel_id=1, source_target_pairs={{0,2},{1,3},{2,0},{3,1},{4,6},{5,7},{6,4},{7,5},{8,10},{9,11},{10,... | collective-permute-start | bytes 1572872 | tf_op jit(solution)/shard_map/ppermute | solution.py:261
  9.4 24.1 %collective-permute-start.2 = (bf16[128,2048]{1,0:T(8,128)(2,1)S(1)}, bf16[128,2048]{1,0:T(8,128)(2,1)S(1)}, u32[]{:S(2)}, u32[]{:S(2)}) collective-permute-start(bf16[128,2048]{1,0:T(8,128)(2,1)S(1)} %get-tuple-element.48), channel_id=1, source_target_pairs={{0,3},{1,2},{2,1},{3,0},{4,7},{5,6},{6,5},{7,4},{8,11},{9,10},{10,... | collective-permute-start | bytes 1572872 | tf_op jit(solution)/shard_map/ppermute | solution.py:261
  9.9 30.5 %collective-permute-start.7 = (bf16[256,1024]{1,0:T(8,128)(2,1)}, bf16[256,1024]{1,0:T(8,128)(2,1)S(1)}, u32[]{:S(2)}, u32[]{:S(2)}) collective-permute-start(bf16[256,1024]{1,0:T(8,128)(2,1)} %cotangent.1), channel_id=1, source_target_pairs={{0,8},{4,12},{8,0},{12,4},{16,24},{20,28},{24,16},{28,20},{1,9},{5... | collective-permute-start | bytes 1572872 | tf_op jit(solution)/shard_map/ppermute | solution.py:260
  20.8 23.5 %collective-permute-start.11 = (bf16[128,1024]{1,0:T(8,128)(2,1)S(1)}, bf16[128,1024]{1,0:T(8,128)(2,1)S(1)}, u32[]{:S(2)}, u32[]{:S(2)}) collective-permute-start(bf16[128,1024]{1,0:T(8,128)(2,1)S(1)} %get-tuple-element.62), channel_id=1, source_target_pairs={{0,1},{1,0},{2,3},{3,2},{4,5},{5,4},{6,7},{7,6},{8,9},{9,8},{10,11... | collective-permute-start | bytes 786440 | tf_op jit(solution)/shard_map/ppermute | solution.py:261
  22.9 25.4 %collective-permute-start.12 = (bf16[128,1024]{1,0:T(8,128)(2,1)S(1)}, bf16[128,1024]{1,0:T(8,128)(2,1)S(1)}, u32[]{:S(2)}, u32[]{:S(2)}) collective-permute-start(bf16[128,1024]{1,0:T(8,128)(2,1)S(1)} %get-tuple-element.63), channel_id=1, source_target_pairs={{0,2},{1,3},{2,0},{3,1},{4,6},{5,7},{6,4},{7,5},{8,10},{9,11},{10,... | collective-permute-start | bytes 786440 | tf_op jit(solution)/shard_map/ppermute | solution.py:261
  32.4 15.9 %collective-permute-start.13 = (bf16[128,1024]{1,0:T(8,128)(2,1)S(1)}, bf16[128,1024]{1,0:T(8,128)(2,1)S(1)}, u32[]{:S(2)}, u32[]{:S(2)}) collective-permute-start(bf16[128,1024]{1,0:T(8,128)(2,1)S(1)} %get-tuple-element.64), channel_id=1, source_target_pairs={{0,3},{1,2},{2,1},{3,0},{4,7},{5,6},{6,5},{7,4},{8,11},{9,10},{10,... | collective-permute-start | bytes 786440 | tf_op jit(solution)/shard_map/ppermute | solution.py:261
  33.5 2.8 %copy-start = (bf16[2,1024,1536]{2,1,0:T(8,128)(2,1)S(1)}, bf16[2,1024,1536]{2,1,0:T(8,128)(2,1)}, u32[]{:S(2)}) copy-start(bf16[2,1024,1536]{2,1,0:T(8,128)(2,1)} %w_in.3) | copy-start | bytes 18874372
  36.3 2.5 %copy-start.2 = (bf16[2,768,1024]{2,1,0:T(8,128)(2,1)S(1)}, bf16[2,768,1024]{2,1,0:T(8,128)(2,1)}, u32[]{:S(2)}) copy-start(bf16[2,768,1024]{2,1,0:T(8,128)(2,1)} %refs_4_.7) | copy-start | bytes 9437188
  36.3 12.0 %slice-start = ((s8[6291456]{0:T(1024)(128)(4,1)}), s8[2097152]{0:T(1024)(128)(4,1)S(1)}, s32[]{:S(2)}) async-start(s8[6291456]{0:T(1024)(128)(4,1)} %bitcast.13), calls=%async_computation.1 | async-start | bytes 4194304
  38.8 9.5 %slice-start.1 = ((s8[6291456]{0:T(1024)(128)(4,1)}), s8[4194304]{0:T(1024)(128)(4,1)S(1)}, s32[]{:S(2)}) async-start(s8[6291456]{0:T(1024)(128)(4,1)} %bitcast.13), calls=%async_computation.2 | async-start | bytes 8388608
  40.4 7.8 %copy-start.4 = (bf16[512,1536]{1,0:T(8,128)(2,1)}, bf16[512,1536]{1,0:T(8,128)(2,1)S(1)}, u32[]{:S(2)}) copy-start(bf16[512,1536]{1,0:T(8,128)(2,1)S(1)} %shard_map.105.pair) | copy-start | bytes 4718596
  41.4 9.3 %collective-permute-start.8 = (bf16[128,1024]{1,0:T(8,128)(2,1)S(1)}, bf16[128,1024]{1,0:T(8,128)(2,1)S(1)}, u32[]{:S(2)}, u32[]{:S(2)}) collective-permute-start(bf16[128,1024]{1,0:T(8,128)(2,1)S(1)} %get-tuple-element.58), channel_id=1, source_target_pairs={{0,1},{1,0},{2,3},{3,2},{4,5},{5,4},{6,7},{7,6},{8,9},{9,8},{10,11... | collective-permute-start | bytes 786440 | tf_op jit(solution)/shard_map/ppermute | solution.py:261
  44.3 11.1 %collective-permute-start.9 = (bf16[128,1024]{1,0:T(8,128)(2,1)S(1)}, bf16[128,1024]{1,0:T(8,128)(2,1)S(1)}, u32[]{:S(2)}, u32[]{:S(2)}) collective-permute-start(bf16[128,1024]{1,0:T(8,128)(2,1)S(1)} %get-tuple-element.59), channel_id=1, source_target_pairs={{0,2},{1,3},{2,0},{3,1},{4,6},{5,7},{6,4},{7,5},{8,10},{9,11},{10,... | collective-permute-start | bytes 786440 | tf_op jit(solution)/shard_map/ppermute | solution.py:261
  44.4 11.1 %collective-permute-start.10 = (bf16[128,1024]{1,0:T(8,128)(2,1)S(1)}, bf16[128,1024]{1,0:T(8,128)(2,1)S(1)}, u32[]{:S(2)}, u32[]{:S(2)}) collective-permute-start(bf16[128,1024]{1,0:T(8,128)(2,1)S(1)} %get-tuple-element.60), channel_id=1, source_target_pairs={{0,3},{1,2},{2,1},{3,0},{4,7},{5,6},{6,5},{7,4},{8,11},{9,10},{10,... | collective-permute-start | bytes 786440 | tf_op jit(solution)/shard_map/ppermute | solution.py:261
  57.1 2.4 %copy-start.6 = (bf16[512,1536]{1,0:T(8,128)(2,1)}, bf16[512,1536]{1,0:T(8,128)(2,1)S(1)}, u32[]{:S(2)}) copy-start(bf16[512,1536]{1,0:T(8,128)(2,1)S(1)} %shard_map.111.pair) | copy-start | bytes 4718596
  59.5 5.6 %collective-permute-start.19 = (bf16[4,128,1536]{2,1,0:T(8,128)(2,1)S(1)}, bf16[4,128,1536]{2,1,0:T(8,128)(2,1)S(1)}, u32[]{:S(2)}, u32[]{:S(2)}) collective-permute-start(bf16[4,128,1536]{2,1,0:T(8,128)(2,1)S(1)} %get-tuple-element.82), channel_id=1, source_target_pairs={{0,4},{4,0},{8,12},{12,8},{16,20},{20,16},{24,28},{28,24},{1,5},{5... | collective-permute-start | bytes 4718600 | tf_op jit(solution)/shard_map/ppermute | solution.py:259
  62.6 2.5 %collective-permute-start.18 = (bf16[4,96,1024]{2,1,0:T(8,128)(2,1)S(1)}, bf16[4,96,1024]{2,1,0:T(8,128)(2,1)S(1)}, u32[]{:S(2)}, u32[]{:S(2)}) collective-permute-start(bf16[4,96,1024]{2,1,0:T(8,128)(2,1)S(1)} %get-tuple-element.76), channel_id=1, source_target_pairs={{0,4},{4,0},{8,12},{12,8},{16,20},{20,16},{24,28},{28,24},{1,5},{5... | collective-permute-start | bytes 2359304 | tf_op jit(solution)/shard_map/ppermute | solution.py:259
  66.0 1.4 %copy-start.3 = (bf16[4,288,1024]{2,1,0:T(8,128)(2,1)}, bf16[4,288,1024]{2,1,0:T(8,128)(2,1)S(1)}, u32[]{:S(2)}) copy-start(bf16[4,288,1024]{2,1,0:T(8,128)(2,1)S(1)} %shard_map.118) | copy-start | bytes 7077892
  67.4 58.4 %all-to-all-start = ((bf16[4,288,1024]{2,1,0:T(8,128)(2,1)}), bf16[4,288,1024]{2,1,0:T(8,128)(2,1)S(1)}, u32[]{:S(2)}, u32[]{:S(2)}) async-start(bf16[4,288,1024]{2,1,0:T(8,128)(2,1)} %copy-done.3), calls=%async_computation | async-start | bytes 4718592 | tf_op jit(solution)/shard_map/all_to_all | solution.py:381
  71.3 2.8 %copy-start.1 = (bf16[2,1024,1536]{2,1,0:T(8,128)(2,1)S(1)}, bf16[2,1024,1536]{2,1,0:T(8,128)(2,1)}, u32[]{:S(2)}) copy-start(bf16[2,1024,1536]{2,1,0:T(8,128)(2,1)} %w_in.3) | copy-start | bytes 18874372
  74.1 1.4 %copy-start.7 = (bf16[512,1536]{1,0:T(8,128)(2,1)S(1)}, bf16[512,1536]{1,0:T(8,128)(2,1)}, u32[]{:S(2)}) copy-start(bf16[512,1536]{1,0:T(8,128)(2,1)} %copy-done.6) | copy-start | bytes 4718596
  77.8 17.4 %copy-start.5 = (bf16[512,1536]{1,0:T(8,128)(2,1)S(1)}, bf16[512,1536]{1,0:T(8,128)(2,1)}, u32[]{:S(2)}) copy-start(bf16[512,1536]{1,0:T(8,128)(2,1)} %copy-done.4) | copy-start | bytes 4718596
  77.9 9.2 %collective-permute-start.14 = (bf16[128,1024]{1,0:T(8,128)(2,1)S(1)}, bf16[128,1024]{1,0:T(8,128)(2,1)S(1)}, u32[]{:S(2)}, u32[]{:S(2)}) collective-permute-start(bf16[128,1024]{1,0:T(8,128)(2,1)S(1)} %get-tuple-element.68), channel_id=1, source_target_pairs={{0,1},{1,0},{2,3},{3,2},{4,5},{5,4},{6,7},{7,6},{8,9},{9,8},{10,11... | collective-permute-start | bytes 786440 | tf_op jit(solution)/shard_map/ppermute | solution.py:261
  78.8 13.9 %collective-permute-start.15 = (bf16[128,1024]{1,0:T(8,128)(2,1)S(1)}, bf16[128,1024]{1,0:T(8,128)(2,1)S(1)}, u32[]{:S(2)}, u32[]{:S(2)}) collective-permute-start(bf16[128,1024]{1,0:T(8,128)(2,1)S(1)} %get-tuple-element.69), channel_id=1, source_target_pairs={{0,2},{1,3},{2,0},{3,1},{4,6},{5,7},{6,4},{7,5},{8,10},{9,11},{10,... | collective-permute-start | bytes 786440 | tf_op jit(solution)/shard_map/ppermute | solution.py:261
  79.2 13.5 %collective-permute-start.16 = (bf16[128,1024]{1,0:T(8,128)(2,1)S(1)}, bf16[128,1024]{1,0:T(8,128)(2,1)S(1)}, u32[]{:S(2)}, u32[]{:S(2)}) collective-permute-start(bf16[128,1024]{1,0:T(8,128)(2,1)S(1)} %get-tuple-element.70), channel_id=1, source_target_pairs={{0,3},{1,2},{2,1},{3,0},{4,7},{5,6},{6,5},{7,4},{8,11},{9,10},{10,... | collective-permute-start | bytes 786440 | tf_op jit(solution)/shard_map/ppermute | solution.py:261
  93.7 27.7 %collective-permute-start.17 = (bf16[256,1024]{1,0:T(8,128)(2,1)S(1)}, bf16[256,1024]{1,0:T(8,128)(2,1)S(1)}, u32[]{:S(2)}, u32[]{:S(2)}) collective-permute-start(bf16[256,1024]{1,0:T(8,128)(2,1)S(1)} %shard_map.113), channel_id=1, source_target_pairs={{0,8},{4,12},{8,0},{12,4},{16,24},{20,28},{24,16},{28,20},{1,9},{5... | collective-permute-start | bytes 1572872 | tf_op jit(solution)/shard_map/ppermute | solution.py:260
  97.7 9.3 %collective-permute-start.3 = (bf16[128,1024]{1,0:T(8,128)(2,1)S(1)}, bf16[128,1024]{1,0:T(8,128)(2,1)S(1)}, u32[]{:S(2)}, u32[]{:S(2)}) collective-permute-start(bf16[128,1024]{1,0:T(8,128)(2,1)S(1)} %get-tuple-element.52), channel_id=1, source_target_pairs={{0,1},{1,0},{2,3},{3,2},{4,5},{5,4},{6,7},{7,6},{8,9},{9,8},{10,11... | collective-permute-start | bytes 786440 | tf_op jit(solution)/shard_map/ppermute | solution.py:261
  98.8 12.0 %collective-permute-start.4 = (bf16[128,1024]{1,0:T(8,128)(2,1)S(1)}, bf16[128,1024]{1,0:T(8,128)(2,1)S(1)}, u32[]{:S(2)}, u32[]{:S(2)}) collective-permute-start(bf16[128,1024]{1,0:T(8,128)(2,1)S(1)} %get-tuple-element.53), channel_id=1, source_target_pairs={{0,2},{1,3},{2,0},{3,1},{4,6},{5,7},{6,4},{7,5},{8,10},{9,11},{10,... | collective-permute-start | bytes 786440 | tf_op jit(solution)/shard_map/ppermute | solution.py:261
  99.5 11.3 %collective-permute-start.5 = (bf16[128,1024]{1,0:T(8,128)(2,1)S(1)}, bf16[128,1024]{1,0:T(8,128)(2,1)S(1)}, u32[]{:S(2)}, u32[]{:S(2)}) collective-permute-start(bf16[128,1024]{1,0:T(8,128)(2,1)S(1)} %get-tuple-element.54), channel_id=1, source_target_pairs={{0,3},{1,2},{2,1},{3,0},{4,7},{5,6},{6,5},{7,4},{8,11},{9,10},{10,... | collective-permute-start | bytes 786440 | tf_op jit(solution)/shard_map/ppermute | solution.py:261
  110.8 15.0 %copy-start.8 = (s32[4]{0:T(128)S(1)}, s32[4]{0:T(128)}, u32[]{:S(2)}) copy-start(s32[4]{0:T(128)} %constant.43.scal) | copy-start | bytes 52

commit v6 on v5

--- a/solution.py
+++ b/solution.py
@@ -154,13 +154,18 @@
         scale_up[:, pl.ds(f, tile)] = activated.astype(BF)
 
 
+def core_rows(sources, offset, nz, part):
+    taken = []
+    for shard in range(nz):
+        start = pl.multiple_of((2 * shard + offset) * part, 16)
+        taken.append(jnp.concatenate([x[pl.ds(start, part), :] for x in sources], axis=1))
+    return jnp.concatenate(taken, axis=0)
+
+
 def shard_rows(sources, scal, nz, part):
-    taken = []
-    for offset in (1 - scal[1], scal[1]):
-        for shard in range(nz):
-            start = pl.multiple_of((2 * shard + offset) * part, 16)
-            taken.append(jnp.concatenate([x[pl.ds(start, part), :] for x in sources], axis=1))
-    return jnp.concatenate(taken, axis=0)
+    return jnp.concatenate(
+        [core_rows(sources, offset, nz, part) for offset in (1 - scal[1], scal[1])], axis=0
+    )
 
 
 def pair_body(column, scal, *refs):
@@ -180,11 +185,15 @@
             out[k] = total.astype(BF)
 
 
-def down_body(n, nz, column, scal, *refs):
-    arrived, hidden, before, (give, keep) = refs[:n], refs[n], refs[n + 1 : -2], refs[-2:]
-    part, width = give.shape[1:]
-    left = shard_rows((hidden,), scal, nz, part)
-    put_shards(dot(left, stack_rows(arrived, column, width)), nz, part, before, give, keep)
+def down_body(n, nz, other, scal, *refs):
+    arrived, (hidden_a, hidden_b, out) = refs[: 2 * n], refs[2 * n :]
+    part, width = out.shape[1:]
+    slots = [stack_rows(arrived[:n], width, width), stack_rows(arrived[n:], 0, width)]
+    offset = 1 - scal[1] if other else scal[1]
+    left = core_rows((hidden_a, hidden_b), offset, nz, part)
+    result = dot(left, jnp.concatenate(slots, axis=0)).astype(BF)
+    for k in range(nz):
+        out[k] = result[k * part : (k + 1) * part]
 
 
 def input_weight_body(nz, scal, rows, pair, *refs):
@@ -316,6 +325,8 @@
     pairs = []
     for g, (column, scales) in enumerate(((width, scales_a), (0, scales_b))):
         pieces = arrived[g][-n:]
+        if g == 0:
+            pieces = [after(pieces[0], scaled[0])] + pieces[1:]
         args = pieces + [w_down] + scales
         pairs += call(
             functools.partial(pair_body, column),
@@ -327,7 +338,7 @@
             specs=[whole(x) for x in pieces] + [of_expert(w_down)] + [whole(x) for x in scales],
         )
 
-    ins, downs = [], []
+    ins = []
     for rows, pair in zip((rows_a, rows_b), pairs):
         ins = call(
             functools.partial(input_weight_body, nz),
@@ -339,17 +350,20 @@
             pair,
             *ins,
         )
-    for g, (column, hidden) in enumerate(((width, hidden_a), (0, hidden_b))):
-        downs = call(
-            functools.partial(down_body, n, nz, column),
-            [bf(nz, ff // ndp, width)] * 2,
+    downs = [
+        call(
+            functools.partial(down_body, n, nz, other),
+            [bf(nz, ff // ndp, width)],
             macs,
             LIMITS[2],
             scal,
-            *arrived[g][-n:],
-            hidden,
-            *downs,
-        )
+            *arrived[0],
+            *arrived[1][n:],
+            hidden_a,
+            hidden_b,
+        )[0]
+        for other in (1, 0)
+    ]
     terms = [downs[1], swap_core(downs[0]), ins[1], swap_core(ins[0])]
     returned = [
         call(

time: 128 us -> 126 us (0.984)
  waiting for transfers between devices: 59.1 us -> 57 us
    ppermute x15, waiting for transfers between devices: 34.3 us -> 32.9 us  [per_device(): lax.ppermute(x, 'expert', [(i, i ^ j) for i in range(n)])]
  transfers between devices with their start and end apart: 21 -> 21, of which waited for: 11 -> 12; matrix products, arithmetic and copies ran while one was open for 1% -> 1% of each run, Pallas kernels for 16% -> 16%
where the time goes in v6:
time: 126 us
  waiting for transfers between devices  57 us (45%)
  Pallas kernels  30 us (24%)
  starting transfers between devices  28.3 us (22%)
  local copies, waits for them, and re-layouts  8.52 us (7%)
    ppermute x15, waiting for transfers between devices, per_device(): lax.ppermute(x, 'expert', [(i, i ^ j) for i in range(n)])  32.9 us
    pallas_call x17, Pallas kernels, call(): return pl.pallas_call(body, **params)(scal, *args)  30 us
    ppermute x3, waiting for transfers between devices, per_device(): lax.ppermute(x, 'dp', [(i, i ^ 2 * k) for i in range(ndp)])  19.7 us
    ppermute x15, starting transfers between devices, per_device(): lax.ppermute(x, 'expert', [(i, i ^ j) for i in range(n)])  19.1 us
    unnamed x22, local copies, waits for them, and re-layouts  8.43 us
    ppermute x3, starting transfers between devices, per_device(): lax.ppermute(x, 'dp', [(i, i ^ 2 * k) for i in range(ndp)])  4.75 us
    all_to_all x1, starting transfers between devices, per_device(): lax.all_to_all(total, 'dp', 0, 0, tiled=True, axis_index_groups=same_core)  3.84 us
    all_to_all x1, waiting for transfers between devices, per_device(): lax.all_to_all(total, 'dp', 0, 0, tiled=True, axis_index_groups=same_core)  3.4 us
  transfers between devices with their start and end apart: 21, of which 12 were waited for; matrix products, arithmetic and copies ran while one was open for 1% of the time, Pallas kernels for 16%

profile of v6, /device:TPU:0, one launch (start us, length us, event | category | flops | bytes accessed | tf_op | source)
XLA Modules:
  0.0 125.8 jit_solution(15439202810190939273)
XLA Ops:
  0.7 2.5 %shard_map.103 = (bf16[128,2048]{1,0:T(8,128)(2,1)S(1)}, bf16[128,2048]{1,0:T(8,128)(2,1)S(1)}, bf16[128,2048]{1,0:T(8,128)(2,1)S(1)}, bf16[128,2048]{1,0:T(8,12...) custom-call(s32[10]{0:T(128)S(1)} %stack.43.scal, f32[2,256]{1,0:T(2,128)} %bitcast.15, ...), custom_call_target="tpu_custom_call" | custom-call | flops 201326592 | bytes 201326 | tf_op jit(solution)/shard_map/pallas_call | solution.py:55
  3.3 3.1 %collective-permute-start = (bf16[272,1024]{1,0:T(8,128)(2,1)S(1)}, bf16[272,1024]{1,0:T(8,128)(2,1)S(1)}, u32[]{:S(2)}, u32[]{:S(2)}) collective-permute-start(bf16[272,1024]{1,0:T(8,128)(2,1)S(1)} %get-tuple-element.43), channel_id=1, source_target_pairs={{0,8},{4,12},{8,0},{12,4},{16,24},{20,28},{24,16},{28,20},{1,9},{5... | collective-permute-start | bytes 1671176 | tf_op jit(solution)/shard_map/ppermute | solution.py:269
  6.4 1.5 %collective-permute-start.2 = (bf16[128,2048]{1,0:T(8,128)(2,1)S(1)}, bf16[128,2048]{1,0:T(8,128)(2,1)S(1)}, u32[]{:S(2)}, u32[]{:S(2)}) collective-permute-start(bf16[128,2048]{1,0:T(8,128)(2,1)S(1)} %get-tuple-element.46), channel_id=1, source_target_pairs={{0,1},{1,0},{2,3},{3,2},{4,5},{5,4},{6,7},{7,6},{8,9},{9,8},{10,11... | collective-permute-start | bytes 1572872 | tf_op jit(solution)/shard_map/ppermute | solution.py:270
  7.9 1.5 %collective-permute-start.3 = (bf16[128,2048]{1,0:T(8,128)(2,1)S(1)}, bf16[128,2048]{1,0:T(8,128)(2,1)S(1)}, u32[]{:S(2)}, u32[]{:S(2)}) collective-permute-start(bf16[128,2048]{1,0:T(8,128)(2,1)S(1)} %get-tuple-element.47), channel_id=1, source_target_pairs={{0,2},{1,3},{2,0},{3,1},{4,6},{5,7},{6,4},{7,5},{8,10},{9,11},{10,... | collective-permute-start | bytes 1572872 | tf_op jit(solution)/shard_map/ppermute | solution.py:270
  10.0 9.9 %collective-permute-done.block = bf16[272,1024]{1,0:T(8,128)(2,1)S(1)} collective-permute-done((bf16[272,1024]{1,0:T(8,128)(2,1)S(1)}, bf16[272,1024]{1,0:T(8,128)(2,1)S(1)}, u32[]{:S(2)}, u32[]{:S(2)}) %collective-permute-start) | collective-permute-done | bytes 557088 | tf_op jit(solution)/shard_map/ppermute | solution.py:269
  19.8 1.0 shard_map.109
  20.8 2.0 %collective-permute-start.11 = (bf16[128,1024]{1,0:T(8,128)(2,1)S(1)}, bf16[128,1024]{1,0:T(8,128)(2,1)S(1)}, u32[]{:S(2)}, u32[]{:S(2)}) collective-permute-start(bf16[128,1024]{1,0:T(8,128)(2,1)S(1)} %get-tuple-element.60), channel_id=1, source_target_pairs={{0,1},{1,0},{2,3},{3,2},{4,5},{5,4},{6,7},{7,6},{8,9},{9,8},{10,11... | collective-permute-start | bytes 786440 | tf_op jit(solution)/shard_map/ppermute | solution.py:270
  22.9 1.5 %collective-permute-start.12 = (bf16[128,1024]{1,0:T(8,128)(2,1)S(1)}, bf16[128,1024]{1,0:T(8,128)(2,1)S(1)}, u32[]{:S(2)}, u32[]{:S(2)}) collective-permute-start(bf16[128,1024]{1,0:T(8,128)(2,1)S(1)} %get-tuple-element.61), channel_id=1, source_target_pairs={{0,2},{1,3},{2,0},{3,1},{4,6},{5,7},{6,4},{7,5},{8,10},{9,11},{10,... | collective-permute-start | bytes 786440 | tf_op jit(solution)/shard_map/ppermute | solution.py:270
  24.4 8.0 %collective-permute-done.3.refs_2_ = bf16[128,2048]{1,0:T(8,128)(2,1)S(1)} collective-permute-done((bf16[128,2048]{1,0:T(8,128)(2,1)S(1)}, bf16[128,2048]{1,0:T(8,128)(2,1)S(1)}, u32[]{:S(2)}, u32[]{:S(2)}) %collective-permute-start.3) | collective-permute-done | bytes 524320 | tf_op jit(solution)/shard_map/ppermute | solution.py:270
  33.5 2.8 %copy-done = bf16[2,1024,1536]{2,1,0:T(8,128)(2,1)S(1)} copy-done((bf16[2,1024,1536]{2,1,0:T(8,128)(2,1)S(1)}, bf16[2,1024,1536]{2,1,0:T(8,128)(2,1)}, u32[]{:S(2)}) %copy-start) | copy-done | bytes 6291480
  36.3 2.5 %shard_map.105 = (bf16[1024,512]{1,0:T(8,128)(2,1)S(1)}, bf16[768,512]{1,0:T(8,128)(2,1)S(1)}, bf16[512,768]{1,0:T(8,128)(2,1)S(1)}, bf16[512,768]{1,0:T(8,128)(2,1)S(1)}) custom-call(s32[10]{0:T(128)S(1)} %stack.43.scal, bf16[128,2048]{1,0:T(8,128)(2,1)S(1)} %get-tuple-element.45.refs_0_, bf16[128,2048]{1,0:T(8,128)(2,1)S(1)} %collective-permute-done.2.refs_1_, ...), custom_call_target="tpu_custom_call" | custom-call | flops 1610612736 | bytes 1610612 | tf_op jit(solution)/shard_map/pallas_call | solution.py:55
  38.8 1.0 shard_map.104
  39.8 2.9 %collective-permute-start.8 = (bf16[128,1024]{1,0:T(8,128)(2,1)S(1)}, bf16[128,1024]{1,0:T(8,128)(2,1)S(1)}, u32[]{:S(2)}, u32[]{:S(2)}) collective-permute-start(bf16[128,1024]{1,0:T(8,128)(2,1)S(1)} %get-tuple-element.56), channel_id=1, source_target_pairs={{0,1},{1,0},{2,3},{3,2},{4,5},{5,4},{6,7},{7,6},{8,9},{9,8},{10,11... | collective-permute-start | bytes 786440 | tf_op jit(solution)/shard_map/ppermute | solution.py:270
  42.7 1.6 %shard_map.106.pair = bf16[512,1536]{1,0:T(8,128)(2,1)S(1)} custom-call(s32[10]{0:T(128)S(1)} %stack.43.scal, bf16[128,2048]{1,0:T(8,128)(2,1)S(1)} %get-tuple-element.45.refs_0_, bf16[128,2048]{1,0:T(8,128)(2,1)S(1)} %collective-permute-done.2.refs_1_, bf16[128,2048]{1,0:T(8,128)(2,1)S(1)} %collective-permute-done.3.refs_2_, ...), custom_call_target="tpu_custom_call" | custom-call | flops 805306368 | bytes 805306 | tf_op jit(solution)/shard_map/pallas_call | solution.py:55
  44.4 1.6 %collective-permute-start.10 = (bf16[128,1024]{1,0:T(8,128)(2,1)S(1)}, bf16[128,1024]{1,0:T(8,128)(2,1)S(1)}, u32[]{:S(2)}, u32[]{:S(2)}) collective-permute-start(bf16[128,1024]{1,0:T(8,128)(2,1)S(1)} %get-tuple-element.58), channel_id=1, source_target_pairs={{0,3},{1,2},{2,1},{3,0},{4,7},{5,6},{6,5},{7,4},{8,11},{9,10},{10,... | collective-permute-start | bytes 786440 | tf_op jit(solution)/shard_map/ppermute | solution.py:270
  46.0 2.3 %shard_map.116 = (bf16[4,128,1536]{2,1,0:T(8,128)(2,1)S(1)}, bf16[4,128,1536]{2,1,0:T(8,128)(2,1)S(1)}) custom-call(s32[10]{0:T(128)S(1)} %stack.43.scal, bf16[1024,512]{1,0:T(8,128)(2,1)S(1)} %get-tuple-element.72.rows, bf16[512,1536]{1,0:T(8,128)(2,1)S(1)} %shard_map.106.pair), custom_call_target="tpu_custom_call" | custom-call | flops 1610612736 | bytes 1610612 | tf_op jit(solution)/shard_map/pallas_call | solution.py:55
  48.4 2.5 %shard_map.110 = (bf16[1024,512]{1,0:T(8,128)(2,1)S(1)}, bf16[768,512]{1,0:T(8,128)(2,1)S(1)}, bf16[512,768]{1,0:T(8,128)(2,1)S(1)}, bf16[512,768]{1,0:T(8,128)(2,1)S(1)}) custom-call(s32[10]{0:T(128)S(1)} %stack.43.scal, bf16[128,1024]{1,0:T(8,128)(2,1)S(1)} %get-tuple-element.59.refs_0_, bf16[128,1024]{1,0:T(8,128)(2,1)S(1)} %collective-permute-done.11.refs_1_, ...), custom_call_target="tpu_custom_call" | custom-call | flops 1610612736 | bytes 1610612 | tf_op jit(solution)/shard_map/pallas_call | solution.py:55
  50.9 3.9 %collective-permute-done.9.refs_2_.refs_6_ = bf16[128,1024]{1,0:T(8,128)(2,1)S(1)} collective-permute-done((bf16[128,1024]{1,0:T(8,128)(2,1)S(1)}, bf16[128,1024]{1,0:T(8,128)(2,1)S(1)}, u32[]{:S(2)}, u32[]{:S(2)}) %collective-permute-start.9) | collective-permute-done | bytes 262176 | tf_op jit(solution)/shard_map/ppermute | solution.py:270
  54.7 1.6 %shard_map.111.pair = bf16[512,1536]{1,0:T(8,128)(2,1)S(1)} custom-call(s32[10]{0:T(128)S(1)} %stack.43.scal, bf16[128,1024]{1,0:T(8,128)(2,1)S(1)} %get-tuple-element.44.refs_0_.refs_4_, bf16[128,1024]{1,0:T(8,128)(2,1)S(1)} %collective-permute-done.8.refs_1_.refs_5_, bf16[128,1024]{1,0:T(8,128)(2,1)S(1)} %collective-permute-done.9.refs_2_.refs_6_, ...), custom_call_target="tpu_custom_call" | custom-call | flops 805306368 | bytes 805306 | tf_op jit(solution)/shard_map/pallas_call | solution.py:55
  56.3 2.3 %shard_map.117 = (bf16[4,128,1536]{2,1,0:T(8,128)(2,1)S(1)}, bf16[4,128,1536]{2,1,0:T(8,128)(2,1)S(1)}) custom-call(s32[10]{0:T(128)S(1)} %stack.43.scal, bf16[1024,512]{1,0:T(8,128)(2,1)S(1)} %get-tuple-element.71.rows, bf16[512,1536]{1,0:T(8,128)(2,1)S(1)} %shard_map.111.pair, bf16[4,128,1536]{2,1,0:T(8,128)(2,1)S(1)} %get-tuple-element.73.refs_0_, ...), custom_call_target="tpu_custom_call" | custom-call | flops 1610612736 | bytes 1610612 | tf_op jit(solution)/shard_map/pallas_call | solution.py:55
  58.8 1.5 %shard_map.115 = bf16[4,96,1024]{2,1,0:T(8,128)(2,1)S(1)} custom-call(s32[10]{0:T(128)S(1)} %stack.43.scal, bf16[128,2048]{1,0:T(8,128)(2,1)S(1)} %get-tuple-element.45.refs_0_, bf16[128,2048]{1,0:T(8,128)(2,1)S(1)} %collective-permute-done.2.refs_1_, bf16[128,2048]{1,0:T(8,128)(2,1)S(1)} %collective-permute-done.3.refs_2_, ...), custom_call_target="tpu_custom_call" | custom-call | flops 805306368 | bytes 805306 | tf_op jit(solution)/shard_map/pallas_call | solution.py:55
  60.9 1.5 %shard_map.114.keep_down = bf16[4,96,1024]{2,1,0:T(8,128)(2,1)S(1)} custom-call(s32[10]{0:T(128)S(1)} %stack.43.scal, bf16[128,2048]{1,0:T(8,128)(2,1)S(1)} %get-tuple-element.45.refs_0_, bf16[128,2048]{1,0:T(8,128)(2,1)S(1)} %collective-permute-done.2.refs_1_, bf16[128,2048]{1,0:T(8,128)(2,1)S(1)} %collective-permute-done.3.refs_2_, ...), custom_call_target="tpu_custom_call" | custom-call | flops 805306368 | bytes 805306 | tf_op jit(solution)/shard_map/pallas_call | solution.py:55
  62.4 0.9 collective-permute-done.18.other_down
  63.3 0.9 shard_map.118
  64.2 1.4 %copy-done.3 = bf16[4,288,1024]{2,1,0:T(8,128)(2,1)} copy-done((bf16[4,288,1024]{2,1,0:T(8,128)(2,1)}, bf16[4,288,1024]{2,1,0:T(8,128)(2,1)S(1)}, u32[]{:S(2)}) %copy-start.3) | copy-done | bytes 2359320
  65.6 3.8 %all-to-all-start = ((bf16[4,288,1024]{2,1,0:T(8,128)(2,1)}), bf16[4,288,1024]{2,1,0:T(8,128)(2,1)S(1)}, u32[]{:S(2)}, u32[]{:S(2)}) async-start(bf16[4,288,1024]{2,1,0:T(8,128)(2,1)} %copy-done.3), calls=%async_computation | async-start | bytes 4718592 | tf_op jit(solution)/shard_map/all_to_all | solution.py:395
  69.5 2.8 %copy-done.1 = bf16[2,1024,1536]{2,1,0:T(8,128)(2,1)S(1)} copy-done((bf16[2,1024,1536]{2,1,0:T(8,128)(2,1)S(1)}, bf16[2,1024,1536]{2,1,0:T(8,128)(2,1)}, u32[]{:S(2)}) %copy-start.1) | copy-done | bytes 6291480
  72.2 1.4 %copy-done.7 = bf16[512,1536]{1,0:T(8,128)(2,1)S(1)} copy-done((bf16[512,1536]{1,0:T(8,128)(2,1)S(1)}, bf16[512,1536]{1,0:T(8,128)(2,1)}, u32[]{:S(2)}) %copy-start.7) | copy-done | bytes 1572888
  73.7 2.4 %shard_map.112 = (bf16[128,1024]{1,0:T(8,128)(2,1)S(1)}, bf16[128,1024]{1,0:T(8,128)(2,1)S(1)}, bf16[128,1024]{1,0:T(8,128)(2,1)S(1)}, bf16[128,1024]{1,0:T(8,128)(2,1)S(1)}) custom-call(s32[10]{0:T(128)S(1)} %stack.43.scal, bf16[512,1536]{1,0:T(8,128)(2,1)S(1)} %copy-done.7, bf16[2,1024,1536]{2,1,0:T(8,128)(2,1)S(1)} %copy-done.1), custom_call_target="tpu_custom_call" | custom-call | flops 1610612736 | bytes 1610612 | tf_op jit(solution)/shard_map/pallas_call | solution.py:55
  76.0 1.4 %collective-permute-start.14 = (bf16[128,1024]{1,0:T(8,128)(2,1)S(1)}, bf16[128,1024]{1,0:T(8,128)(2,1)S(1)}, u32[]{:S(2)}, u32[]{:S(2)}) collective-permute-start(bf16[128,1024]{1,0:T(8,128)(2,1)S(1)} %get-tuple-element.66), channel_id=1, source_target_pairs={{0,1},{1,0},{2,3},{3,2},{4,5},{5,4},{6,7},{7,6},{8,9},{9,8},{10,11... | collective-permute-start | bytes 786440 | tf_op jit(solution)/shard_map/ppermute | solution.py:270
  77.4 0.8 collective-permute-start.15
  78.1 1.4 %collective-permute-start.16 = (bf16[128,1024]{1,0:T(8,128)(2,1)S(1)}, bf16[128,1024]{1,0:T(8,128)(2,1)S(1)}, u32[]{:S(2)}, u32[]{:S(2)}) collective-permute-start(bf16[128,1024]{1,0:T(8,128)(2,1)S(1)} %get-tuple-element.68), channel_id=1, source_target_pairs={{0,3},{1,2},{2,1},{3,0},{4,7},{5,6},{6,5},{7,4},{8,11},{9,10},{10,... | collective-permute-start | bytes 786440 | tf_op jit(solution)/shard_map/ppermute | solution.py:270
  79.6 5.7 %collective-permute-done.14.refs_1_ = bf16[128,1024]{1,0:T(8,128)(2,1)S(1)} collective-permute-done((bf16[128,1024]{1,0:T(8,128)(2,1)S(1)}, bf16[128,1024]{1,0:T(8,128)(2,1)S(1)}, u32[]{:S(2)}, u32[]{:S(2)}) %collective-permute-start.14) | collective-permute-done | bytes 262176 | tf_op jit(solution)/shard_map/ppermute | solution.py:270
  85.3 1.0 collective-permute-done.15.refs_2_
  86.3 4.8 %collective-permute-done.16.refs_3_ = bf16[128,1024]{1,0:T(8,128)(2,1)S(1)} collective-permute-done((bf16[128,1024]{1,0:T(8,128)(2,1)S(1)}, bf16[128,1024]{1,0:T(8,128)(2,1)S(1)}, u32[]{:S(2)}, u32[]{:S(2)}) %collective-permute-start.16) | collective-permute-done | bytes 262176 | tf_op jit(solution)/shard_map/ppermute | solution.py:270
  91.1 1.0 shard_map.113
  92.0 1.6 %collective-permute-start.17 = (bf16[256,1024]{1,0:T(8,128)(2,1)S(1)}, bf16[256,1024]{1,0:T(8,128)(2,1)S(1)}, u32[]{:S(2)}, u32[]{:S(2)}) collective-permute-start(bf16[256,1024]{1,0:T(8,128)(2,1)S(1)} %shard_map.113), channel_id=1, source_target_pairs={{0,8},{4,12},{8,0},{12,4},{16,24},{20,28},{24,16},{28,20},{1,9},{5... | collective-permute-start | bytes 1572872 | tf_op jit(solution)/shard_map/ppermute | solution.py:269
  93.6 2.4 %shard_map.107 = (bf16[128,1024]{1,0:T(8,128)(2,1)S(1)}, bf16[128,1024]{1,0:T(8,128)(2,1)S(1)}, bf16[128,1024]{1,0:T(8,128)(2,1)S(1)}, bf16[128,1024]{1,0:T(8,128)(2,1)S(1)}) custom-call(s32[10]{0:T(128)S(1)} %stack.43.scal, bf16[512,1536]{1,0:T(8,128)(2,1)S(1)} %copy-done.5, bf16[2,1024,1536]{2,1,0:T(8,128)(2,1)S(1)} %copy-done.1), custom_call_target="tpu_custom_call" | custom-call | flops 1610612736 | bytes 1610612 | tf_op jit(solution)/shard_map/pallas_call | solution.py:55
  96.0 0.8 collective-permute-start.5
  96.8 1.5 %collective-permute-start.6 = (bf16[128,1024]{1,0:T(8,128)(2,1)S(1)}, bf16[128,1024]{1,0:T(8,128)(2,1)S(1)}, u32[]{:S(2)}, u32[]{:S(2)}) collective-permute-start(bf16[128,1024]{1,0:T(8,128)(2,1)S(1)} %get-tuple-element.53), channel_id=1, source_target_pairs={{0,2},{1,3},{2,0},{3,1},{4,6},{5,7},{6,4},{7,5},{8,10},{9,11},{10,... | collective-permute-start | bytes 786440 | tf_op jit(solution)/shard_map/ppermute | solution.py:270
  98.3 1.3 %collective-permute-start.7 = (bf16[128,1024]{1,0:T(8,128)(2,1)S(1)}, bf16[128,1024]{1,0:T(8,128)(2,1)S(1)}, u32[]{:S(2)}, u32[]{:S(2)}) collective-permute-start(bf16[128,1024]{1,0:T(8,128)(2,1)S(1)} %get-tuple-element.54), channel_id=1, source_target_pairs={{0,3},{1,2},{2,1},{3,0},{4,7},{5,6},{6,5},{7,4},{8,11},{9,10},{10,... | collective-permute-start | bytes 786440 | tf_op jit(solution)/shard_map/ppermute | solution.py:270
  99.6 5.8 %collective-permute-done.5.refs_1_ = bf16[128,1024]{1,0:T(8,128)(2,1)S(1)} collective-permute-done((bf16[128,1024]{1,0:T(8,128)(2,1)S(1)}, bf16[128,1024]{1,0:T(8,128)(2,1)S(1)}, u32[]{:S(2)}, u32[]{:S(2)}) %collective-permute-start.5) | collective-permute-done | bytes 262176 | tf_op jit(solution)/shard_map/ppermute | solution.py:270
  105.3 3.2 %collective-permute-done.6.refs_2_ = bf16[128,1024]{1,0:T(8,128)(2,1)S(1)} collective-permute-done((bf16[128,1024]{1,0:T(8,128)(2,1)S(1)}, bf16[128,1024]{1,0:T(8,128)(2,1)S(1)}, u32[]{:S(2)}, u32[]{:S(2)}) %collective-permute-start.6) | collective-permute-done | bytes 262176 | tf_op jit(solution)/shard_map/ppermute | solution.py:270
  108.5 1.0 shard_map.108
  109.5 9.9 %collective-permute-done.17 = bf16[256,1024]{1,0:T(8,128)(2,1)S(1)} collective-permute-done((bf16[256,1024]{1,0:T(8,128)(2,1)S(1)}, bf16[256,1024]{1,0:T(8,128)(2,1)S(1)}, u32[]{:S(2)}, u32[]{:S(2)}) %collective-permute-start.17) | collective-permute-done | bytes 524320 | tf_op jit(solution)/shard_map/ppermute | solution.py:269
  119.4 1.0 add_convert_fusion
  120.3 3.4 %all-to-all-done.refs_0_.refs_1_ = bf16[4,288,1024]{2,1,0:T(8,128)(2,1)S(1)} async-done(((bf16[4,288,1024]{2,1,0:T(8,128)(2,1)}), bf16[4,288,1024]{2,1,0:T(8,128)(2,1)S(1)}, u32[]{:S(2)}, u32[]{:S(2)}) %all-to-all-start) | async-done | bytes 2359328 | tf_op jit(solution)/shard_map/all_to_all | solution.py:395
  123.7 2.0 %shard_map.119 = (f32[2,128,1536]{2,1,0:T(8,128)}, f32[2,96,1024]{2,1,0:T(8,128)}) custom-call(s32[4]{0:T(128)S(1)} %copy-done.8, bf16[4,288,1024]{2,1,0:T(8,128)(2,1)S(1)} %all-to-all-done.refs_0_.refs_1_, bf16[4,288,1024]{2,1,0:T(8,128)(2,1)S(1)} %all-to-all-done.refs_0_.refs_1_), custom_call_target="tpu_custom_call" | custom-call | flops 1 | tf_op jit(solution)/shard_map/pallas_call | solution.py:55
  (36 shorter events, 2.4 us)
Async XLA Ops:
  3.3 16.5 %collective-permute-start = (bf16[272,1024]{1,0:T(8,128)(2,1)S(1)}, bf16[272,1024]{1,0:T(8,128)(2,1)S(1)}, u32[]{:S(2)}, u32[]{:S(2)}) collective-permute-start(bf16[272,1024]{1,0:T(8,128)(2,1)S(1)} %get-tuple-element.43), channel_id=1, source_target_pairs={{0,8},{4,12},{8,0},{12,4},{16,24},{20,28},{24,16},{28,20},{1,9},{5... | collective-permute-start | bytes 1671176 | tf_op jit(solution)/shard_map/ppermute | solution.py:269
  6.4 16.5 %collective-permute-start.2 = (bf16[128,2048]{1,0:T(8,128)(2,1)S(1)}, bf16[128,2048]{1,0:T(8,128)(2,1)S(1)}, u32[]{:S(2)}, u32[]{:S(2)}) collective-permute-start(bf16[128,2048]{1,0:T(8,128)(2,1)S(1)} %get-tuple-element.46), channel_id=1, source_target_pairs={{0,1},{1,0},{2,3},{3,2},{4,5},{5,4},{6,7},{7,6},{8,9},{9,8},{10,11... | collective-permute-start | bytes 1572872 | tf_op jit(solution)/shard_map/ppermute | solution.py:270
  7.9 24.5 %collective-permute-start.3 = (bf16[128,2048]{1,0:T(8,128)(2,1)S(1)}, bf16[128,2048]{1,0:T(8,128)(2,1)S(1)}, u32[]{:S(2)}, u32[]{:S(2)}) collective-permute-start(bf16[128,2048]{1,0:T(8,128)(2,1)S(1)} %get-tuple-element.47), channel_id=1, source_target_pairs={{0,2},{1,3},{2,0},{3,1},{4,6},{5,7},{6,4},{7,5},{8,10},{9,11},{10,... | collective-permute-start | bytes 1572872 | tf_op jit(solution)/shard_map/ppermute | solution.py:270
  9.4 24.1 %collective-permute-start.4 = (bf16[128,2048]{1,0:T(8,128)(2,1)S(1)}, bf16[128,2048]{1,0:T(8,128)(2,1)S(1)}, u32[]{:S(2)}, u32[]{:S(2)}) collective-permute-start(bf16[128,2048]{1,0:T(8,128)(2,1)S(1)} %get-tuple-element.48), channel_id=1, source_target_pairs={{0,3},{1,2},{2,1},{3,0},{4,7},{5,6},{6,5},{7,4},{8,11},{9,10},{10,... | collective-permute-start | bytes 1572872 | tf_op jit(solution)/shard_map/ppermute | solution.py:270
  9.9 28.9 %collective-permute-start.1 = (bf16[256,1024]{1,0:T(8,128)(2,1)}, bf16[256,1024]{1,0:T(8,128)(2,1)S(1)}, u32[]{:S(2)}, u32[]{:S(2)}) collective-permute-start(bf16[256,1024]{1,0:T(8,128)(2,1)} %cotangent.1), channel_id=1, source_target_pairs={{0,8},{4,12},{8,0},{12,4},{16,24},{20,28},{24,16},{28,20},{1,9},{5... | collective-permute-start | bytes 1572872 | tf_op jit(solution)/shard_map/ppermute | solution.py:269
  20.8 23.5 %collective-permute-start.11 = (bf16[128,1024]{1,0:T(8,128)(2,1)S(1)}, bf16[128,1024]{1,0:T(8,128)(2,1)S(1)}, u32[]{:S(2)}, u32[]{:S(2)}) collective-permute-start(bf16[128,1024]{1,0:T(8,128)(2,1)S(1)} %get-tuple-element.60), channel_id=1, source_target_pairs={{0,1},{1,0},{2,3},{3,2},{4,5},{5,4},{6,7},{7,6},{8,9},{9,8},{10,11... | collective-permute-start | bytes 786440 | tf_op jit(solution)/shard_map/ppermute | solution.py:270
  22.9 25.4 %collective-permute-start.12 = (bf16[128,1024]{1,0:T(8,128)(2,1)S(1)}, bf16[128,1024]{1,0:T(8,128)(2,1)S(1)}, u32[]{:S(2)}, u32[]{:S(2)}) collective-permute-start(bf16[128,1024]{1,0:T(8,128)(2,1)S(1)} %get-tuple-element.61), channel_id=1, source_target_pairs={{0,2},{1,3},{2,0},{3,1},{4,6},{5,7},{6,4},{7,5},{8,10},{9,11},{10,... | collective-permute-start | bytes 786440 | tf_op jit(solution)/shard_map/ppermute | solution.py:270
  32.4 16.0 %collective-permute-start.13 = (bf16[128,1024]{1,0:T(8,128)(2,1)S(1)}, bf16[128,1024]{1,0:T(8,128)(2,1)S(1)}, u32[]{:S(2)}, u32[]{:S(2)}) collective-permute-start(bf16[128,1024]{1,0:T(8,128)(2,1)S(1)} %get-tuple-element.62), channel_id=1, source_target_pairs={{0,3},{1,2},{2,1},{3,0},{4,7},{5,6},{6,5},{7,4},{8,11},{9,10},{10,... | collective-permute-start | bytes 786440 | tf_op jit(solution)/shard_map/ppermute | solution.py:270
  33.5 2.8 %copy-start = (bf16[2,1024,1536]{2,1,0:T(8,128)(2,1)S(1)}, bf16[2,1024,1536]{2,1,0:T(8,128)(2,1)}, u32[]{:S(2)}) copy-start(bf16[2,1024,1536]{2,1,0:T(8,128)(2,1)} %w_in.3) | copy-start | bytes 18874372
  36.3 6.5 %copy-start.2 = (bf16[2,768,1024]{2,1,0:T(8,128)(2,1)S(1)}, bf16[2,768,1024]{2,1,0:T(8,128)(2,1)}, u32[]{:S(2)}) copy-start(bf16[2,768,1024]{2,1,0:T(8,128)(2,1)} %refs_4_.7) | copy-start | bytes 9437188
  38.8 9.6 %slice-start = ((s8[6291456]{0:T(1024)(128)(4,1)}), s8[4194304]{0:T(1024)(128)(4,1)S(1)}, s32[]{:S(2)}) async-start(s8[6291456]{0:T(1024)(128)(4,1)} %bitcast.13), calls=%async_computation.1 | async-start | bytes 8388608
  39.8 11.0 %collective-permute-start.8 = (bf16[128,1024]{1,0:T(8,128)(2,1)S(1)}, bf16[128,1024]{1,0:T(8,128)(2,1)S(1)}, u32[]{:S(2)}, u32[]{:S(2)}) collective-permute-start(bf16[128,1024]{1,0:T(8,128)(2,1)S(1)} %get-tuple-element.56), channel_id=1, source_target_pairs={{0,1},{1,0},{2,3},{3,2},{4,5},{5,4},{6,7},{7,6},{8,9},{9,8},{10,11... | collective-permute-start | bytes 786440 | tf_op jit(solution)/shard_map/ppermute | solution.py:270
  42.7 12.0 %collective-permute-start.9 = (bf16[128,1024]{1,0:T(8,128)(2,1)S(1)}, bf16[128,1024]{1,0:T(8,128)(2,1)S(1)}, u32[]{:S(2)}, u32[]{:S(2)}) collective-permute-start(bf16[128,1024]{1,0:T(8,128)(2,1)S(1)} %get-tuple-element.57), channel_id=1, source_target_pairs={{0,2},{1,3},{2,0},{3,1},{4,6},{5,7},{6,4},{7,5},{8,10},{9,11},{10,... | collective-permute-start | bytes 786440 | tf_op jit(solution)/shard_map/ppermute | solution.py:270
  42.7 5.6 %slice-start.1 = ((s8[6291456]{0:T(1024)(128)(4,1)}), s8[2097152]{0:T(1024)(128)(4,1)S(1)}, s32[]{:S(2)}) async-start(s8[6291456]{0:T(1024)(128)(4,1)} %bitcast.13), calls=%async_computation.2 | async-start | bytes 4194304
  44.3 4.0 %copy-start.4 = (bf16[512,1536]{1,0:T(8,128)(2,1)}, bf16[512,1536]{1,0:T(8,128)(2,1)S(1)}, u32[]{:S(2)}) copy-start(bf16[512,1536]{1,0:T(8,128)(2,1)S(1)} %shard_map.106.pair) | copy-start | bytes 4718596
  44.4 10.4 %collective-permute-start.10 = (bf16[128,1024]{1,0:T(8,128)(2,1)S(1)}, bf16[128,1024]{1,0:T(8,128)(2,1)S(1)}, u32[]{:S(2)}, u32[]{:S(2)}) collective-permute-start(bf16[128,1024]{1,0:T(8,128)(2,1)S(1)} %get-tuple-element.58), channel_id=1, source_target_pairs={{0,3},{1,2},{2,1},{3,0},{4,7},{5,6},{6,5},{7,4},{8,11},{9,10},{10,... | collective-permute-start | bytes 786440 | tf_op jit(solution)/shard_map/ppermute | solution.py:270
  56.3 2.4 %copy-start.6 = (bf16[512,1536]{1,0:T(8,128)(2,1)}, bf16[512,1536]{1,0:T(8,128)(2,1)S(1)}, u32[]{:S(2)}) copy-start(bf16[512,1536]{1,0:T(8,128)(2,1)S(1)} %shard_map.111.pair) | copy-start | bytes 4718596
  58.7 4.6 %collective-permute-start.19 = (bf16[4,128,1536]{2,1,0:T(8,128)(2,1)S(1)}, bf16[4,128,1536]{2,1,0:T(8,128)(2,1)S(1)}, u32[]{:S(2)}, u32[]{:S(2)}) collective-permute-start(bf16[4,128,1536]{2,1,0:T(8,128)(2,1)S(1)} %get-tuple-element.76), channel_id=1, source_target_pairs={{0,4},{4,0},{8,12},{12,8},{16,20},{20,16},{24,28},{28,24},{1,5},{5... | collective-permute-start | bytes 4718600 | tf_op jit(solution)/shard_map/ppermute | solution.py:268
  60.3 3.0 %collective-permute-start.18 = (bf16[4,96,1024]{2,1,0:T(8,128)(2,1)S(1)}, bf16[4,96,1024]{2,1,0:T(8,128)(2,1)S(1)}, u32[]{:S(2)}, u32[]{:S(2)}) collective-permute-start(bf16[4,96,1024]{2,1,0:T(8,128)(2,1)S(1)} %shard_map.115), channel_id=1, source_target_pairs={{0,4},{4,0},{8,12},{12,8},{16,20},{20,16},{24,28},{28,24},{1,5},{5... | collective-permute-start | bytes 2359304 | tf_op jit(solution)/shard_map/ppermute | solution.py:268
  64.2 1.4 %copy-start.3 = (bf16[4,288,1024]{2,1,0:T(8,128)(2,1)}, bf16[4,288,1024]{2,1,0:T(8,128)(2,1)S(1)}, u32[]{:S(2)}) copy-start(bf16[4,288,1024]{2,1,0:T(8,128)(2,1)S(1)} %shard_map.118) | copy-start | bytes 7077892
  65.6 58.1 %all-to-all-start = ((bf16[4,288,1024]{2,1,0:T(8,128)(2,1)}), bf16[4,288,1024]{2,1,0:T(8,128)(2,1)S(1)}, u32[]{:S(2)}, u32[]{:S(2)}) async-start(bf16[4,288,1024]{2,1,0:T(8,128)(2,1)} %copy-done.3), calls=%async_computation | async-start | bytes 4718592 | tf_op jit(solution)/shard_map/all_to_all | solution.py:395
  69.5 2.8 %copy-start.1 = (bf16[2,1024,1536]{2,1,0:T(8,128)(2,1)S(1)}, bf16[2,1024,1536]{2,1,0:T(8,128)(2,1)}, u32[]{:S(2)}) copy-start(bf16[2,1024,1536]{2,1,0:T(8,128)(2,1)} %w_in.3) | copy-start | bytes 18874372
  72.2 1.4 %copy-start.7 = (bf16[512,1536]{1,0:T(8,128)(2,1)S(1)}, bf16[512,1536]{1,0:T(8,128)(2,1)}, u32[]{:S(2)}) copy-start(bf16[512,1536]{1,0:T(8,128)(2,1)} %copy-done.6) | copy-start | bytes 4718596
  76.0 17.6 %copy-start.5 = (bf16[512,1536]{1,0:T(8,128)(2,1)S(1)}, bf16[512,1536]{1,0:T(8,128)(2,1)}, u32[]{:S(2)}) copy-start(bf16[512,1536]{1,0:T(8,128)(2,1)} %copy-done.4) | copy-start | bytes 4718596
  76.0 9.2 %collective-permute-start.14 = (bf16[128,1024]{1,0:T(8,128)(2,1)S(1)}, bf16[128,1024]{1,0:T(8,128)(2,1)S(1)}, u32[]{:S(2)}, u32[]{:S(2)}) collective-permute-start(bf16[128,1024]{1,0:T(8,128)(2,1)S(1)} %get-tuple-element.66), channel_id=1, source_target_pairs={{0,1},{1,0},{2,3},{3,2},{4,5},{5,4},{6,7},{7,6},{8,9},{9,8},{10,11... | collective-permute-start | bytes 786440 | tf_op jit(solution)/shard_map/ppermute | solution.py:270
  77.4 8.9 %collective-permute-start.15 = (bf16[128,1024]{1,0:T(8,128)(2,1)S(1)}, bf16[128,1024]{1,0:T(8,128)(2,1)S(1)}, u32[]{:S(2)}, u32[]{:S(2)}) collective-permute-start(bf16[128,1024]{1,0:T(8,128)(2,1)S(1)} %get-tuple-element.67), channel_id=1, source_target_pairs={{0,2},{1,3},{2,0},{3,1},{4,6},{5,7},{6,4},{7,5},{8,10},{9,11},{10,... | collective-permute-start | bytes 786440 | tf_op jit(solution)/shard_map/ppermute | solution.py:270
  78.1 12.9 %collective-permute-start.16 = (bf16[128,1024]{1,0:T(8,128)(2,1)S(1)}, bf16[128,1024]{1,0:T(8,128)(2,1)S(1)}, u32[]{:S(2)}, u32[]{:S(2)}) collective-permute-start(bf16[128,1024]{1,0:T(8,128)(2,1)S(1)} %get-tuple-element.68), channel_id=1, source_target_pairs={{0,3},{1,2},{2,1},{3,0},{4,7},{5,6},{6,5},{7,4},{8,11},{9,10},{10,... | collective-permute-start | bytes 786440 | tf_op jit(solution)/shard_map/ppermute | solution.py:270
  92.0 27.3 %collective-permute-start.17 = (bf16[256,1024]{1,0:T(8,128)(2,1)S(1)}, bf16[256,1024]{1,0:T(8,128)(2,1)S(1)}, u32[]{:S(2)}, u32[]{:S(2)}) collective-permute-start(bf16[256,1024]{1,0:T(8,128)(2,1)S(1)} %shard_map.113), channel_id=1, source_target_pairs={{0,8},{4,12},{8,0},{12,4},{16,24},{20,28},{24,16},{28,20},{1,9},{5... | collective-permute-start | bytes 1572872 | tf_op jit(solution)/shard_map/ppermute | solution.py:269
  96.0 9.3 %collective-permute-start.5 = (bf16[128,1024]{1,0:T(8,128)(2,1)S(1)}, bf16[128,1024]{1,0:T(8,128)(2,1)S(1)}, u32[]{:S(2)}, u32[]{:S(2)}) collective-permute-start(bf16[128,1024]{1,0:T(8,128)(2,1)S(1)} %get-tuple-element.52), channel_id=1, source_target_pairs={{0,1},{1,0},{2,3},{3,2},{4,5},{5,4},{6,7},{7,6},{8,9},{9,8},{10,11... | collective-permute-start | bytes 786440 | tf_op jit(solution)/shard_map/ppermute | solution.py:270
  96.8 11.7 %collective-permute-start.6 = (bf16[128,1024]{1,0:T(8,128)(2,1)S(1)}, bf16[128,1024]{1,0:T(8,128)(2,1)S(1)}, u32[]{:S(2)}, u32[]{:S(2)}) collective-permute-start(bf16[128,1024]{1,0:T(8,128)(2,1)S(1)} %get-tuple-element.53), channel_id=1, source_target_pairs={{0,2},{1,3},{2,0},{3,1},{4,6},{5,7},{6,4},{7,5},{8,10},{9,11},{10,... | collective-permute-start | bytes 786440 | tf_op jit(solution)/shard_map/ppermute | solution.py:270
  98.3 10.2 %collective-permute-start.7 = (bf16[128,1024]{1,0:T(8,128)(2,1)S(1)}, bf16[128,1024]{1,0:T(8,128)(2,1)S(1)}, u32[]{:S(2)}, u32[]{:S(2)}) collective-permute-start(bf16[128,1024]{1,0:T(8,128)(2,1)S(1)} %get-tuple-element.54), channel_id=1, source_target_pairs={{0,3},{1,2},{2,1},{3,0},{4,7},{5,6},{6,5},{7,4},{8,11},{9,10},{10,... | collective-permute-start | bytes 786440 | tf_op jit(solution)/shard_map/ppermute | solution.py:270
  108.5 15.2 %copy-start.8 = (s32[4]{0:T(128)S(1)}, s32[4]{0:T(128)}, u32[]{:S(2)}) copy-start(s32[4]{0:T(128)} %constant.43.scal) | copy-start | bytes 52
